TPU v7x, 32 devices: a whole 2x2x4 slice. The times are simulated.
32 devices in a mesh: row: 8 (over y, x, core), col: 4 (over z).
Axes of the slice: x: 2, y: 2, z: 4, core: 2. Of those that a mesh axis runs over, the one named last changes fastest.
Arguments:
- tokens: bfloat16 [1536, 18432], P('col', 'row'), may hold values from -6 to 6
- out_grad: bfloat16 [1536, 18432], P('col', 'row'), may hold values from -6 to 6
- logratio: float32 [1536], P('col'), as said below
- token_session: int32 [1536], P('col'), may hold values from 0 to 7
- token_position: int32 [1536], P('col'), may hold values from 0 to 3
- pad_mask: int32 [1536], P('col'), may hold values from 0 to 1, as said below
- w_in: float32 [18432, 3072], P('row', 'col'), may hold values from -0.046875 to 0.046875
- m_in: float32 [18432, 3072], P('row', 'col'), may hold values from -6 to 6
- v_in: float32 [18432, 3072], P('row', 'col'), may hold values from 0.2 to 5
- w_out: float32 [3072, 18432], P('col', 'row'), may hold values from -0.109375 to 0.109375
- m_out: float32 [3072, 18432], P('col', 'row'), may hold values from -6 to 6
- v_out: float32 [3072, 18432], P('col', 'row'), may hold values from 0.2 to 5
Outputs:
- new_w_in: float32 [18432, 3072], P('row', 'col')
- new_m_in: float32 [18432, 3072], P('row', 'col')
- new_v_in: float32 [18432, 3072], P('row', 'col')
- new_w_out: float32 [3072, 18432], P('col', 'row')
- new_m_out: float32 [3072, 18432], P('col', 'row')
- new_v_out: float32 [3072, 18432], P('col', 'row')
Inputs may be any that keep to these rules, and one draw needn't show every extreme that they name: `pad_mask`: some tokens are padding in every draw. `logratio`: Real-valued log-probability differences of order one.
All inputs are finite; a program needn't handle non-finite values.
Results may differ from a plain program's by a relative error of at most 0.0013.
Values may be sent and summed in bfloat16 or wider, within the bound.
No kernel may reach another device: no remote copies, remote signals or barrier semaphores. Data moves between devices by JAX's collectives and lax.ppermute only.
A program may use at most 256 MiB of HBM per device.

v0:
```python
import math

import jax
import jax.numpy as jnp
from jax import lax
from jax.sharding import PartitionSpec as P

SESSIONS = 8
LIST = 4


def listwise_grad(scores):
    s = scores.reshape(SESSIONS, LIST)
    later = s[:, None, :] - s[:, :, None]
    order = jnp.arange(LIST)
    after = (order[None, :] > order[:, None]).astype(jnp.float32)
    before = (order[None, :] < order[:, None]).astype(jnp.float32)
    worse = -jnp.sum(after[None] * jax.nn.sigmoid(later), axis=2)
    better = jnp.sum(before[None] * jax.nn.sigmoid(-later), axis=2)
    return (worse + better).reshape(SESSIONS * LIST)


def adamw(weight, first, second, grad):
    new_first = 0.9 * first + 0.1 * grad
    new_second = 0.95 * second + 0.05 * grad * grad
    step = (
        new_first / (1.0 - 0.9**20) / (jnp.sqrt(new_second / (1.0 - 0.95**20)) + 1e-08)
        + 0.1 * weight
    )
    return (weight - 0.0003 * step, new_first, new_second)


def over_rows(left, right):
    return lax.dot_general(
        left, right, (((0,), (0,)), ((), ())), preferred_element_type=jnp.float32
    )


def against(left, right):
    return lax.dot_general(
        left, right, (((1,), (1,)), ((), ())), preferred_element_type=jnp.float32
    )


def elementwise(pre, back):
    positive = jnp.maximum(pre, 0.0)
    act = (positive * positive).astype(jnp.bfloat16)
    dpre = (back * 2.0 * positive).astype(jnp.bfloat16)
    return (act, dpre)


def on_device(
    tokens,
    out_grad,
    logratio,
    token_session,
    token_position,
    pad_mask,
    w_in,
    m_in,
    v_in,
    w_out,
    m_out,
    v_out,
):
    all_rows = tokens.shape[0] * lax.axis_size("col")
    response = token_session * LIST + token_position
    onehot = (response[:, None] == jnp.arange(SESSIONS * LIST, dtype=jnp.int32)[None, :]).astype(
        jnp.float32
    )
    live = pad_mask.astype(jnp.float32)
    local_sums = jnp.sum(onehot * (live * logratio)[:, None], axis=0)
    factor = math.sqrt(SESSIONS * LIST / all_rows)
    scores = factor * lax.psum(local_sums, "col")
    response_grad = listwise_grad(scores)
    coeff = 0.1 * live * jnp.sum(onehot * response_grad[None, :], axis=1)
    dy = (coeff[:, None] * out_grad.astype(jnp.float32)).astype(jnp.bfloat16)
    w_in16 = w_in.astype(jnp.bfloat16)
    w_out16 = w_out.astype(jnp.bfloat16)
    token_panel, dy_panel = (
        lax.all_gather(tokens, "col", axis=0, tiled=True),
        lax.all_gather(dy, "col", axis=0, tiled=True),
    )
    pre_part = jnp.dot(token_panel, w_in16, preferred_element_type=jnp.float32)
    back_part = against(dy_panel, w_out16)
    pre, back = lax.psum((pre_part, back_part), "row")
    act, dpre = elementwise(pre, back)
    grad_in = over_rows(token_panel, dpre)
    grad_out = over_rows(act, dy_panel)
    new_w_in, new_m_in, new_v_in = adamw(w_in, m_in, v_in, grad_in)
    new_w_out, new_m_out, new_v_out = adamw(w_out, m_out, v_out, grad_out)
    return (new_w_in, new_m_in, new_v_in, new_w_out, new_m_out, new_v_out)


def solution(mesh):
    in_specs = (
        P("col", "row"),
        P("col", "row"),
        P("col"),
        P("col"),
        P("col"),
        P("col"),
        P("row", "col"),
        P("row", "col"),
        P("row", "col"),
        P("col", "row"),
        P("col", "row"),
        P("col", "row"),
    )
    out_specs = (
        P("row", "col"),
        P("row", "col"),
        P("row", "col"),
        P("col", "row"),
        P("col", "row"),
        P("col", "row"),
    )
    return jax.shard_map(
        on_device, mesh=mesh, in_specs=in_specs, out_specs=out_specs, check_vma=False
    )
```

profile of v0, /device:TPU:0, one launch (start us, length us, event | category | flops | bytes accessed | tf_op | source)
XLA Modules:
  0.0 506.9 jit_solution(17730754178534902113)
XLA Ops:
  7.2 0.7 multiply_add_fusion.1
  7.9 0.7 convert_multiply_fusion
  8.6 0.1 select_reduce_fusion.1
  8.7 13.5 %psum.21 = f32[32]{0:T(128)S(1)} all-reduce(f32[32]{0:T(128)S(1)} %select_reduce_fusion.1), channel_id=1, replica_groups=mesh['row'=8,'col'=4] {'col'}, use_global_device_ids=true, to_apply=%region_1.0 | all-reduce | flops 32 | bytes 256 | tf_op jit(solution)/shard_map/psum | solution.py:74
  22.3 0.1 copy.33
  22.4 0.1 fusion.16
  22.5 0.1 copy.35
  22.6 0.1 select_reduce_fusion
  22.7 0.7 multiply_multiply_fusion.2
  23.4 3.0 multiply_convert_fusion.2
  26.5 0.7 all-gather.5.cloned.1.call-update
  27.3 125.8 %all-gather.3.cloned.1.call-done = bf16[1536,2304]{1,0:T(8,128)(2,1)} async-done(((bf16[384,2304]{1,0:T(8,128)(2,1)}), bf16[1536,2304]{1,0:T(8,128)(2,1)}) %all-gather.3.cloned.1.call-update) | async-done | bytes 7077904 | tf_op jit(solution)/shard_map/all_gather | solution.py:82
  153.1 11.4 %fusion.5 = f32[1536,768]{1,0:T(8,128)} fusion(bf16[1536,2304]{1,0:T(8,128)(2,1)} %all-gather.3.cloned.1.call-done, f32[768,2304]{1,0:T(8,128)} %param.21), kind=kOutput, calls=%fused_computation.13 | convolution fusion | flops 5437587456 | bytes 18874368 | tf_op jit(solution)/shard_map/dot_general | solution.py:40
  164.4 116.7 %all-gather.5.cloned.1.call-done = bf16[1536,2304]{1,0:T(8,128)(2,1)} async-done(((bf16[384,2304]{1,0:T(8,128)(2,1)}), bf16[1536,2304]{1,0:T(8,128)(2,1)}) %all-gather.5.cloned.1.call-update) | async-done | bytes 7077904 | tf_op jit(solution)/shard_map/all_gather | solution.py:81
  281.1 11.3 %fusion.3 = f32[1536,768]{1,0:T(8,128)} fusion(bf16[1536,2304]{1,0:T(8,128)(2,1)} %all-gather.5.cloned.1.call-done, f32[2304,768]{1,0:T(8,128)} %param.18), kind=kOutput, calls=%fused_computation.11 | convolution fusion | flops 5437587456 | bytes 18874368 | tf_op jit(solution)/shard_map/dot_general | solution.py:84
  292.4 8.1 %copy.38 = f32[2304,768]{0,1:T(8,128)} copy(f32[2304,768]{1,0:T(8,128)} %param.18) | data formatting | bytes 14155776 | tf_op args[6]
  300.6 8.1 %copy.32 = f32[2304,768]{0,1:T(8,128)} copy(f32[2304,768]{1,0:T(8,128)} %param.19) | data formatting | bytes 14155776 | tf_op args[7]
  308.7 8.1 %copy.36 = f32[2304,768]{0,1:T(8,128)} copy(f32[2304,768]{1,0:T(8,128)} %param.20) | data formatting | bytes 14155776 | tf_op args[8]
  316.8 112.3 %all-reduce.3.cloned.1.call-done = (f32[1536,768]{1,0:T(8,128)}, f32[1536,768]{1,0:T(8,128)}) async-done(((f32[1536,768]{1,0:T(8,128)}, f32[1536,768]{1,0:T(8,128)}), (f32[1536,768]{1,0:T(8,128)}, f32[1536,768]{1,0:T(8,128)})) %all-reduce.3.cloned.1.call-update) | async-done | bytes 9437200 | tf_op jit(solution)/shard_map/psum | solution.py:86
  429.1 24.3 %multiply_subtract_fusion.1 = (f32[2304,768]{0,1:T(8,128)}, f32[2304,768]{0,1:T(8,128)}, f32[2304,768]{0,1:T(8,128)}) fusion(f32[2304,768]{0,1:T(8,128)} %copy.38, f32[2304,768]{0,1:T(8,128)} %copy.32, f32[2304,768]{0,1:T(8,128)} %copy.36, bf16[1536,2304]{1,0:T(8,128)(2,1)} %all-gather.5.cloned.1.call-done, f32[1536,768]{1,0:T(8,128)} %get-tuple-element.26, ...), kind=kOutput, calls=%fused_computation.8 | convolution fusion | flops 5467078656 | bytes 58982400 | tf_op jit(solution)/shard_map/dot_general | solution.py:34
  453.4 8.0 %copy.39 = f32[2304,768]{1,0:T(8,128)} copy(f32[2304,768]{0,1:T(8,128)} %get-tuple-element.31) | data formatting | bytes 14155776
  461.4 8.0 %copy.40 = f32[2304,768]{1,0:T(8,128)} copy(f32[2304,768]{0,1:T(8,128)} %get-tuple-element.32) | data formatting | bytes 14155776
  469.4 8.0 %copy.41 = f32[2304,768]{1,0:T(8,128)} copy(f32[2304,768]{0,1:T(8,128)} %get-tuple-element.33) | data formatting | bytes 14155776
  477.4 23.0 %multiply_subtract_fusion = (f32[768,2304]{1,0:T(8,128)}, f32[768,2304]{1,0:T(8,128)}, f32[768,2304]{1,0:T(8,128)}) fusion(f32[768,2304]{1,0:T(8,128)} %param.21, f32[768,2304]{1,0:T(8,128)} %param.22, f32[768,2304]{1,0:T(8,128)} %param.23, bf16[1536,2304]{1,0:T(8,128)(2,1)} %all-gather.3.cloned.1.call-done, f32[1536,768]{1,0:T(8,128)} %get-tuple-element.27), kind=kOutput, calls=%fused_computation.6 | convolution fusion | flops 5465899008 | bytes 54263808 | tf_op jit(solution)/shard_map/dot_general | solution.py:34
  (10 shorter events, 0.3 us)
Async XLA Ops:
  7.2 145.9 %all-gather.3.cloned.1.call-start = ((), (), s32[]{:S(2)}) async-start(), calls=%async_computation | async-start | bytes 8847360 | tf_op jit(solution)/shard_map/all_gather | solution.py:82
  26.5 254.6 %all-gather.5.cloned.1.call-start = ((), (), s32[]{:S(2)}) async-start(), calls=%async_computation.1 | async-start | bytes 8847360 | tf_op jit(solution)/shard_map/all_gather | solution.py:81
  27.2 401.9 %all-reduce.3.cloned.1.call-start = ((), (), s32[]{:S(2)}) async-start(), calls=%async_computation.2 | async-start | bytes 18874368 | tf_op jit(solution)/shard_map/psum | solution.py:86
Sparse Core Ops, SparseCore 0:
  26.6 126.4 all-gather.2
  154.6 126.4 all-gather.4
  292.6 136.4 all-reduce.2
where the time goes:
time: 508 us; the launch traced here: 507 us
  waiting for transfers between devices  355 us (70%)
  matrix products  70 us (14%)
  local copies, waits for them, and re-layouts  48.7 us (10%)
  between operations  13.8 us (3%)
  blocking collectives  13.5 us (3%)
  other arithmetic  5.45 us (1%)
    all_gather x1, waiting for transfers between devices, on_device(): lax.all_gather(dy, 'col', axis=0, tiled=True)  126 us
    all_gather x1, waiting for transfers between devices, on_device(): lax.all_gather(tokens, 'col', axis=0, tiled=True)  117 us
    psum x1, waiting for transfers between devices, on_device(): pre, back = lax.psum((pre_part, back_part), 'row')  112 us
    unnamed x6, local copies, waits for them, and re-layouts  48.3 us
    dot_general x2, matrix products, over_rows(): lax.dot_general(left, right, (((0,), (0,)), ((), ())), preferred_element_...  47.3 us
    psum x1, blocking collectives, on_device(): scores = factor * lax.psum(local_sums, 'col')  13.5 us
    dot_general x1, matrix products, against(): lax.dot_general(left, right, (((1,), (1,)), ((), ())), preferred_element_...  11.4 us
    dot_general x1, matrix products, on_device(): pre_part = jnp.dot(token_panel, w_in16, preferred_element_type=jnp.float32)  11.3 us
  transfers between devices with their start and end apart: 3, of which 3 were waited for; matrix products, arithmetic and copies ran while one was open for 7% of the time, Pallas kernels for 0%

commit v1 on v0

--- a/solution.py
+++ b/solution.py
@@ -1,8 +1,11 @@
+import functools
 import math
 
 import jax
 import jax.numpy as jnp
 from jax import lax
+from jax.experimental import pallas as pl
+from jax.experimental.pallas import tpu as pltpu
 from jax.sharding import PartitionSpec as P
 
 SESSIONS = 8
@@ -42,11 +45,124 @@
     )
 
 
-def elementwise(pre, back):
-    positive = jnp.maximum(pre, 0.0)
-    act = (positive * positive).astype(jnp.bfloat16)
-    dpre = (back * 2.0 * positive).astype(jnp.bfloat16)
-    return (act, dpre)
+def block_of(size, most):
+    block = most
+    while size % block:
+        block -= 128
+    return block
+
+
+def grad_kernel(parts, *refs):
+    lefts, rights, out = refs[:parts], refs[parts : 2 * parts], refs[2 * parts]
+    total = over_rows(lefts[0][...], rights[0][...])
+    for left, right in zip(lefts[1:], rights[1:]):
+        total += over_rows(left[...], right[...])
+    out[...] = total
+
+
+def grad_sum(lefts, rights, most):
+    rows, height = lefts[0].shape
+    width = rights[0].shape[1]
+    parts = len(lefts)
+    block = block_of(height, most)
+    return pl.pallas_call(
+        functools.partial(grad_kernel, parts),
+        grid=(height // block,),
+        in_specs=[pl.BlockSpec((rows, block), lambda i: (0, i))] * parts
+        + [pl.BlockSpec((rows, width), lambda i: (0, 0))] * parts,
+        out_specs=pl.BlockSpec((block, width), lambda i: (i, 0)),
+        out_shape=jax.ShapeDtypeStruct((height, width), jnp.float32),
+        compiler_params=pltpu.CompilerParams(vmem_limit_bytes=44 * 2**20),
+        cost_estimate=pl.CostEstimate(
+            flops=2 * parts * rows * height * width,
+            bytes_accessed=4 * height * width + 2 * parts * rows * (height + width),
+            transcendentals=0,
+        ),
+    )(*lefts, *rights)
+
+
+def update_kernel(left, right, grad, w, m, v, new_w, new_m, new_v):
+    total = grad[...] + over_rows(left[...], right[...])
+    new_w[...], new_m[...], new_v[...] = adamw(w[...], m[...], v[...], total)
+
+
+def update(left, right, grad, w, m, v, most):
+    rows, height = left.shape
+    width = right.shape[1]
+    block = block_of(height, most)
+    panel = pl.BlockSpec((block, width), lambda i: (i, 0))
+    shape = jax.ShapeDtypeStruct((height, width), jnp.float32)
+    return pl.pallas_call(
+        update_kernel,
+        grid=(height // block,),
+        in_specs=[
+            pl.BlockSpec((rows, block), lambda i: (0, i)),
+            pl.BlockSpec((rows, width), lambda i: (0, 0)),
+            panel,
+            panel,
+            panel,
+            panel,
+        ],
+        out_specs=[panel] * 3,
+        out_shape=[shape] * 3,
+        compiler_params=pltpu.CompilerParams(vmem_limit_bytes=44 * 2**20),
+        cost_estimate=pl.CostEstimate(
+            flops=2 * rows * height * width,
+            bytes_accessed=7 * 4 * height * width + 2 * rows * (height + width),
+            transcendentals=2 * height * width,
+        ),
+    )(left, right, grad, w, m, v)
+
+
+def link_pairs(n, first, step):
+    pairs = []
+    for low in range(first, n - 1, 2):
+        if low - (step - 1) >= 0:
+            pairs.append((low, low + 1))
+        if low + step <= n - 1:
+            pairs.append((low + 1, low))
+    return pairs
+
+
+def arrivals(n, c):
+    order = []
+    for step in range(1, n):
+        from_right, from_left = c + step <= n - 1, c - step >= 0
+        over = (from_right, from_left) if c % 2 == 0 else (from_left, from_right)
+        order += [(links, step) for links in (0, 1) if over[links]]
+    return order
+
+
+def line_gather(shard, axis):
+    n = lax.axis_size(axis)
+    here = lax.axis_index(axis)
+    came = {(0, 0): shard, (1, 0): shard}
+    for step in range(1, n):
+        for links in (0, 1):
+            pairs = link_pairs(n, links, step)
+            if pairs:
+                came[links, step] = lax.ppermute(came[1 - links, step - 1], axis, pairs)
+    slots = [shard]
+    tables = [arrivals(n, c) for c in range(n)]
+    for slot in range(n - 1):
+        users = {}
+        for c in range(n):
+            users.setdefault(tables[c][slot], []).append(c)
+        choice = None
+        for source, places in users.items():
+            if choice is None:
+                choice = came[source]
+            else:
+                mine = functools.reduce(jnp.logical_or, [here == c for c in places])
+                choice = jnp.where(mine, came[source], choice)
+        slots.append(choice)
+    return slots
+
+
+def row_sum(parts, earlier):
+    if earlier is not None:
+        parts, _ = lax.optimization_barrier((parts, earlier))
+    return lax.psum(parts, "row")
 
 
 def on_device(
@@ -63,7 +179,9 @@
     m_out,
     v_out,
 ):
-    all_rows = tokens.shape[0] * lax.axis_size("col")
+    n = lax.axis_size("col")
+    token_slots = line_gather(tokens, "col")
+    all_rows = tokens.shape[0] * n
     response = token_session * LIST + token_position
     onehot = (response[:, None] == jnp.arange(SESSIONS * LIST, dtype=jnp.int32)[None, :]).astype(
         jnp.float32
@@ -75,21 +193,33 @@
     response_grad = listwise_grad(scores)
     coeff = 0.1 * live * jnp.sum(onehot * response_grad[None, :], axis=1)
     dy = (coeff[:, None] * out_grad.astype(jnp.float32)).astype(jnp.bfloat16)
-    w_in16 = w_in.astype(jnp.bfloat16)
-    w_out16 = w_out.astype(jnp.bfloat16)
-    token_panel, dy_panel = (
-        lax.all_gather(tokens, "col", axis=0, tiled=True),
-        lax.all_gather(dy, "col", axis=0, tiled=True),
-    )
-    pre_part = jnp.dot(token_panel, w_in16, preferred_element_type=jnp.float32)
-    back_part = against(dy_panel, w_out16)
-    pre, back = lax.psum((pre_part, back_part), "row")
-    act, dpre = elementwise(pre, back)
-    grad_in = over_rows(token_panel, dpre)
-    grad_out = over_rows(act, dy_panel)
-    new_w_in, new_m_in, new_v_in = adamw(w_in, m_in, v_in, grad_in)
-    new_w_out, new_m_out, new_v_out = adamw(w_out, m_out, v_out, grad_out)
-    return (new_w_in, new_m_in, new_v_in, new_w_out, new_m_out, new_v_out)
+    dy_slots = line_gather(dy, "col")
+    w_in16, w_out16 = lax.optimization_barrier(
+        (w_in.astype(jnp.bfloat16), w_out.astype(jnp.bfloat16))
+    )
+    acts, dpres = [], []
+    last = None
+    for slot in range(n - 1):
+        pre_part = jnp.dot(token_slots[slot], w_in16, preferred_element_type=jnp.float32)
+        back_part = against(dy_slots[slot], w_out16)
+        pre, back = last = row_sum((pre_part, back_part), last)
+        positive = jnp.maximum(pre, 0.0)
+        acts.append((positive * positive).astype(jnp.bfloat16))
+        dpres.append((back * 2.0 * positive).astype(jnp.bfloat16))
+    grad_in = grad_sum(token_slots[:-1], dpres, 256)
+    grad_out = grad_sum(acts, dy_slots[:-1], 128)
+    tokens_last, dy_last = token_slots[-1], dy_slots[-1]
+    pre_part = jnp.dot(tokens_last, w_in16, preferred_element_type=jnp.float32)
+    (pre,) = last = row_sum((pre_part,), last)
+    positive = jnp.maximum(pre, 0.0)
+    act = (positive * positive).astype(jnp.bfloat16)
+    dy_last, grad_in, grad_out = lax.optimization_barrier((dy_last, grad_in, grad_out))
+    (back,) = row_sum((against(dy_last, w_out16),), last)
+    outs_out = update(act, dy_last, grad_out, w_out, m_out, v_out, 128)
+    back, outs_out = lax.optimization_barrier((back, outs_out))
+    dpre = (back * 2.0 * positive).astype(jnp.bfloat16)
+    outs_in = update(tokens_last, dpre, grad_in, w_in, m_in, v_in, 256)
+    return (*outs_in, *outs_out)
 
 
 def solution(mesh):

time: 508 us -> 448 us (0.88)
  waiting for transfers between devices: 355 us -> 286 us
  Pallas kernels: 0 us -> 58.6 us
  matrix products: 70 us -> 24.6 us
  local copies, waits for them, and re-layouts: 48.7 us -> 9.81 us
  other arithmetic: 5.45 us -> 24.4 us
  starting transfers between devices: 0.12 us -> 15.6 us
    all_gather x2 -> x0, waiting for transfers between devices: 242 us -> none  [the longest x1 126 us: on_device(): lax.all_gather(dy, 'col', axis=0, tiled=True)]
    ppermute x0 -> x10, waiting for transfers between devices: none -> 97.7 us  [line_gather(): came[links, step] = lax.ppermute(came[1 - links, step - 1], axis, pairs)]
    psum x1 -> x5, waiting for transfers between devices: 112 us -> 188 us  [row_sum(): return lax.psum(parts, 'row')]
    pallas_call x0 -> x4, Pallas kernels: none -> 58.6 us  [the longest x2 38.1 us: update(): pl.pallas_call(update_kernel, grid=(height // block,), in_specs=[pl.Block...]
    dot_general x3 -> x4, matrix products: 58.6 us -> 11.8 us  [the longest x3 9.2 us: on_device(): jnp.dot(token_slots[slot], w_in16, preferred_element_type=jnp.float32)]
    unnamed x6 -> x40, local copies, waits for them, and re-layouts: 48.3 us -> 9.48 us
    ppermute x0 -> x10, starting transfers between devices: none -> 15.4 us  [line_gather(): came[links, step] = lax.ppermute(came[1 - links, step - 1], axis, pairs)]
    convert_element_type x0 -> x7, other arithmetic: none -> 13.1 us  [the longest x3 6.06 us: on_device(): acts.append((positive * positive).astype(jnp.bfloat16))]
  transfers between devices with their start and end apart: 3 -> 15, of which waited for: 3 -> 9; matrix products, arithmetic and copies ran while one was open for 7% -> 10% of each run, Pallas kernels for 0% -> 9%
where the time goes in v1:
time: 448 us; the launch traced here: 447 us
  waiting for transfers between devices  286 us (64%)
  Pallas kernels  58.6 us (13%)
  matrix products  24.6 us (5%)
  other arithmetic  24.4 us (5%)
  starting transfers between devices  15.6 us (3%)
  between operations  14 us (3%)
  blocking collectives  13.5 us (3%)
  local copies, waits for them, and re-layouts  9.81 us (2%)
    psum x5, waiting for transfers between devices, row_sum(): return lax.psum(parts, 'row')  188 us
    ppermute x10, waiting for transfers between devices, line_gather(): came[links, step] = lax.ppermute(came[1 - links, step - 1], axis, pairs)  97.7 us
    pallas_call x2, Pallas kernels, update(): pl.pallas_call(update_kernel, grid=(height // block,), in_specs=[pl.Block...  38.1 us
    pallas_call x2, Pallas kernels, grad_sum(): pl.pallas_call(functools.partial(grad_kernel, parts), grid=(height // blo...  20.4 us
    ppermute x10, starting transfers between devices, line_gather(): came[links, step] = lax.ppermute(came[1 - links, step - 1], axis, pairs)  15.4 us
    psum x1, blocking collectives, on_device(): scores = factor * lax.psum(local_sums, 'col')  13.5 us
    dot_general x4, matrix products, against(): lax.dot_general(left, right, (((1,), (1,)), ((), ())), preferred_element_...  12.9 us
    unnamed x40, local copies, waits for them, and re-layouts  9.48 us
  transfers between devices with their start and end apart: 15, of which 9 were waited for; matrix products, arithmetic and copies ran while one was open for 10% of the time, Pallas kernels for 9%

profile of v1, /device:TPU:0, one launch (start us, length us, event | category | flops | bytes accessed | tf_op | source)
XLA Modules:
  0.0 446.6 jit_solution(15124405075687321134)
XLA Ops:
  8.7 13.5 %psum.63 = f32[32]{0:T(128)S(1)} all-reduce(f32[32]{0:T(128)S(1)} %select_reduce_fusion.1), channel_id=1, replica_groups=mesh['row'=8,'col'=4] {'col'}, use_global_device_ids=true, to_apply=%region_1.2 | all-reduce | flops 32 | bytes 256 | tf_op jit(solution)/shard_map/psum | solution.py:192
  31.3 3.5 convert_element_type.59
  37.9 2.6 fusion.11
  44.8 26.1 %collective-permute-done.3.refs_4_ = bf16[384,2304]{1,0:T(8,128)(2,1)} collective-permute-done((bf16[384,2304]{1,0:T(8,128)(2,1)S(1)}, bf16[384,2304]{1,0:T(8,128)(2,1)}, u32[]{:S(2)}, u32[]{:S(2)}) %collective-permute-start.3) | collective-permute-done | bytes 1769504 | tf_op jit(solution)/shard_map/ppermute | solution.py:144
  70.9 5.1 %fusion.12 = f32[384,768]{1,0:T(8,128)} fusion(bf16[384,2304]{1,0:T(8,128)(2,1)} %collective-permute-done.3.refs_4_, bf16[768,2304]{1,0:T(8,128)(2,1)} %copy-done.11), kind=kOutput, calls=%fused_computation.39 | convolution fusion | flops 1358954496 | bytes 6488064 | tf_op jit(solution)/shard_map/dot_general | solution.py:43
  76.0 32.8 %collective-permute-done.refs_1_ = bf16[384,2304]{1,0:T(8,128)(2,1)} collective-permute-done((bf16[384,2304]{1,0:T(8,128)(2,1)S(1)}, bf16[384,2304]{1,0:T(8,128)(2,1)}, u32[]{:S(2)}, u32[]{:S(2)}) %collective-permute-start) | collective-permute-done | bytes 1769504 | tf_op jit(solution)/shard_map/ppermute | solution.py:144
  108.8 4.1 convolution_bitcast_fusion
  112.9 24.2 %all-reduce.17.cloned.1.call-done = (f32[384,768]{1,0:T(8,128)}, f32[384,768]{1,0:T(8,128)}) async-done(((f32[384,768]{1,0:T(8,128)}, f32[384,768]{1,0:T(8,128)}), (f32[384,768]{1,0:T(8,128)}, f32[384,768]{1,0:T(8,128)})) %all-reduce.17.cloned.1.call-update) | async-done | bytes 2359312 | tf_op jit(solution)/shard_map/psum | solution.py:165
  140.9 5.8 %collective-permute-done.9 = bf16[384,2304]{1,0:T(8,128)(2,1)} collective-permute-done((bf16[384,2304]{1,0:T(8,128)(2,1)}, bf16[384,2304]{1,0:T(8,128)(2,1)}, u32[]{:S(2)}, u32[]{:S(2)}) %collective-permute-start.9) | collective-permute-done | bytes 1769504 | tf_op jit(solution)/shard_map/ppermute | solution.py:144
  148.4 33.0 %collective-permute-done.7 = bf16[384,2304]{1,0:T(8,128)(2,1)} collective-permute-done((bf16[384,2304]{1,0:T(8,128)(2,1)}, bf16[384,2304]{1,0:T(8,128)(2,1)}, u32[]{:S(2)}, u32[]{:S(2)}) %collective-permute-start.7) | collective-permute-done | bytes 1769504 | tf_op jit(solution)/shard_map/ppermute | solution.py:144
  183.1 2.6 fusion.14
  185.7 2.6 fusion.13
  188.2 15.5 %all-reduce.15.cloned.1.call-done = (f32[384,768]{1,0:T(8,128)}, f32[384,768]{1,0:T(8,128)}) async-done(((f32[384,768]{1,0:T(8,128)}, f32[384,768]{1,0:T(8,128)}), (f32[384,768]{1,0:T(8,128)}, f32[384,768]{1,0:T(8,128)})) %all-reduce.15.cloned.1.call-update) | async-done | bytes 2359312 | tf_op jit(solution)/shard_map/psum | solution.py:165
  205.3 2.8 multiply_convert_fusion.5
  210.9 59.3 %all-reduce.13.cloned.1.call-done = (f32[384,768]{1,0:T(8,128)}, f32[384,768]{1,0:T(8,128)}) async-done(((f32[384,768]{1,0:T(8,128)}, f32[384,768]{1,0:T(8,128)}), (f32[384,768]{1,0:T(8,128)}, f32[384,768]{1,0:T(8,128)})) %all-reduce.13.cloned.1.call-update) | async-done | bytes 2359312 | tf_op jit(solution)/shard_map/psum | solution.py:165
  272.6 9.7 %shard_map.164.grad = f32[768,2304]{1,0:T(8,128)} custom-call(bf16[384,768]{1,0:T(8,128)(2,1)S(1)} %copy-done.6, bf16[384,768]{1,0:T(8,128)(2,1)S(1)} %copy-done.7, bf16[384,768]{1,0:T(8,128)(2,1)S(1)} %get-tuple-element.56.refs_2_, bf16[384,2304]{1,0:T(8,128)(2,1)S(1)} %multiply_convert_fusion.refs_3_, bf16[384,2304]{1,0:T(8,128)(2,1)} %collective-permute-done.3.refs_4_, ...), custom_call_target="tpu_custom_call" | custom-call | flops 4076863488 | bytes 14155776 | tf_op jit(solution)/shard_map/pallas_call | solution.py:68
  282.3 10.7 %shard_map.163.grad = f32[2304,768]{1,0:T(8,128)} custom-call(bf16[384,2304]{1,0:T(8,128)(2,1)S(1)} %copy-done.9, bf16[384,2304]{1,0:T(8,128)(2,1)} %collective-permute-done.refs_1_, bf16[384,2304]{1,0:T(8,128)(2,1)S(1)} %broadcast_select_fusion.1.refs_2_, bf16[384,768]{1,0:T(8,128)(2,1)S(1)} %copy-done.4, bf16[384,768]{1,0:T(8,128)(2,1)S(1)} %copy-done.5, ...), custom_call_target="tpu_custom_call" | custom-call | flops 4076863488 | bytes 14155776 | tf_op jit(solution)/shard_map/pallas_call | solution.py:68
  300.8 2.6 fusion.15
  303.3 51.5 %all-reduce.9.cloned.1.call-done = f32[384,768]{1,0:T(8,128)} async-done(((f32[384,768]{1,0:T(8,128)}), f32[384,768]{1,0:T(8,128)}) %all-reduce.9.cloned.1.call-update) | async-done | bytes 1179664 | tf_op jit(solution)/shard_map/psum | solution.py:165
  356.2 3.0 copy-done.1
  359.2 17.6 %shard_map.165 = (f32[768,2304]{1,0:T(8,128)}, f32[768,2304]{1,0:T(8,128)}, f32[768,2304]{1,0:T(8,128)}) custom-call(bf16[384,768]{1,0:T(8,128)(2,1)S(1)} %multiply_convert_fusion.2.left, bf16[384,2304]{1,0:T(8,128)(2,1)S(1)} %broadcast_select_fusion.2.right, f32[768,2304]{1,0:T(8,128)S(1)} %copy-done.1, f32[768,2304]{1,0:T(8,128)} %w.2, f32[768,2304]{1,0:T(8,128)} %m.2, ...), custom_call_target="tpu_custom_call" | custom-call | flops 1358954496 | bytes 51904512 | tf_op jit(solution)/shard_map/pallas_call | solution.py:95
  376.8 37.9 %all-reduce.11.cloned.1.call-done = f32[384,768]{1,0:T(8,128)} async-done(((f32[384,768]{1,0:T(8,128)}), f32[384,768]{1,0:T(8,128)}) %all-reduce.11.cloned.1.call-update) | async-done | bytes 1179664 | tf_op jit(solution)/shard_map/psum | solution.py:165
  416.5 3.0 copy-done
  419.5 20.6 %shard_map.166 = (f32[2304,768]{1,0:T(8,128)}, f32[2304,768]{1,0:T(8,128)}, f32[2304,768]{1,0:T(8,128)}) custom-call(bf16[384,2304]{1,0:T(8,128)(2,1)S(1)} %broadcast_select_fusion.3.left, bf16[384,768]{1,0:T(8,128)(2,1)S(1)} %multiply_convert_fusion.1.right, f32[2304,768]{1,0:T(8,128)S(1)} %copy-done, f32[2304,768]{1,0:T(8,128)} %w.3, f32[2304,768]{1,0:T(8,128)} %m.3, ...), custom_call_target="tpu_custom_call" | custom-call | flops 1358954496 | bytes 51904512 | tf_op jit(solution)/shard_map/pallas_call | solution.py:95
  (89 shorter events, 42.7 us)
Async XLA Ops:
  7.2 129.9 %all-reduce.17.cloned.1.call-start = ((), (), s32[]{:S(2)}) async-start(), calls=%async_computation.4 | async-start | bytes 4718592 | tf_op jit(solution)/shard_map/psum | solution.py:165
  25.4 11.2 %collective-permute-start.8 = (bf16[384,2304]{1,0:T(8,128)(2,1)S(1)}, bf16[384,2304]{1,0:T(8,128)(2,1)}, u32[]{:S(2)}, u32[]{:S(2)}) collective-permute-start(bf16[384,2304]{1,0:T(8,128)(2,1)S(1)} %multiply_convert_fusion.refs_3_), channel_id=1, source_target_pairs={{1,2},{2,1},{5,6},{6,5},{9,10},{10,9},{13,14},{14,13},{17,18},{18,... | collective-permute-start | bytes 5308424 | tf_op jit(solution)/shard_map/ppermute | solution.py:144
  27.3 15.9 %collective-permute-start.6 = (bf16[384,2304]{1,0:T(8,128)(2,1)S(1)}, bf16[384,2304]{1,0:T(8,128)(2,1)}, u32[]{:S(2)}, u32[]{:S(2)}) collective-permute-start(bf16[384,2304]{1,0:T(8,128)(2,1)S(1)} %copy-done.8), channel_id=1, source_target_pairs={{1,2},{2,1},{5,6},{6,5},{9,10},{10,9},{13,14},{14,13},{17,18},{18,... | collective-permute-start | bytes 5308424 | tf_op jit(solution)/shard_map/ppermute | solution.py:144
  29.2 41.7 %collective-permute-start.3 = (bf16[384,2304]{1,0:T(8,128)(2,1)S(1)}, bf16[384,2304]{1,0:T(8,128)(2,1)}, u32[]{:S(2)}, u32[]{:S(2)}) collective-permute-start(bf16[384,2304]{1,0:T(8,128)(2,1)S(1)} %multiply_convert_fusion.refs_3_), channel_id=1, source_target_pairs={{0,1},{1,0},{2,3},{3,2},{4,5},{5,4},{6,7},{7,6},{8,9},{9,8},{10,11... | collective-permute-start | bytes 5308424 | tf_op jit(solution)/shard_map/ppermute | solution.py:144
  29.9 78.9 %collective-permute-start = (bf16[384,2304]{1,0:T(8,128)(2,1)S(1)}, bf16[384,2304]{1,0:T(8,128)(2,1)}, u32[]{:S(2)}, u32[]{:S(2)}) collective-permute-start(bf16[384,2304]{1,0:T(8,128)(2,1)S(1)} %copy-done.8), channel_id=1, source_target_pairs={{0,1},{1,0},{2,3},{3,2},{4,5},{5,4},{6,7},{7,6},{8,9},{9,8},{10,11... | collective-permute-start | bytes 5308424 | tf_op jit(solution)/shard_map/ppermute | solution.py:144
  31.3 5.0 %copy-start.10 = (f32[768,2304]{1,0:T(8,128)S(1)}, f32[768,2304]{1,0:T(8,128)}, u32[]{:S(2)}) copy-start(f32[768,2304]{1,0:T(8,128)} %w.2) | copy-start | bytes 21233668
  36.6 110.1 %collective-permute-start.9 = (bf16[384,2304]{1,0:T(8,128)(2,1)}, bf16[384,2304]{1,0:T(8,128)(2,1)}, u32[]{:S(2)}, u32[]{:S(2)}) collective-permute-start(bf16[384,2304]{1,0:T(8,128)(2,1)} %collective-permute-done.8), channel_id=1, source_target_pairs={{1,0},{2,3},{5,4},{6,7},{9,8},{10,11},{13,12},{14,15},{17,16},{18,... | collective-permute-start | bytes 5308424 | tf_op jit(solution)/shard_map/ppermute | solution.py:144
  43.1 160.6 %all-reduce.15.cloned.1.call-start = ((), (), s32[]{:S(2)}) async-start(), calls=%async_computation.3 | async-start | bytes 4718592 | tf_op jit(solution)/shard_map/psum | solution.py:165
  43.2 65.6 %copy-start.15 = (bf16[2304,768]{1,0:T(8,128)(2,1)S(1)}, bf16[2304,768]{1,0:T(8,128)(2,1)}, u32[]{:S(2)}) copy-start(bf16[2304,768]{1,0:T(8,128)(2,1)} %copy-done.14) | copy-start | bytes 10616836
  43.2 138.2 %collective-permute-start.7 = (bf16[384,2304]{1,0:T(8,128)(2,1)}, bf16[384,2304]{1,0:T(8,128)(2,1)}, u32[]{:S(2)}, u32[]{:S(2)}) collective-permute-start(bf16[384,2304]{1,0:T(8,128)(2,1)} %collective-permute-done.6), channel_id=1, source_target_pairs={{1,0},{2,3},{5,4},{6,7},{9,8},{10,11},{13,12},{14,15},{17,16},{18,... | collective-permute-start | bytes 5308424 | tf_op jit(solution)/shard_map/ppermute | solution.py:144
  137.1 133.1 %all-reduce.13.cloned.1.call-start = ((), (), s32[]{:S(2)}) async-start(), calls=%async_computation.2 | async-start | bytes 4718592 | tf_op jit(solution)/shard_map/psum | solution.py:165
  137.1 72.3 %collective-permute-start.4 = (bf16[384,2304]{1,0:T(8,128)(2,1)}, bf16[384,2304]{1,0:T(8,128)(2,1)}, u32[]{:S(2)}, u32[]{:S(2)}) collective-permute-start(bf16[384,2304]{1,0:T(8,128)(2,1)} %collective-permute-done.3.refs_4_), channel_id=1, source_target_pairs={{1,2},{2,1},{5,6},{6,5},{9,10},{10,9},{13,14},{14,13},{17,18},{18,... | collective-permute-start | bytes 5308424 | tf_op jit(solution)/shard_map/ppermute | solution.py:144
  139.0 64.9 %collective-permute-start.1 = (bf16[384,2304]{1,0:T(8,128)(2,1)}, bf16[384,2304]{1,0:T(8,128)(2,1)}, u32[]{:S(2)}, u32[]{:S(2)}) collective-permute-start(bf16[384,2304]{1,0:T(8,128)(2,1)} %collective-permute-done.refs_1_), channel_id=1, source_target_pairs={{1,2},{2,1},{5,6},{6,5},{9,10},{10,9},{13,14},{14,13},{17,18},{18,... | collective-permute-start | bytes 5308424 | tf_op jit(solution)/shard_map/ppermute | solution.py:144
  148.4 34.7 %copy-start.2 = (bf16[384,2304]{1,0:T(8,128)(2,1)}, bf16[384,2304]{1,0:T(8,128)(2,1)S(1)}, u32[]{:S(2)}) copy-start(bf16[384,2304]{1,0:T(8,128)(2,1)S(1)} %broadcast_select_fusion.refs_5_) | copy-start | bytes 5308420
  148.4 34.6 %copy-start.12 = (bf16[768,2304]{1,0:T(8,128)(2,1)S(1)}, bf16[768,2304]{1,0:T(8,128)(2,1)}, u32[]{:S(2)}) copy-start(bf16[768,2304]{1,0:T(8,128)(2,1)} %copy-done.11) | copy-start | bytes 10616836
  203.8 151.0 %all-reduce.9.cloned.1.call-start = ((), (), s32[]{:S(2)}) async-start(), calls=%async_computation | async-start | bytes 2359296 | tf_op jit(solution)/shard_map/psum | solution.py:165
  203.8 4.3 copy-start.18
  203.9 4.3 copy-start.19
  203.9 89.2 %collective-permute-start.2 = (bf16[384,2304]{1,0:T(8,128)(2,1)}, bf16[384,2304]{1,0:T(8,128)(2,1)}, u32[]{:S(2)}, u32[]{:S(2)}) collective-permute-start(bf16[384,2304]{1,0:T(8,128)(2,1)} %collective-permute-done.1), channel_id=1, source_target_pairs={{1,0},{2,3},{5,4},{6,7},{9,8},{10,11},{13,12},{14,15},{17,16},{18,... | collective-permute-start | bytes 5308424 | tf_op jit(solution)/shard_map/ppermute | solution.py:144
  209.4 88.8 %collective-permute-start.5 = (bf16[384,2304]{1,0:T(8,128)(2,1)}, bf16[384,2304]{1,0:T(8,128)(2,1)}, u32[]{:S(2)}, u32[]{:S(2)}) collective-permute-start(bf16[384,2304]{1,0:T(8,128)(2,1)} %collective-permute-done.4), channel_id=1, source_target_pairs={{1,0},{2,3},{5,4},{6,7},{9,8},{10,11},{13,12},{14,15},{17,16},{18,... | collective-permute-start | bytes 5308424 | tf_op jit(solution)/shard_map/ppermute | solution.py:144
  272.6 9.7 %copy-start.4 = (bf16[384,768]{1,0:T(8,128)(2,1)S(1)}, bf16[384,768]{1,0:T(8,128)(2,1)}, u32[]{:S(2)}) copy-start(bf16[384,768]{1,0:T(8,128)(2,1)} %get-tuple-element.61.refs_3_) | copy-start | bytes 1769476
  272.6 9.7 %copy-start.5 = (bf16[384,768]{1,0:T(8,128)(2,1)S(1)}, bf16[384,768]{1,0:T(8,128)(2,1)}, u32[]{:S(2)}) copy-start(bf16[384,768]{1,0:T(8,128)(2,1)} %get-tuple-element.59.refs_4_) | copy-start | bytes 1769476
  272.6 9.7 %copy-start.9 = (bf16[384,2304]{1,0:T(8,128)(2,1)S(1)}, bf16[384,2304]{1,0:T(8,128)(2,1)}, u32[]{:S(2)}) copy-start(bf16[384,2304]{1,0:T(8,128)(2,1)} %refs_0_.1) | copy-start | bytes 5308420
  298.2 116.5 %all-reduce.11.cloned.1.call-start = ((), (), s32[]{:S(2)}) async-start(), calls=%async_computation.1 | async-start | bytes 2359296 | tf_op jit(solution)/shard_map/psum | solution.py:165
  (11 other events, 32.7 us)
Sparse Core Ops, SparseCore 0:
  43.3 93.7 all-reduce.16
  141.3 62.4 all-reduce.14
  207.7 62.4 all-reduce.12
  298.3 56.4 all-reduce.8
  358.4 56.1 all-reduce.10

commit v2 on v1

--- a/solution.py
+++ b/solution.py
@@ -142,12 +142,15 @@
             pairs = link_pairs(n, links, step)
             if pairs:
                 came[links, step] = lax.ppermute(came[1 - links, step - 1], axis, pairs)
-    slots = [shard]
+    slots, owners = [shard], [here]
     tables = [arrivals(n, c) for c in range(n)]
     for slot in range(n - 1):
         users = {}
+        origins = []
         for c in range(n):
-            users.setdefault(tables[c][slot], []).append(c)
+            links, step = tables[c][slot]
+            users.setdefault((links, step), []).append(c)
+            origins.append(c + step if links == c % 2 else c - step)
         choice = None
         for source, places in users.items():
             if choice is None:
@@ -156,13 +159,55 @@
                 mine = functools.reduce(jnp.logical_or, [here == c for c in places])
                 choice = jnp.where(mine, came[source], choice)
         slots.append(choice)
-    return slots
-
-
-def row_sum(parts, earlier):
-    if earlier is not None:
-        parts, _ = lax.optimization_barrier((parts, earlier))
-    return lax.psum(parts, "row")
+        owners.append(jnp.array(origins, dtype=jnp.int32)[here])
+    return slots, owners, came[0, 1]
+
+
+def halving_sum(part, axis):
+    n = lax.axis_size(axis)
+    here = lax.axis_index(axis)
+    bit = 1
+    while bit < n:
+        half = part.shape[-2] // 2
+        high = (here // bit) % 2
+        kept = lax.dynamic_slice_in_dim(part, high * half, half, axis=-2)
+        sent = lax.dynamic_slice_in_dim(part, (1 - high) * half, half, axis=-2)
+        came = lax.ppermute(sent, axis, [(i, i ^ bit) for i in range(n)])
+        part = kept + came
+        bit *= 2
+    return part
+
+
+def doubling_gather(part, axis):
+    n = lax.axis_size(axis)
+    here = lax.axis_index(axis)
+    bit = n // 2
+    while bit:
+        came = lax.ppermute(part, axis, [(i, i ^ bit) for i in range(n)])
+        part = jnp.where(
+            (here // bit) % 2 == 1,
+            jnp.concatenate([came, part], axis=-2),
+            jnp.concatenate([part, came], axis=-2),
+        )
+        bit //= 2
+    return part
+
+
+def response_codes(logratio, token_session, token_position, pad_mask):
+    live = pad_mask.astype(jnp.float32)
+    response = (token_session * LIST + token_position).astype(jnp.float32)
+    return jnp.stack([live * logratio, jnp.where(pad_mask != 0, response, -1.0)])
+
+
+def coefficients(codes):
+    n, _, rows = codes.shape
+    onehot = (
+        codes[:, 1, :, None] == jnp.arange(SESSIONS * LIST, dtype=jnp.float32)
+    ).astype(jnp.float32)
+    sums = jnp.sum(onehot * codes[:, 0, :, None], axis=(0, 1))
+    scores = math.sqrt(SESSIONS * LIST / (n * rows)) * sums
+    response_grad = listwise_grad(scores)
+    return 0.1 * jnp.sum(onehot * response_grad, axis=2)
 
 
 def on_device(
@@ -180,45 +225,49 @@
     v_out,
 ):
     n = lax.axis_size("col")
-    token_slots = line_gather(tokens, "col")
-    all_rows = tokens.shape[0] * n
-    response = token_session * LIST + token_position
-    onehot = (response[:, None] == jnp.arange(SESSIONS * LIST, dtype=jnp.int32)[None, :]).astype(
-        jnp.float32
-    )
-    live = pad_mask.astype(jnp.float32)
-    local_sums = jnp.sum(onehot * (live * logratio)[:, None], axis=0)
-    factor = math.sqrt(SESSIONS * LIST / all_rows)
-    scores = factor * lax.psum(local_sums, "col")
-    response_grad = listwise_grad(scores)
-    coeff = 0.1 * live * jnp.sum(onehot * response_grad[None, :], axis=1)
-    dy = (coeff[:, None] * out_grad.astype(jnp.float32)).astype(jnp.bfloat16)
-    dy_slots = line_gather(dy, "col")
+    token_slots, owners, first = line_gather(tokens, "col")
+    out_grad_slots, _, _ = line_gather(out_grad, "col")
+    codes = response_codes(logratio, token_session, token_position, pad_mask)
+    codes, _ = lax.optimization_barrier((codes, first))
+    coeff = coefficients(lax.all_gather(codes, "col", axis=0))
     w_in16, w_out16 = lax.optimization_barrier(
         (w_in.astype(jnp.bfloat16), w_out.astype(jnp.bfloat16))
     )
-    acts, dpres = [], []
-    last = None
-    for slot in range(n - 1):
-        pre_part = jnp.dot(token_slots[slot], w_in16, preferred_element_type=jnp.float32)
-        back_part = against(dy_slots[slot], w_out16)
-        pre, back = last = row_sum((pre_part, back_part), last)
+
+    def scaled(slot):
+        mine = lax.dynamic_index_in_dim(coeff, owners[slot], 0, keepdims=False)
+        return (mine[:, None] * out_grad_slots[slot].astype(jnp.float32)).astype(jnp.bfloat16)
+
+    def pre_of(slot):
+        return jnp.dot(token_slots[slot], w_in16, preferred_element_type=jnp.float32)
+
+    def square(pre):
         positive = jnp.maximum(pre, 0.0)
-        acts.append((positive * positive).astype(jnp.bfloat16))
-        dpres.append((back * 2.0 * positive).astype(jnp.bfloat16))
+        return (positive * positive).astype(jnp.bfloat16)
+
+    def chain(pre, back):
+        return (back * 2.0 * jnp.maximum(pre, 0.0)).astype(jnp.bfloat16)
+
+    early = range(n - 2)
+    dys = [scaled(slot) for slot in range(n - 1)]
+    sums = lax.psum([(pre_of(slot), against(dys[slot], w_out16)) for slot in early], "row")
+    acts = [square(pre) for pre, _ in sums]
+    dpres = [chain(pre, back) for pre, back in sums]
+    both = halving_sum(jnp.stack([pre_of(n - 2), against(dys[n - 2], w_out16)]), "row")
+    both = doubling_gather(jnp.stack([square(both[0]), chain(both[0], both[1])]), "row")
+    acts.append(both[0])
+    dpres.append(both[1])
     grad_in = grad_sum(token_slots[:-1], dpres, 256)
-    grad_out = grad_sum(acts, dy_slots[:-1], 128)
-    tokens_last, dy_last = token_slots[-1], dy_slots[-1]
-    pre_part = jnp.dot(tokens_last, w_in16, preferred_element_type=jnp.float32)
-    (pre,) = last = row_sum((pre_part,), last)
-    positive = jnp.maximum(pre, 0.0)
-    act = (positive * positive).astype(jnp.bfloat16)
-    dy_last, grad_in, grad_out = lax.optimization_barrier((dy_last, grad_in, grad_out))
-    (back,) = row_sum((against(dy_last, w_out16),), last)
-    outs_out = update(act, dy_last, grad_out, w_out, m_out, v_out, 128)
-    back, outs_out = lax.optimization_barrier((back, outs_out))
-    dpre = (back * 2.0 * positive).astype(jnp.bfloat16)
-    outs_in = update(tokens_last, dpre, grad_in, w_in, m_in, v_in, 256)
+    grad_out = grad_sum(acts, dys, 128)
+
+    pre = halving_sum(pre_of(n - 1), "row")
+    act = doubling_gather(square(pre), "row")
+    dy = scaled(n - 1)
+    dy, grad_in, grad_out, act = lax.optimization_barrier((dy, grad_in, grad_out, act))
+    back = halving_sum(against(dy, w_out16), "row")
+    outs_out = update(act, dy, grad_out, w_out, m_out, v_out, 128)
+    dpre = doubling_gather(chain(pre, back), "row")
+    outs_in = update(token_slots[-1], dpre, grad_in, w_in, m_in, v_in, 256)
     return (*outs_in, *outs_out)
 
 

time: 448 us -> 411 us (0.917)
  waiting for transfers between devices: 286 us -> 164 us
  blocking collectives: 13.5 us -> 80.9 us
  starting transfers between devices: 15.6 us -> 32.4 us
  between operations: 14 us -> 20.6 us
    psum x5 -> x1, waiting for transfers between devices: 188 us -> 59.1 us  [on_device(): lax.psum([(pre_of(slot), against(dys[slot], w_out16)) for slot in early],...]
    all_gather x0 -> x1, blocking collectives: none -> 80.9 us  [on_device(): coeff = coefficients(lax.all_gather(codes, 'col', axis=0))]
    ppermute x0 -> x18, waiting for transfers between devices: none -> 40.6 us  [the longest x9 26.6 us: halving_sum(): came = lax.ppermute(sent, axis, [(i, i ^ bit) for i in range(n)])]
    ppermute x10, waiting for transfers between devices: 97.7 us -> 64.8 us  [line_gather(): came[links, step] = lax.ppermute(came[1 - links, step - 1], axis, pairs)]
    psum x1 -> x0, blocking collectives: 13.5 us -> none  [on_device(): scores = factor * lax.psum(local_sums, 'col')]
    ppermute x0 -> x18, starting transfers between devices: none -> 13.3 us  [the longest x9 7.17 us: halving_sum(): came = lax.ppermute(sent, axis, [(i, i ^ bit) for i in range(n)])]
    unnamed x40 -> x49, local copies, waits for them, and re-layouts: 9.48 us -> 3.68 us
    dynamic_slice x0 -> x12, local copies, waits for them, and re-layouts: none -> 5.65 us  [the longest x3 3.74 us: line_gather(): owners.append(jnp.array(origins, dtype=jnp.int32)[here])]
  transfers between devices with their start and end apart: 15 -> 29, of which waited for: 9 -> 14; matrix products, arithmetic and copies ran while one was open for 10% -> 12% of each run, Pallas kernels for 9% -> 9%
where the time goes in v2:
time: 411 us; the launch traced here: 410 us
  waiting for transfers between devices  164 us (40%)
  blocking collectives  80.9 us (20%)
  Pallas kernels  55.7 us (14%)
  starting transfers between devices  32.4 us (8%)
  other arithmetic  25.2 us (6%)
  matrix products  20.7 us (5%)
  between operations  20.6 us (5%)
  local copies, waits for them, and re-layouts  9.75 us (2%)
    all_gather x1, blocking collectives, on_device(): coeff = coefficients(lax.all_gather(codes, 'col', axis=0))  80.9 us
    ppermute x10, waiting for transfers between devices, line_gather(): came[links, step] = lax.ppermute(came[1 - links, step - 1], axis, pairs)  64.8 us
    psum x1, waiting for transfers between devices, on_device(): lax.psum([(pre_of(slot), against(dys[slot], w_out16)) for slot in early],...  59.1 us
    pallas_call x2, Pallas kernels, update(): pl.pallas_call(update_kernel, grid=(height // block,), in_specs=[pl.Block...  38.9 us
    ppermute x9, waiting for transfers between devices, halving_sum(): came = lax.ppermute(sent, axis, [(i, i ^ bit) for i in range(n)])  26.6 us
    ppermute x10, starting transfers between devices, line_gather(): came[links, step] = lax.ppermute(came[1 - links, step - 1], axis, pairs)  19.1 us
    pallas_call x2, Pallas kernels, grad_sum(): pl.pallas_call(functools.partial(grad_kernel, parts), grid=(height // blo...  16.8 us
    ppermute x9, waiting for transfers between devices, doubling_gather(): came = lax.ppermute(part, axis, [(i, i ^ bit) for i in range(n)])  13.9 us
  transfers between devices with their start and end apart: 29, of which 14 were waited for; matrix products, arithmetic and copies ran while one was open for 12% of the time, Pallas kernels for 9%

profile of v2, /device:TPU:0, one launch (start us, length us, event | category | flops | bytes accessed | tf_op | source)
XLA Modules:
  0.0 409.8 jit_solution(5384067083643495546)
XLA Ops:
  7.2 3.1 collective-permute-start
  12.2 3.2 collective-permute-start.3
  25.9 5.3 %convert_element_type.85 = bf16[2304,768]{1,0:T(8,128)(2,1)} convert(f32[2304,768]{1,0:T(8,128)} %w.2) | non-fusion elementwise | flops 1769472 | bytes 10616832 | tf_op jit(solution)/shard_map/convert_element_type | solution.py:234
  36.8 4.6 %convolution_bitcast_fusion.1 = f32[384,768]{1,0:T(8,128)} fusion(bf16[384,2304]{1,0:T(8,128)(2,1)S(1)} %copy-done.8, bf16[2304,768]{1,0:T(8,128)(2,1)} %convert_element_type.85), kind=kOutput, calls=%fused_computation.11 | convolution fusion | flops 1358954496 | bytes 6488064 | tf_op jit(solution)/shard_map/dot_general | solution.py:242
  41.4 8.6 %collective-permute-done.refs_1_ = bf16[384,2304]{1,0:T(8,128)(2,1)S(1)} collective-permute-done((bf16[384,2304]{1,0:T(8,128)(2,1)}, bf16[384,2304]{1,0:T(8,128)(2,1)S(1)}, u32[]{:S(2)}, u32[]{:S(2)}) %collective-permute-start) | collective-permute-done | bytes 1769504 | tf_op jit(solution)/shard_map/ppermute | solution.py:144
  51.2 80.9 %all-gather.1 = f32[4,2,384]{2,1,0:T(2,128)S(1)} all-gather(f32[1,2,384]{2,1,0:T(2,128)S(1)} %bitcast.40), channel_id=2, replica_groups=mesh['row'=8,'col'=4] {'col'}, dimensions={0}, use_global_device_ids=true | all-gather | bytes 15360 | tf_op jit(solution)/shard_map/all_gather | solution.py:232
  139.2 36.2 %collective-permute-done.7 = bf16[384,2304]{1,0:T(8,128)(2,1)S(1)} collective-permute-done((bf16[384,2304]{1,0:T(8,128)(2,1)}, bf16[384,2304]{1,0:T(8,128)(2,1)S(1)}, u32[]{:S(2)}, u32[]{:S(2)}) %collective-permute-start.7) | collective-permute-done | bytes 1769504 | tf_op jit(solution)/shard_map/ppermute | solution.py:144
  183.2 2.6 fusion.22
  187.4 2.6 fusion.21
  190.0 2.6 convolution_bitcast_fusion
  194.6 7.3 %collective-permute-done.11 = f32[2,96,768]{2,1,0:T(8,128)} collective-permute-done((f32[2,96,768]{2,1,0:T(8,128)S(1)}, f32[2,96,768]{2,1,0:T(8,128)}, u32[]{:S(2)}, u32[]{:S(2)}) %collective-permute-start.11) | collective-permute-done | bytes 589856 | tf_op jit(solution)/shard_map/ppermute | solution.py:175
  205.2 19.9 %collective-permute-done.2 = bf16[384,2304]{1,0:T(8,128)(2,1)} collective-permute-done((bf16[384,2304]{1,0:T(8,128)(2,1)}, bf16[384,2304]{1,0:T(8,128)(2,1)}, u32[]{:S(2)}, u32[]{:S(2)}) %collective-permute-start.2) | collective-permute-done | bytes 1769504 | tf_op jit(solution)/shard_map/ppermute | solution.py:144
  236.0 59.1 %all-reduce.3.cloned.1.call-done = (f32[384,768]{1,0:T(8,128)}, f32[384,768]{1,0:T(8,128)}, f32[384,768]{1,0:T(8,128)}, f32[384,768]{1,0:T(8,128)}) async-done(((f32[384,768]{1,0:T(8,128)}, f32[384,768]{1,0:T(8,128)}, f32[384,768]{1,0:T(8,128)}, f32[384,768]{1,0:T(8,128)}), (f32[384,768]{1,0:T(8,128)}, f32[384,768]{1,0:T(8,128)}, f32[384,768]{1,0:T(8,128)}, ...) | async-done | bytes 4718608 | tf_op jit(solution)/shard_map/psum | solution.py:253
  299.7 4.4 %collective-permute-done.18 = f32[48,768]{1,0:T(8,128)S(1)} collective-permute-done((f32[48,768]{1,0:T(8,128)S(1)}, f32[48,768]{1,0:T(8,128)S(1)}, u32[]{:S(2)}, u32[]{:S(2)}) %collective-permute-start.18) | collective-permute-done | bytes 147488 | tf_op jit(solution)/shard_map/ppermute | solution.py:175
  311.3 2.4 collective-permute-done.20
  316.1 8.1 %shard_map.191.grad = f32[768,2304]{1,0:T(8,128)} custom-call(bf16[384,768]{1,0:T(8,128)(2,1)S(1)} %get-tuple-element.46.refs_0_, bf16[384,768]{1,0:T(8,128)(2,1)S(1)} %get-tuple-element.44.refs_1_, bf16[384,768]{1,0:T(8,128)(2,1)S(1)} %get-tuple-element.42.refs_2_, bf16[384,2304]{1,0:T(8,128)(2,1)S(1)} %copy-done.1, bf16[384,2304]{1,0:T(8,128)(2,1)S(1)} %copy-done.7, ...), custom_call_target="tpu_custom_call" | custom-call | flops 4076863488 | bytes 14155776 | tf_op jit(solution)/shard_map/pallas_call | solution.py:68
  324.2 8.7 %shard_map.190.grad = f32[2304,768]{1,0:T(8,128)} custom-call(bf16[384,2304]{1,0:T(8,128)(2,1)S(1)} %copy-done.9, bf16[384,2304]{1,0:T(8,128)(2,1)S(1)} %copy-done.11, bf16[384,2304]{1,0:T(8,128)(2,1)S(1)} %copy-done.3, bf16[384,768]{1,0:T(8,128)(2,1)S(1)} %get-tuple-element.47.refs_3_, bf16[384,768]{1,0:T(8,128)(2,1)S(1)} %get-tuple-element.45.refs_4_, ...), custom_call_target="tpu_custom_call" | custom-call | flops 4076863488 | bytes 14155776 | tf_op jit(solution)/shard_map/pallas_call | solution.py:68
  333.0 3.7 fusion.24
  339.7 8.7 %collective-permute-done.23 = f32[96,768]{1,0:T(8,128)S(1)} collective-permute-done((f32[96,768]{1,0:T(8,128)S(1)}, f32[96,768]{1,0:T(8,128)S(1)}, u32[]{:S(2)}, u32[]{:S(2)}) %collective-permute-start.23) | collective-permute-done | bytes 294944 | tf_op jit(solution)/shard_map/ppermute | solution.py:175
  349.4 4.5 %collective-permute-done.24 = f32[48,768]{1,0:T(8,128)S(1)} collective-permute-done((f32[48,768]{1,0:T(8,128)S(1)}, f32[48,768]{1,0:T(8,128)S(1)}, u32[]{:S(2)}, u32[]{:S(2)}) %collective-permute-start.24) | collective-permute-done | bytes 147488 | tf_op jit(solution)/shard_map/ppermute | solution.py:175
  354.8 3.6 collective-permute-done.25
  359.0 4.6 %collective-permute-done.26 = bf16[96,768]{1,0:T(8,128)(2,1)S(1)} collective-permute-done((bf16[96,768]{1,0:T(8,128)(2,1)S(1)}, bf16[96,768]{1,0:T(8,128)(2,1)S(1)}, u32[]{:S(2)}, u32[]{:S(2)}) %collective-permute-start.26) | collective-permute-done | bytes 147488 | tf_op jit(solution)/shard_map/ppermute | solution.py:186
  363.8 18.4 %shard_map.193 = (f32[768,2304]{1,0:T(8,128)}, f32[768,2304]{1,0:T(8,128)}, f32[768,2304]{1,0:T(8,128)}) custom-call(bf16[384,768]{1,0:T(8,128)(2,1)S(1)} %maximum_select_fusion.2.left, bf16[384,2304]{1,0:T(8,128)(2,1)S(1)} %multiply_convert_fusion.3.right, f32[768,2304]{1,0:T(8,128)S(1)} %bitcast.39, f32[768,2304]{1,0:T(8,128)} %w.3, f32[768,2304]{1,0:T(8,128)} %m.3, ...), custom_call_target="tpu_custom_call" | custom-call | flops 1358954496 | bytes 51904512 | tf_op jit(solution)/shard_map/pallas_call | solution.py:95
  382.3 20.6 %shard_map.192 = (f32[2304,768]{1,0:T(8,128)}, f32[2304,768]{1,0:T(8,128)}, f32[2304,768]{1,0:T(8,128)}) custom-call(bf16[384,2304]{1,0:T(8,128)(2,1)S(1)} %broadcast_select_fusion.1.left, bf16[384,768]{1,0:T(8,128)(2,1)S(1)} %maximum_select_fusion.3.right, f32[2304,768]{1,0:T(8,128)S(1)} %bitcast.37, f32[2304,768]{1,0:T(8,128)} %w.2, f32[2304,768]{1,0:T(8,128)} %m.2, ...), custom_call_target="tpu_custom_call" | custom-call | flops 1358954496 | bytes 51904512 | tf_op jit(solution)/shard_map/pallas_call | solution.py:95
  (159 shorter events, 65.4 us)
Async XLA Ops:
  7.2 288.0 %all-reduce.3.cloned.1.call-start = ((), (), s32[]{:S(2)}) async-start(), calls=%async_computation | async-start | bytes 9437184 | tf_op jit(solution)/shard_map/psum | solution.py:253
  7.2 42.7 %collective-permute-start = (bf16[384,2304]{1,0:T(8,128)(2,1)}, bf16[384,2304]{1,0:T(8,128)(2,1)S(1)}, u32[]{:S(2)}, u32[]{:S(2)}) collective-permute-start(bf16[384,2304]{1,0:T(8,128)(2,1)} %refs_0_.1), channel_id=1, source_target_pairs={{0,1},{1,0},{2,3},{3,2},{4,5},{5,4},{6,7},{7,6},{8,9},{9,8},{10,11... | collective-permute-start | bytes 5308424 | tf_op jit(solution)/shard_map/ppermute | solution.py:144
  10.3 39.7 %collective-permute-start.8 = (bf16[384,2304]{1,0:T(8,128)(2,1)}, bf16[384,2304]{1,0:T(8,128)(2,1)}, u32[]{:S(2)}, u32[]{:S(2)}) collective-permute-start(bf16[384,2304]{1,0:T(8,128)(2,1)} %param.16), channel_id=1, source_target_pairs={{1,2},{2,1},{5,6},{6,5},{9,10},{10,9},{13,14},{14,13},{17,18},{18,... | collective-permute-start | bytes 5308424 | tf_op jit(solution)/shard_map/ppermute | solution.py:144
  12.2 167.9 %collective-permute-start.3 = (bf16[384,2304]{1,0:T(8,128)(2,1)}, bf16[384,2304]{1,0:T(8,128)(2,1)}, u32[]{:S(2)}, u32[]{:S(2)}) collective-permute-start(bf16[384,2304]{1,0:T(8,128)(2,1)} %param.16), channel_id=1, source_target_pairs={{0,1},{1,0},{2,3},{3,2},{4,5},{5,4},{6,7},{7,6},{8,9},{9,8},{10,11... | collective-permute-start | bytes 5308424 | tf_op jit(solution)/shard_map/ppermute | solution.py:144
  15.4 119.9 %collective-permute-start.6 = (bf16[384,2304]{1,0:T(8,128)(2,1)}, bf16[384,2304]{1,0:T(8,128)(2,1)}, u32[]{:S(2)}, u32[]{:S(2)}) collective-permute-start(bf16[384,2304]{1,0:T(8,128)(2,1)} %refs_0_.1), channel_id=1, source_target_pairs={{1,2},{2,1},{5,6},{6,5},{9,10},{10,9},{13,14},{14,13},{17,18},{18,... | collective-permute-start | bytes 5308424 | tf_op jit(solution)/shard_map/ppermute | solution.py:144
  50.0 88.7 %collective-permute-start.9 = (bf16[384,2304]{1,0:T(8,128)(2,1)}, bf16[384,2304]{1,0:T(8,128)(2,1)S(1)}, u32[]{:S(2)}, u32[]{:S(2)}) collective-permute-start(bf16[384,2304]{1,0:T(8,128)(2,1)} %collective-permute-done.8), channel_id=1, source_target_pairs={{1,0},{2,3},{5,4},{6,7},{9,8},{10,11},{13,12},{14,15},{17,16},{18,... | collective-permute-start | bytes 5308424 | tf_op jit(solution)/shard_map/ppermute | solution.py:144
  133.5 48.5 %collective-permute-start.1 = (bf16[384,2304]{1,0:T(8,128)(2,1)S(1)}, bf16[384,2304]{1,0:T(8,128)(2,1)}, u32[]{:S(2)}, u32[]{:S(2)}) collective-permute-start(bf16[384,2304]{1,0:T(8,128)(2,1)S(1)} %collective-permute-done.refs_1_), channel_id=1, source_target_pairs={{1,2},{2,1},{5,6},{6,5},{9,10},{10,9},{13,14},{14,13},{17,18},{18,... | collective-permute-start | bytes 5308424 | tf_op jit(solution)/shard_map/ppermute | solution.py:144
  135.4 40.1 %collective-permute-start.7 = (bf16[384,2304]{1,0:T(8,128)(2,1)}, bf16[384,2304]{1,0:T(8,128)(2,1)S(1)}, u32[]{:S(2)}, u32[]{:S(2)}) collective-permute-start(bf16[384,2304]{1,0:T(8,128)(2,1)} %collective-permute-done.6), channel_id=1, source_target_pairs={{1,0},{2,3},{5,4},{6,7},{9,8},{10,11},{13,12},{14,15},{17,16},{18,... | collective-permute-start | bytes 5308424 | tf_op jit(solution)/shard_map/ppermute | solution.py:144
  180.0 5.9 %collective-permute-start.10 = (f32[2,192,768]{2,1,0:T(8,128)S(1)}, f32[2,192,768]{2,1,0:T(8,128)S(1)}, u32[]{:S(2)}, u32[]{:S(2)}) collective-permute-start(f32[2,192,768]{2,1,0:T(8,128)S(1)} %fusion), channel_id=1, source_target_pairs={{0,4},{4,0},{8,12},{12,8},{16,20},{20,16},{24,28},{28,24},{1,5},{5... | collective-permute-start | bytes 3538952 | tf_op jit(solution)/shard_map/ppermute | solution.py:175
  181.9 43.2 %collective-permute-start.2 = (bf16[384,2304]{1,0:T(8,128)(2,1)}, bf16[384,2304]{1,0:T(8,128)(2,1)}, u32[]{:S(2)}, u32[]{:S(2)}) collective-permute-start(bf16[384,2304]{1,0:T(8,128)(2,1)} %collective-permute-done.1), channel_id=1, source_target_pairs={{1,0},{2,3},{5,4},{6,7},{9,8},{10,11},{13,12},{14,15},{17,16},{18,... | collective-permute-start | bytes 5308424 | tf_op jit(solution)/shard_map/ppermute | solution.py:144
  186.0 15.9 %collective-permute-start.11 = (f32[2,96,768]{2,1,0:T(8,128)S(1)}, f32[2,96,768]{2,1,0:T(8,128)}, u32[]{:S(2)}, u32[]{:S(2)}) collective-permute-start(f32[2,96,768]{2,1,0:T(8,128)S(1)} %constant_dynamic-slice_fusion.7), channel_id=1, source_target_pairs={{0,8},{4,12},{8,0},{12,4},{16,24},{20,28},{24,16},{28,20},{1,9},{5... | collective-permute-start | bytes 1769480 | tf_op jit(solution)/shard_map/ppermute | solution.py:175
  192.7 36.7 %collective-permute-start.4 = (bf16[384,2304]{1,0:T(8,128)(2,1)}, bf16[384,2304]{1,0:T(8,128)(2,1)}, u32[]{:S(2)}, u32[]{:S(2)}) collective-permute-start(bf16[384,2304]{1,0:T(8,128)(2,1)} %collective-permute-done.3), channel_id=1, source_target_pairs={{1,2},{2,1},{5,6},{6,5},{9,10},{10,9},{13,14},{14,13},{17,18},{18,... | collective-permute-start | bytes 5308424 | tf_op jit(solution)/shard_map/ppermute | solution.py:144
  203.8 26.8 %collective-permute-start.12 = (f32[2,48,768]{2,1,0:T(8,128)}, f32[2,48,768]{2,1,0:T(8,128)}, u32[]{:S(2)}, u32[]{:S(2)}) collective-permute-start(f32[2,48,768]{2,1,0:T(8,128)} %constant_dynamic-slice_fusion.6), channel_id=1, source_target_pairs={{0,16},{4,20},{8,24},{12,28},{16,0},{20,4},{24,8},{28,12},{1,17},{... | collective-permute-start | bytes 884744 | tf_op jit(solution)/shard_map/ppermute | solution.py:175
  229.3 79.9 %collective-permute-start.5 = (bf16[384,2304]{1,0:T(8,128)(2,1)}, bf16[384,2304]{1,0:T(8,128)(2,1)}, u32[]{:S(2)}, u32[]{:S(2)}) collective-permute-start(bf16[384,2304]{1,0:T(8,128)(2,1)} %collective-permute-done.4), channel_id=1, source_target_pairs={{1,0},{2,3},{5,4},{6,7},{9,8},{10,11},{13,12},{14,15},{17,16},{18,... | collective-permute-start | bytes 5308424 | tf_op jit(solution)/shard_map/ppermute | solution.py:144
  231.8 65.3 %collective-permute-start.13 = (bf16[2,48,768]{2,1,0:T(8,128)(2,1)S(1)}, bf16[2,48,768]{2,1,0:T(8,128)(2,1)S(1)}, u32[]{:S(2)}, u32[]{:S(2)}) collective-permute-start(bf16[2,48,768]{2,1,0:T(8,128)(2,1)S(1)} %pad_maximum_fusion), channel_id=1, source_target_pairs={{0,16},{4,20},{8,24},{12,28},{16,0},{20,4},{24,8},{28,12},{1,17},{... | collective-permute-start | bytes 442376 | tf_op jit(solution)/shard_map/ppermute | solution.py:186
  234.5 64.3 %collective-permute-start.17 = (f32[96,768]{1,0:T(8,128)S(1)}, f32[96,768]{1,0:T(8,128)S(1)}, u32[]{:S(2)}, u32[]{:S(2)}) collective-permute-start(f32[96,768]{1,0:T(8,128)S(1)} %constant_dynamic-slice_fusion.4), channel_id=1, source_target_pairs={{0,8},{4,12},{8,0},{12,4},{16,24},{20,28},{24,16},{28,20},{1,9},{5... | collective-permute-start | bytes 884744 | tf_op jit(solution)/shard_map/ppermute | solution.py:175
  297.2 8.8 %collective-permute-start.14 = (bf16[2,96,768]{2,1,0:T(8,128)(2,1)S(1)}, bf16[2,96,768]{2,1,0:T(8,128)(2,1)S(1)}, u32[]{:S(2)}, u32[]{:S(2)}) collective-permute-start(bf16[2,96,768]{2,1,0:T(8,128)(2,1)S(1)} %maximum_select_fusion.4), channel_id=1, source_target_pairs={{0,8},{4,12},{8,0},{12,4},{16,24},{20,28},{24,16},{28,20},{1,9},{5... | collective-permute-start | bytes 884744 | tf_op jit(solution)/shard_map/ppermute | solution.py:186
  298.8 5.3 %collective-permute-start.18 = (f32[48,768]{1,0:T(8,128)S(1)}, f32[48,768]{1,0:T(8,128)S(1)}, u32[]{:S(2)}, u32[]{:S(2)}) collective-permute-start(f32[48,768]{1,0:T(8,128)S(1)} %constant_dynamic-slice_fusion.3), channel_id=1, source_target_pairs={{0,16},{4,20},{8,24},{12,28},{16,0},{20,4},{24,8},{28,12},{1,17},{... | collective-permute-start | bytes 442376 | tf_op jit(solution)/shard_map/ppermute | solution.py:175
  306.1 7.8 %collective-permute-start.15 = (bf16[2,192,768]{2,1,0:T(8,128)(2,1)S(1)}, bf16[2,192,768]{2,1,0:T(8,128)(2,1)S(1)}, u32[]{:S(2)}, u32[]{:S(2)}) collective-permute-start(bf16[2,192,768]{2,1,0:T(8,128)(2,1)S(1)} %maximum_select_fusion.1), channel_id=1, source_target_pairs={{0,4},{4,0},{8,12},{12,8},{16,20},{20,16},{24,28},{28,24},{1,5},{5... | collective-permute-start | bytes 1769480 | tf_op jit(solution)/shard_map/ppermute | solution.py:186
  308.6 5.2 %collective-permute-start.20 = (bf16[96,768]{1,0:T(8,128)(2,1)S(1)}, bf16[96,768]{1,0:T(8,128)(2,1)S(1)}, u32[]{:S(2)}, u32[]{:S(2)}) collective-permute-start(bf16[96,768]{1,0:T(8,128)(2,1)S(1)} %maximum_select_fusion.7), channel_id=1, source_target_pairs={{0,8},{4,12},{8,0},{12,4},{16,24},{20,28},{24,16},{28,20},{1,9},{5... | collective-permute-start | bytes 442376 | tf_op jit(solution)/shard_map/ppermute | solution.py:186
  313.8 19.0 %collective-permute-start.21 = (bf16[192,768]{1,0:T(8,128)(2,1)S(1)}, bf16[192,768]{1,0:T(8,128)(2,1)S(1)}, u32[]{:S(2)}, u32[]{:S(2)}) collective-permute-start(bf16[192,768]{1,0:T(8,128)(2,1)S(1)} %maximum_select_fusion.5), channel_id=1, source_target_pairs={{0,4},{4,0},{8,12},{12,8},{16,20},{20,16},{24,28},{28,24},{1,5},{5... | collective-permute-start | bytes 884744 | tf_op jit(solution)/shard_map/ppermute | solution.py:186
  339.1 9.4 %collective-permute-start.23 = (f32[96,768]{1,0:T(8,128)S(1)}, f32[96,768]{1,0:T(8,128)S(1)}, u32[]{:S(2)}, u32[]{:S(2)}) collective-permute-start(f32[96,768]{1,0:T(8,128)S(1)} %constant_dynamic-slice_fusion.1), channel_id=1, source_target_pairs={{0,8},{4,12},{8,0},{12,4},{16,24},{20,28},{24,16},{28,20},{1,9},{5... | collective-permute-start | bytes 884744 | tf_op jit(solution)/shard_map/ppermute | solution.py:175
  348.5 5.4 %collective-permute-start.24 = (f32[48,768]{1,0:T(8,128)S(1)}, f32[48,768]{1,0:T(8,128)S(1)}, u32[]{:S(2)}, u32[]{:S(2)}) collective-permute-start(f32[48,768]{1,0:T(8,128)S(1)} %constant_dynamic-slice_fusion), channel_id=1, source_target_pairs={{0,16},{4,20},{8,24},{12,28},{16,0},{20,4},{24,8},{28,12},{1,17},{... | collective-permute-start | bytes 442376 | tf_op jit(solution)/shard_map/ppermute | solution.py:175
  363.7 18.5 %collective-permute-start.27 = (bf16[192,768]{1,0:T(8,128)(2,1)S(1)}, bf16[192,768]{1,0:T(8,128)(2,1)S(1)}, u32[]{:S(2)}, u32[]{:S(2)}) collective-permute-start(bf16[192,768]{1,0:T(8,128)(2,1)S(1)} %maximum_select_fusion.6), channel_id=1, source_target_pairs={{0,4},{4,0},{8,12},{12,8},{16,20},{20,16},{24,28},{28,24},{1,5},{5... | collective-permute-start | bytes 884744 | tf_op jit(solution)/shard_map/ppermute | solution.py:186
  (29 other events, 469.0 us)
Sparse Core Ops, SparseCore 0:
  192.8 102.3 all-reduce.2

commit v3 on v2

--- a/solution.py
+++ b/solution.py
@@ -25,12 +25,13 @@
 
 def adamw(weight, first, second, grad):
     new_first = 0.9 * first + 0.1 * grad
-    new_second = 0.95 * second + 0.05 * grad * grad
-    step = (
-        new_first / (1.0 - 0.9**20) / (jnp.sqrt(new_second / (1.0 - 0.95**20)) + 1e-08)
-        + 0.1 * weight
-    )
-    return (weight - 0.0003 * step, new_first, new_second)
+    new_second = 0.95 * second + 0.05 * (grad * grad)
+    scaled = new_second * (1.0 / (1.0 - 0.95**20))
+    below = scaled * lax.rsqrt(scaled) + 1e-08
+    inverse = pl.reciprocal(below, approx=True)
+    inverse = inverse * (2.0 - below * inverse)
+    step = (0.0003 / (1.0 - 0.9**20)) * (new_first * inverse)
+    return (weight * (1.0 - 0.0003 * 0.1) - step, new_first, new_second)
 
 
 def over_rows(left, right):
@@ -81,37 +82,40 @@
     )(*lefts, *rights)
 
 
-def update_kernel(left, right, grad, w, m, v, new_w, new_m, new_v):
+def update_kernel(left, right, grad, w, m, v, *refs):
+    new_w, new_m, new_v = refs[-3:]
     total = grad[...] + over_rows(left[...], right[...])
     new_w[...], new_m[...], new_v[...] = adamw(w[...], m[...], v[...], total)
 
 
-def update(left, right, grad, w, m, v, most):
+def update(left, right, grad, w, m, v, rows_most, part=0, parts=1, so_far=()):
     rows, height = left.shape
-    width = right.shape[1]
-    block = block_of(height, most)
-    panel = pl.BlockSpec((block, width), lambda i: (i, 0))
-    shape = jax.ShapeDtypeStruct((height, width), jnp.float32)
+    width = right.shape[1] // parts
+    block = block_of(height, rows_most)
+    panel = pl.BlockSpec((block, width), lambda i: (i, part))
+    shape = jax.ShapeDtypeStruct(w.shape, jnp.float32)
     return pl.pallas_call(
         update_kernel,
         grid=(height // block,),
         in_specs=[
             pl.BlockSpec((rows, block), lambda i: (0, i)),
-            pl.BlockSpec((rows, width), lambda i: (0, 0)),
+            pl.BlockSpec((rows, width), lambda i: (0, part)),
             panel,
             panel,
             panel,
             panel,
-        ],
+        ]
+        + [pl.BlockSpec(memory_space=pl.ANY)] * len(so_far),
         out_specs=[panel] * 3,
         out_shape=[shape] * 3,
-        compiler_params=pltpu.CompilerParams(vmem_limit_bytes=44 * 2**20),
+        input_output_aliases={6 + i: i for i in range(len(so_far))},
+        compiler_params=pltpu.CompilerParams(vmem_limit_bytes=56 * 2**20),
         cost_estimate=pl.CostEstimate(
             flops=2 * rows * height * width,
             bytes_accessed=7 * 4 * height * width + 2 * rows * (height + width),
             transcendentals=2 * height * width,
         ),
-    )(left, right, grad, w, m, v)
+    )(left, right, grad, w, m, v, *so_far)
 
 
 def link_pairs(n, first, step):
@@ -160,10 +164,16 @@
                 choice = jnp.where(mine, came[source], choice)
         slots.append(choice)
         owners.append(jnp.array(origins, dtype=jnp.int32)[here])
-    return slots, owners, came[0, 1]
-
-
-def halving_sum(part, axis):
+    return slots, owners
+
+
+def together(came, beside):
+    if beside:
+        came, _ = lax.optimization_barrier((came, beside.pop(0)()))
+    return came
+
+
+def halving_sum(part, axis, beside=None):
     n = lax.axis_size(axis)
     here = lax.axis_index(axis)
     bit = 1
@@ -173,17 +183,20 @@
         kept = lax.dynamic_slice_in_dim(part, high * half, half, axis=-2)
         sent = lax.dynamic_slice_in_dim(part, (1 - high) * half, half, axis=-2)
         came = lax.ppermute(sent, axis, [(i, i ^ bit) for i in range(n)])
+        if bit > 1:
+            came = together(came, beside)
         part = kept + came
         bit *= 2
     return part
 
 
-def doubling_gather(part, axis):
+def doubling_gather(part, axis, beside=None):
     n = lax.axis_size(axis)
     here = lax.axis_index(axis)
     bit = n // 2
     while bit:
         came = lax.ppermute(part, axis, [(i, i ^ bit) for i in range(n)])
+        came = together(came, beside)
         part = jnp.where(
             (here // bit) % 2 == 1,
             jnp.concatenate([came, part], axis=-2),
@@ -225,17 +238,28 @@
     v_out,
 ):
     n = lax.axis_size("col")
-    token_slots, owners, first = line_gather(tokens, "col")
-    out_grad_slots, _, _ = line_gather(out_grad, "col")
+    here = lax.axis_index("col")
+    token_slots, owners = line_gather(tokens, "col")
     codes = response_codes(logratio, token_session, token_position, pad_mask)
-    codes, _ = lax.optimization_barrier((codes, first))
-    coeff = coefficients(lax.all_gather(codes, "col", axis=0))
+    codes = jnp.stack(
+        [codes]
+        + [
+            lax.ppermute(codes, "col", [(i, (i + shift) % n) for i in range(n)])
+            for shift in range(1, n)
+        ]
+    )
+    out_grad, codes = lax.optimization_barrier((out_grad, codes))
+    out_grad_slots, _ = line_gather(out_grad, "col")
+    coeff = coefficients(codes)
     w_in16, w_out16 = lax.optimization_barrier(
         (w_in.astype(jnp.bfloat16), w_out.astype(jnp.bfloat16))
     )
 
-    def scaled(slot):
-        mine = lax.dynamic_index_in_dim(coeff, owners[slot], 0, keepdims=False)
+    def scaled(slot, after=None):
+        shift = (here - owners[slot] + n) % n
+        mine = lax.dynamic_index_in_dim(coeff, shift, 0, keepdims=False)
+        if after is not None:
+            mine, _ = lax.optimization_barrier((mine, after))
         return (mine[:, None] * out_grad_slots[slot].astype(jnp.float32)).astype(jnp.bfloat16)
 
     def pre_of(slot):
@@ -251,22 +275,35 @@
     early = range(n - 2)
     dys = [scaled(slot) for slot in range(n - 1)]
     sums = lax.psum([(pre_of(slot), against(dys[slot], w_out16)) for slot in early], "row")
-    acts = [square(pre) for pre, _ in sums]
-    dpres = [chain(pre, back) for pre, back in sums]
     both = halving_sum(jnp.stack([pre_of(n - 2), against(dys[n - 2], w_out16)]), "row")
     both = doubling_gather(jnp.stack([square(both[0]), chain(both[0], both[1])]), "row")
-    acts.append(both[0])
-    dpres.append(both[1])
+    sums, both = lax.optimization_barrier((sums, both))
+    acts = [square(pre) for pre, _ in sums] + [both[0]]
+    dpres = [chain(pre, back) for pre, back in sums] + [both[1]]
     grad_in = grad_sum(token_slots[:-1], dpres, 256)
     grad_out = grad_sum(acts, dys, 128)
 
     pre = halving_sum(pre_of(n - 1), "row")
     act = doubling_gather(square(pre), "row")
-    dy = scaled(n - 1)
-    dy, grad_in, grad_out, act = lax.optimization_barrier((dy, grad_in, grad_out, act))
-    back = halving_sum(against(dy, w_out16), "row")
-    outs_out = update(act, dy, grad_out, w_out, m_out, v_out, 128)
-    dpre = doubling_gather(chain(pre, back), "row")
+    dy = scaled(n - 1, (grad_in, grad_out, act))
+    parts = 3
+    outs_out = ()
+
+    def update_part(part):
+        def run():
+            nonlocal outs_out
+            outs_out = update(
+                act, dy, grad_out, w_out, m_out, v_out, 256, part, parts, outs_out
+            )
+            return outs_out
+
+        return run
+
+    beside = [update_part(part) for part in range(parts)]
+    back = halving_sum(against(dy, w_out16), "row", beside)
+    dpre = doubling_gather(chain(pre, back), "row", beside)
+    while beside:
+        beside.pop(0)()
     outs_in = update(token_slots[-1], dpre, grad_in, w_in, m_in, v_in, 256)
     return (*outs_in, *outs_out)
 

time: 411 us -> 420 us (1.022)
  blocking collectives: 80.9 us -> 0 us
  waiting for transfers between devices: 164 us -> 227 us
  Pallas kernels: 55.7 us -> 66.6 us
  other arithmetic: 25.2 us -> 35.3 us
  local copies, waits for them, and re-layouts: 9.75 us -> 17.7 us
  starting transfers between devices: 32.4 us -> 39.6 us
    all_gather x1 -> x0, blocking collectives: 80.9 us -> none  [on_device(): coeff = coefficients(lax.all_gather(codes, 'col', axis=0))]
    ppermute x10, waiting for transfers between devices: 64.8 us -> 126 us  [line_gather(): came[links, step] = lax.ppermute(came[1 - links, step - 1], axis, pairs)]
    ppermute x9, waiting for transfers between devices: 13.9 us -> 34 us  [doubling_gather(): came = lax.ppermute(part, axis, [(i, i ^ bit) for i in range(n)])]
    ppermute x9, waiting for transfers between devices: 26.6 us -> 7.48 us  [halving_sum(): came = lax.ppermute(sent, axis, [(i, i ^ bit) for i in range(n)])]
    ppermute x0 -> x3, waiting for transfers between devices: none -> 19.1 us  [on_device(): lax.ppermute(codes, 'col', [(i, (i + shift) % n) for i in range(n)])]
    psum x1, waiting for transfers between devices: 59.1 us -> 40.5 us  [on_device(): lax.psum([(pre_of(slot), against(dys[slot], w_out16)) for slot in early],...]
    select_n x9, other arithmetic: 1.21 us -> 13 us  [doubling_gather(): jnp.where(here // bit % 2 == 1, jnp.concatenate([came, part], axis=-2), j...]
    pallas_call x2 -> x4, Pallas kernels: 38.9 us -> 49.8 us  [update(): pl.pallas_call(update_kernel, grid=(height // block,), in_specs=[pl.Block...]
  transfers between devices with their start and end apart: 29 -> 32, of which waited for: 14 -> 15; matrix products, arithmetic and copies ran while one was open for 12% -> 13% of each run, Pallas kernels for 9% -> 11%
where the time goes in v3:
time: 420 us; the launch traced here: 419 us
  waiting for transfers between devices  227 us (54%)
  Pallas kernels  66.6 us (16%)
  starting transfers between devices  39.6 us (9%)
  other arithmetic  35.3 us (8%)
  local copies, waits for them, and re-layouts  17.7 us (4%)
  between operations  16.6 us (4%)
  matrix products  16.5 us (4%)
    ppermute x10, waiting for transfers between devices, line_gather(): came[links, step] = lax.ppermute(came[1 - links, step - 1], axis, pairs)  126 us
    pallas_call x4, Pallas kernels, update(): pl.pallas_call(update_kernel, grid=(height // block,), in_specs=[pl.Block...  49.8 us
    psum x1, waiting for transfers between devices, on_device(): lax.psum([(pre_of(slot), against(dys[slot], w_out16)) for slot in early],...  40.5 us
    ppermute x9, waiting for transfers between devices, doubling_gather(): came = lax.ppermute(part, axis, [(i, i ^ bit) for i in range(n)])  34 us
    ppermute x10, starting transfers between devices, line_gather(): came[links, step] = lax.ppermute(came[1 - links, step - 1], axis, pairs)  20.3 us
    ppermute x3, waiting for transfers between devices, on_device(): lax.ppermute(codes, 'col', [(i, (i + shift) % n) for i in range(n)])  19.1 us
    pallas_call x2, Pallas kernels, grad_sum(): pl.pallas_call(functools.partial(grad_kernel, parts), grid=(height // blo...  16.8 us
    select_n x9, other arithmetic, doubling_gather(): jnp.where(here // bit % 2 == 1, jnp.concatenate([came, part], axis=-2), j...  13 us
  transfers between devices with their start and end apart: 32, of which 15 were waited for; matrix products, arithmetic and copies ran while one was open for 13% of the time, Pallas kernels for 11%

profile of v3, /device:TPU:0, one launch (start us, length us, event | category | flops | bytes accessed | tf_op | source)
XLA Modules:
  0.0 419.5 jit_solution(6681156867763127284)
XLA Ops:
  9.1 4.7 %collective-permute-start = (bf16[384,2304]{1,0:T(8,128)(2,1)}, bf16[384,2304]{1,0:T(8,128)(2,1)S(1)}, u32[]{:S(2)}, u32[]{:S(2)}) collective-permute-start(bf16[384,2304]{1,0:T(8,128)(2,1)} %refs_0_.1), channel_id=1, source_target_pairs={{0,1},{1,0},{2,3},{3,2},{4,5},{5,4},{6,7},{7,6},{8,9},{9,8},{10,11... | collective-permute-start | bytes 5308424 | tf_op jit(solution)/shard_map/ppermute | solution.py:148
  16.6 2.8 collective-permute-start.5
  21.3 3.5 convert_element_type.81
  34.4 18.0 %collective-permute-done.4 = f32[2,384]{1,0:T(2,128)S(1)} collective-permute-done((f32[2,384]{1,0:T(2,128)S(1)}, f32[2,384]{1,0:T(2,128)S(1)}, u32[]{:S(2)}, u32[]{:S(2)}) %collective-permute-start.4) | collective-permute-done | bytes 3104 | tf_op jit(solution)/shard_map/ppermute | solution.py:247
  65.0 2.6 fusion.20
  69.4 66.1 %collective-permute-done.7 = bf16[384,2304]{1,0:T(8,128)(2,1)} collective-permute-done((bf16[384,2304]{1,0:T(8,128)(2,1)}, bf16[384,2304]{1,0:T(8,128)(2,1)}, u32[]{:S(2)}, u32[]{:S(2)}) %collective-permute-start.7) | collective-permute-done | bytes 1769504 | tf_op jit(solution)/shard_map/ppermute | solution.py:148
  138.7 34.6 %collective-permute-done.10 = bf16[384,2304]{1,0:T(8,128)(2,1)S(1)} collective-permute-done((bf16[384,2304]{1,0:T(8,128)(2,1)}, bf16[384,2304]{1,0:T(8,128)(2,1)S(1)}, u32[]{:S(2)}, u32[]{:S(2)}) %collective-permute-start.10) | collective-permute-done | bytes 1769504 | tf_op jit(solution)/shard_map/ppermute | solution.py:148
  177.0 2.6 convolution_bitcast_fusion
  183.2 25.3 %collective-permute-done.2 = bf16[384,2304]{1,0:T(8,128)(2,1)S(1)} collective-permute-done((bf16[384,2304]{1,0:T(8,128)(2,1)}, bf16[384,2304]{1,0:T(8,128)(2,1)S(1)}, u32[]{:S(2)}, u32[]{:S(2)}) %collective-permute-start.2) | collective-permute-done | bytes 1769504 | tf_op jit(solution)/shard_map/ppermute | solution.py:148
  214.4 2.6 fusion.21
  218.9 3.7 collective-permute-done.13
  230.4 8.4 %collective-permute-done.14 = bf16[2,48,768]{2,1,0:T(8,128)(2,1)} collective-permute-done((bf16[2,48,768]{2,1,0:T(8,128)(2,1)}, bf16[2,48,768]{2,1,0:T(8,128)(2,1)}, u32[]{:S(2)}, u32[]{:S(2)}) %collective-permute-start.14) | collective-permute-done | bytes 147488 | tf_op jit(solution)/shard_map/ppermute | solution.py:198
  246.9 8.6 %collective-permute-done.15 = bf16[2,96,768]{2,1,0:T(8,128)(2,1)} collective-permute-done((bf16[2,96,768]{2,1,0:T(8,128)(2,1)}, bf16[2,96,768]{2,1,0:T(8,128)(2,1)}, u32[]{:S(2)}, u32[]{:S(2)}) %collective-permute-start.15) | collective-permute-done | bytes 294944 | tf_op jit(solution)/shard_map/ppermute | solution.py:198
  260.3 3.2 collective-permute-done.20
  266.0 7.7 %collective-permute-done.21 = bf16[96,768]{1,0:T(8,128)(2,1)} collective-permute-done((bf16[96,768]{1,0:T(8,128)(2,1)}, bf16[96,768]{1,0:T(8,128)(2,1)}, u32[]{:S(2)}, u32[]{:S(2)}) %collective-permute-start.21) | collective-permute-done | bytes 147488 | tf_op jit(solution)/shard_map/ppermute | solution.py:198
  275.6 3.0 maximum_select_fusion
  278.6 40.5 %all-reduce.3.cloned.1.call-done = (f32[384,768]{1,0:T(8,128)}, f32[384,768]{1,0:T(8,128)}, f32[384,768]{1,0:T(8,128)}, f32[384,768]{1,0:T(8,128)}) async-done(((f32[384,768]{1,0:T(8,128)}, f32[384,768]{1,0:T(8,128)}, f32[384,768]{1,0:T(8,128)}, f32[384,768]{1,0:T(8,128)}), (f32[384,768]{1,0:T(8,128)}, f32[384,768]{1,0:T(8,128)}, f32[384,768]{1,0:T(8,128)}, ...) | async-done | bytes 4718608 | tf_op jit(solution)/shard_map/psum | solution.py:277
  324.7 8.1 %shard_map.191.grad = f32[768,2304]{1,0:T(8,128)} custom-call(bf16[384,768]{1,0:T(8,128)(2,1)S(1)} %get-tuple-element.70.refs_0_, bf16[384,768]{1,0:T(8,128)(2,1)S(1)} %get-tuple-element.68.refs_1_, bf16[384,768]{1,0:T(8,128)(2,1)S(1)} %get-tuple-element.66.refs_2_, bf16[384,2304]{1,0:T(8,128)(2,1)S(1)} %multiply_convert_fusion.3.refs_3_, ...), custom_call_target="tpu_custom_call" | custom-call | flops 4076863488 | bytes 14155776 | tf_op jit(solution)/shard_map/pallas_call | solution.py:69
  332.8 8.7 %shard_map.190.grad = f32[2304,768]{1,0:T(8,128)} custom-call(bf16[384,2304]{1,0:T(8,128)(2,1)S(1)} %copy-done.5, bf16[384,2304]{1,0:T(8,128)(2,1)S(1)} %copy-done.8, bf16[384,2304]{1,0:T(8,128)(2,1)S(1)} %broadcast_select_fusion.refs_2_, bf16[384,768]{1,0:T(8,128)(2,1)S(1)} %get-tuple-element.71.refs_3_, bf16[384,768]{1,0:T(8,128)(2,1)S(1)} %get-tuple-element.69.refs_4_, ...), custom_call_target="tpu_custom_call" | custom-call | flops 4076863488 | bytes 14155776 | tf_op jit(solution)/shard_map/pallas_call | solution.py:69
  351.7 9.1 %shard_map.192 = (f32[768,2304]{1,0:T(8,128)}, f32[768,2304]{1,0:T(8,128)}, f32[768,2304]{1,0:T(8,128)}) custom-call(bf16[384,768]{1,0:T(8,128)(2,1)} %maximum_select_fusion.2.left, bf16[384,2304]{1,0:T(8,128)(2,1)} %copy-done.10, f32[768,2304]{1,0:T(8,128)} %shard_map.191.grad, f32[768,2304]{1,0:T(8,128)} %w.6, f32[768,2304]{1,0:T(8,128)} %m.6, f32[768,2304]{1,0:T(8,128)} %v.6), custom_call_target="tpu_custom_call" | custom-call | flops 452984832 | bytes 17694720 | tf_op jit(solution)/shard_map/pallas_call | solution.py:97
  361.6 9.1 %shard_map.193 = (f32[768,2304]{1,0:T(8,128)}, f32[768,2304]{1,0:T(8,128)}, f32[768,2304]{1,0:T(8,128)}) custom-call(bf16[384,768]{1,0:T(8,128)(2,1)} %maximum_select_fusion.2.left, bf16[384,2304]{1,0:T(8,128)(2,1)} %copy-done.10, f32[768,2304]{1,0:T(8,128)} %shard_map.191.grad, ...), custom_call_target="tpu_custom_call", output_to_operand_aliasing={{0}: (6, {}), {1}: (7, {}), {2}: (8, {})} | custom-call | flops 452984832 | bytes 17694720 | tf_op jit(solution)/shard_map/pallas_call | solution.py:97
  373.1 9.1 %shard_map.194 = (f32[768,2304]{1,0:T(8,128)}, f32[768,2304]{1,0:T(8,128)}, f32[768,2304]{1,0:T(8,128)}) custom-call(bf16[384,768]{1,0:T(8,128)(2,1)} %maximum_select_fusion.2.left, bf16[384,2304]{1,0:T(8,128)(2,1)} %copy-done.10, f32[768,2304]{1,0:T(8,128)} %shard_map.191.grad, ...), custom_call_target="tpu_custom_call", output_to_operand_aliasing={{0}: (6, {}), {1}: (7, {}), {2}: (8, {})} | custom-call | flops 452984832 | bytes 17694720 | tf_op jit(solution)/shard_map/pallas_call | solution.py:97
  382.9 4.6 %collective-permute-done.29 = bf16[96,768]{1,0:T(8,128)(2,1)S(1)} collective-permute-done((bf16[96,768]{1,0:T(8,128)(2,1)S(1)}, bf16[96,768]{1,0:T(8,128)(2,1)S(1)}, u32[]{:S(2)}, u32[]{:S(2)}) %collective-permute-start.29) | collective-permute-done | bytes 147488 | tf_op jit(solution)/shard_map/ppermute | solution.py:198
  390.2 22.4 %shard_map.195 = (f32[2304,768]{1,0:T(8,128)}, f32[2304,768]{1,0:T(8,128)}, f32[2304,768]{1,0:T(8,128)}) custom-call(bf16[384,2304]{1,0:T(8,128)(2,1)} %copy-done.11, bf16[384,768]{1,0:T(8,128)(2,1)} %maximum_select_fusion.3.right, f32[2304,768]{1,0:T(8,128)} %shard_map.190.grad, f32[2304,768]{1,0:T(8,128)} %w.7, f32[2304,768]{1,0:T(8,128)} %m.7, f32[2304,768]{1,0:T(8,128)} %v.7), custom_call_target="tpu_custom_call" | custom-call | flops 1358954496 | bytes 51904512 | tf_op jit(solution)/shard_map/pallas_call | solution.py:97
  (178 shorter events, 93.8 us)
Async XLA Ops:
  7.2 312.0 %all-reduce.3.cloned.1.call-start = ((), (), s32[]{:S(2)}) async-start(), calls=%async_computation | async-start | bytes 9437184 | tf_op jit(solution)/shard_map/psum | solution.py:277
  7.2 50.9 %collective-permute-start.6 = (bf16[384,2304]{1,0:T(8,128)(2,1)}, bf16[384,2304]{1,0:T(8,128)(2,1)}, u32[]{:S(2)}, u32[]{:S(2)}) collective-permute-start(bf16[384,2304]{1,0:T(8,128)(2,1)} %refs_0_.1), channel_id=1, source_target_pairs={{1,2},{2,1},{5,6},{6,5},{9,10},{10,9},{13,14},{14,13},{17,18},{18,... | collective-permute-start | bytes 5308424 | tf_op jit(solution)/shard_map/ppermute | solution.py:148
  9.1 50.4 %collective-permute-start = (bf16[384,2304]{1,0:T(8,128)(2,1)}, bf16[384,2304]{1,0:T(8,128)(2,1)S(1)}, u32[]{:S(2)}, u32[]{:S(2)}) collective-permute-start(bf16[384,2304]{1,0:T(8,128)(2,1)} %refs_0_.1), channel_id=1, source_target_pairs={{0,1},{1,0},{2,3},{3,2},{4,5},{5,4},{6,7},{7,6},{8,9},{9,8},{10,11... | collective-permute-start | bytes 5308424 | tf_op jit(solution)/shard_map/ppermute | solution.py:148
  14.6 37.8 %collective-permute-start.4 = (f32[2,384]{1,0:T(2,128)S(1)}, f32[2,384]{1,0:T(2,128)S(1)}, u32[]{:S(2)}, u32[]{:S(2)}) collective-permute-start(f32[2,384]{1,0:T(2,128)S(1)} %get-tuple-element.77), channel_id=1, source_target_pairs={{0,2},{1,3},{2,0},{3,1},{4,6},{5,7},{6,4},{7,5},{8,10},{9,11},{10,... | collective-permute-start | bytes 9224 | tf_op jit(solution)/shard_map/ppermute | solution.py:247
  15.6 38.0 %collective-permute-start.3 = (f32[2,384]{1,0:T(2,128)S(1)}, f32[2,384]{1,0:T(2,128)S(1)}, u32[]{:S(2)}, u32[]{:S(2)}) collective-permute-start(f32[2,384]{1,0:T(2,128)S(1)} %get-tuple-element.77), channel_id=1, source_target_pairs={{0,1},{1,2},{2,3},{3,0},{4,5},{5,6},{6,7},{7,4},{8,9},{9,10},{10,1... | collective-permute-start | bytes 9224 | tf_op jit(solution)/shard_map/ppermute | solution.py:247
  16.6 37.0 %collective-permute-start.5 = (f32[2,384]{1,0:T(2,128)S(1)}, f32[2,384]{1,0:T(2,128)S(1)}, u32[]{:S(2)}, u32[]{:S(2)}) collective-permute-start(f32[2,384]{1,0:T(2,128)S(1)} %get-tuple-element.77), channel_id=1, source_target_pairs={{0,3},{1,0},{2,1},{3,2},{4,7},{5,4},{6,5},{7,6},{8,11},{9,8},{10,9... | collective-permute-start | bytes 9224 | tf_op jit(solution)/shard_map/ppermute | solution.py:247
  53.6 10.1 %collective-permute-start.9 = (bf16[384,2304]{1,0:T(8,128)(2,1)}, bf16[384,2304]{1,0:T(8,128)(2,1)}, u32[]{:S(2)}, u32[]{:S(2)}) collective-permute-start(bf16[384,2304]{1,0:T(8,128)(2,1)} %param.16), channel_id=1, source_target_pairs={{1,2},{2,1},{5,6},{6,5},{9,10},{10,9},{13,14},{14,13},{17,18},{18,... | collective-permute-start | bytes 5308424 | tf_op jit(solution)/shard_map/ppermute | solution.py:148
  55.5 124.1 %collective-permute-start.8 = (bf16[384,2304]{1,0:T(8,128)(2,1)}, bf16[384,2304]{1,0:T(8,128)(2,1)}, u32[]{:S(2)}, u32[]{:S(2)}) collective-permute-start(bf16[384,2304]{1,0:T(8,128)(2,1)} %param.16), channel_id=1, source_target_pairs={{0,1},{1,0},{2,3},{3,2},{4,5},{5,4},{6,7},{7,6},{8,9},{9,8},{10,11... | collective-permute-start | bytes 5308424 | tf_op jit(solution)/shard_map/ppermute | solution.py:148
  58.1 77.3 %collective-permute-start.7 = (bf16[384,2304]{1,0:T(8,128)(2,1)}, bf16[384,2304]{1,0:T(8,128)(2,1)}, u32[]{:S(2)}, u32[]{:S(2)}) collective-permute-start(bf16[384,2304]{1,0:T(8,128)(2,1)} %collective-permute-done.6), channel_id=1, source_target_pairs={{1,0},{2,3},{5,4},{6,7},{9,8},{10,11},{13,12},{14,15},{17,16},{18,... | collective-permute-start | bytes 5308424 | tf_op jit(solution)/shard_map/ppermute | solution.py:148
  63.7 109.6 %collective-permute-start.10 = (bf16[384,2304]{1,0:T(8,128)(2,1)}, bf16[384,2304]{1,0:T(8,128)(2,1)S(1)}, u32[]{:S(2)}, u32[]{:S(2)}) collective-permute-start(bf16[384,2304]{1,0:T(8,128)(2,1)} %collective-permute-done.9), channel_id=1, source_target_pairs={{1,0},{2,3},{5,4},{6,7},{9,8},{10,11},{13,12},{14,15},{17,16},{18,... | collective-permute-start | bytes 5308424 | tf_op jit(solution)/shard_map/ppermute | solution.py:148
  67.6 140.9 %collective-permute-start.2 = (bf16[384,2304]{1,0:T(8,128)(2,1)}, bf16[384,2304]{1,0:T(8,128)(2,1)S(1)}, u32[]{:S(2)}, u32[]{:S(2)}) collective-permute-start(bf16[384,2304]{1,0:T(8,128)(2,1)} %collective-permute-done.1), channel_id=1, source_target_pairs={{1,0},{2,3},{5,4},{6,7},{9,8},{10,11},{13,12},{14,15},{17,16},{18,... | collective-permute-start | bytes 5308424 | tf_op jit(solution)/shard_map/ppermute | solution.py:148
  181.6 29.6 %collective-permute-start.12 = (f32[2,96,768]{2,1,0:T(8,128)S(1)}, f32[2,96,768]{2,1,0:T(8,128)S(1)}, u32[]{:S(2)}, u32[]{:S(2)}) collective-permute-start(f32[2,96,768]{2,1,0:T(8,128)S(1)} %constant_dynamic-slice_fusion.7), channel_id=1, source_target_pairs={{0,8},{4,12},{8,0},{12,4},{16,24},{20,28},{24,16},{28,20},{1,9},{5... | collective-permute-start | bytes 1769480 | tf_op jit(solution)/shard_map/ppermute | solution.py:185
  211.2 12.6 %collective-permute-start.17 = (f32[192,768]{1,0:T(8,128)}, f32[192,768]{1,0:T(8,128)}, u32[]{:S(2)}, u32[]{:S(2)}) collective-permute-start(f32[192,768]{1,0:T(8,128)} %constant_dynamic-slice_fusion.5), channel_id=1, source_target_pairs={{0,4},{4,0},{8,12},{12,8},{16,20},{20,16},{24,28},{28,24},{1,5},{5... | collective-permute-start | bytes 1769480 | tf_op jit(solution)/shard_map/ppermute | solution.py:185
  217.0 47.5 %collective-permute-start.23 = (bf16[384,2304]{1,0:T(8,128)(2,1)}, bf16[384,2304]{1,0:T(8,128)(2,1)}, u32[]{:S(2)}, u32[]{:S(2)}) collective-permute-start(bf16[384,2304]{1,0:T(8,128)(2,1)} %collective-permute-done.8), channel_id=1, source_target_pairs={{1,2},{2,1},{5,6},{6,5},{9,10},{10,9},{13,14},{14,13},{17,18},{18,... | collective-permute-start | bytes 5308424 | tf_op jit(solution)/shard_map/ppermute | solution.py:148
  226.7 16.2 %collective-permute-start.18 = (f32[96,768]{1,0:T(8,128)}, f32[96,768]{1,0:T(8,128)}, u32[]{:S(2)}, u32[]{:S(2)}) collective-permute-start(f32[96,768]{1,0:T(8,128)} %constant_dynamic-slice_fusion.4), channel_id=1, source_target_pairs={{0,8},{4,12},{8,0},{12,4},{16,24},{20,28},{24,16},{28,20},{1,9},{5... | collective-permute-start | bytes 884744 | tf_op jit(solution)/shard_map/ppermute | solution.py:185
  228.9 9.9 %collective-permute-start.14 = (bf16[2,48,768]{2,1,0:T(8,128)(2,1)}, bf16[2,48,768]{2,1,0:T(8,128)(2,1)}, u32[]{:S(2)}, u32[]{:S(2)}) collective-permute-start(bf16[2,48,768]{2,1,0:T(8,128)(2,1)} %pad_maximum_fusion), channel_id=1, source_target_pairs={{0,16},{4,20},{8,24},{12,28},{16,0},{20,4},{24,8},{28,12},{1,17},{... | collective-permute-start | bytes 442376 | tf_op jit(solution)/shard_map/ppermute | solution.py:198
  240.7 14.8 %collective-permute-start.15 = (bf16[2,96,768]{2,1,0:T(8,128)(2,1)}, bf16[2,96,768]{2,1,0:T(8,128)(2,1)}, u32[]{:S(2)}, u32[]{:S(2)}) collective-permute-start(bf16[2,96,768]{2,1,0:T(8,128)(2,1)} %maximum_select_fusion.4), channel_id=1, source_target_pairs={{0,8},{4,12},{8,0},{12,4},{16,24},{20,28},{24,16},{28,20},{1,9},{5... | collective-permute-start | bytes 884744 | tf_op jit(solution)/shard_map/ppermute | solution.py:198
  245.4 12.4 %collective-permute-start.19 = (f32[48,768]{1,0:T(8,128)}, f32[48,768]{1,0:T(8,128)}, u32[]{:S(2)}, u32[]{:S(2)}) collective-permute-start(f32[48,768]{1,0:T(8,128)} %constant_dynamic-slice_fusion.3), channel_id=1, source_target_pairs={{0,16},{4,20},{8,24},{12,28},{16,0},{20,4},{24,8},{28,12},{1,17},{... | collective-permute-start | bytes 442376 | tf_op jit(solution)/shard_map/ppermute | solution.py:185
  257.7 17.9 %collective-permute-start.16 = (bf16[2,192,768]{2,1,0:T(8,128)(2,1)}, bf16[2,192,768]{2,1,0:T(8,128)(2,1)}, u32[]{:S(2)}, u32[]{:S(2)}) collective-permute-start(bf16[2,192,768]{2,1,0:T(8,128)(2,1)} %maximum_select_fusion.1), channel_id=1, source_target_pairs={{0,4},{4,0},{8,12},{12,8},{16,20},{20,16},{24,28},{28,24},{1,5},{5... | collective-permute-start | bytes 1769480 | tf_op jit(solution)/shard_map/ppermute | solution.py:198
  264.5 79.3 %collective-permute-start.24 = (bf16[384,2304]{1,0:T(8,128)(2,1)}, bf16[384,2304]{1,0:T(8,128)(2,1)}, u32[]{:S(2)}, u32[]{:S(2)}) collective-permute-start(bf16[384,2304]{1,0:T(8,128)(2,1)} %collective-permute-done.23), channel_id=1, source_target_pairs={{1,0},{2,3},{5,4},{6,7},{9,8},{10,11},{13,12},{14,15},{17,16},{18,... | collective-permute-start | bytes 5308424 | tf_op jit(solution)/shard_map/ppermute | solution.py:148
  275.6 66.0 %collective-permute-start.22 = (bf16[192,768]{1,0:T(8,128)(2,1)}, bf16[192,768]{1,0:T(8,128)(2,1)}, u32[]{:S(2)}, u32[]{:S(2)}) collective-permute-start(bf16[192,768]{1,0:T(8,128)(2,1)} %maximum_select_fusion.5), channel_id=1, source_target_pairs={{0,4},{4,0},{8,12},{12,8},{16,20},{20,16},{24,28},{28,24},{1,5},{5... | collective-permute-start | bytes 884744 | tf_op jit(solution)/shard_map/ppermute | solution.py:198
  350.1 10.7 %collective-permute-start.26 = (f32[96,768]{1,0:T(8,128)S(1)}, f32[96,768]{1,0:T(8,128)S(1)}, u32[]{:S(2)}, u32[]{:S(2)}) collective-permute-start(f32[96,768]{1,0:T(8,128)S(1)} %constant_dynamic-slice_fusion.1), channel_id=1, source_target_pairs={{0,8},{4,12},{8,0},{12,4},{16,24},{20,28},{24,16},{28,20},{1,9},{5... | collective-permute-start | bytes 884744 | tf_op jit(solution)/shard_map/ppermute | solution.py:185
  360.9 9.8 %collective-permute-start.27 = (f32[48,768]{1,0:T(8,128)S(1)}, f32[48,768]{1,0:T(8,128)S(1)}, u32[]{:S(2)}, u32[]{:S(2)}) collective-permute-start(f32[48,768]{1,0:T(8,128)S(1)} %constant_dynamic-slice_fusion), channel_id=1, source_target_pairs={{0,16},{4,20},{8,24},{12,28},{16,0},{20,4},{24,8},{28,12},{1,17},{... | collective-permute-start | bytes 442376 | tf_op jit(solution)/shard_map/ppermute | solution.py:185
  371.6 10.6 %collective-permute-start.28 = (bf16[48,768]{1,0:T(8,128)(2,1)S(1)}, bf16[48,768]{1,0:T(8,128)(2,1)S(1)}, u32[]{:S(2)}, u32[]{:S(2)}) collective-permute-start(bf16[48,768]{1,0:T(8,128)(2,1)S(1)} %multiply_convert_fusion.8), channel_id=1, source_target_pairs={{0,16},{4,20},{8,24},{12,28},{16,0},{20,4},{24,8},{28,12},{1,17},{... | collective-permute-start | bytes 221192 | tf_op jit(solution)/shard_map/ppermute | solution.py:198
  (37 other events, 233.6 us)
Sparse Core Ops, SparseCore 0:
  217.2 101.9 all-reduce.2

commit v4 on v3

--- a/solution.py
+++ b/solution.py
@@ -82,40 +82,50 @@
     )(*lefts, *rights)
 
 
-def update_kernel(left, right, grad, w, m, v, *refs):
-    new_w, new_m, new_v = refs[-3:]
-    total = grad[...] + over_rows(left[...], right[...])
-    new_w[...], new_m[...], new_v[...] = adamw(w[...], m[...], v[...], total)
-
-
-def update(left, right, grad, w, m, v, rows_most, part=0, parts=1, so_far=()):
-    rows, height = left.shape
-    width = right.shape[1] // parts
-    block = block_of(height, rows_most)
+def update_kernel(shards, *refs):
+    lefts, rights = refs[:shards], refs[shards : 2 * shards]
+    grad, w, m, v = refs[2 * shards : 2 * shards + 4]
+    new_w, new_m, new_v, total = refs[-4:]
+    summed = grad[...]
+    for left, right in zip(lefts, rights):
+        summed += over_rows(left[...], right[...])
+    total[...] = summed
+
+    def eight_rows(i, carry):
+        rows = pl.ds(pl.multiple_of(8 * i, 8), 8)
+        new_w[rows, :], new_m[rows, :], new_v[rows, :] = adamw(
+            w[rows, :], m[rows, :], v[rows, :], total[rows, :]
+        )
+        return carry
+
+    lax.fori_loop(0, total.shape[0] // 8, eight_rows, 0, unroll=2)
+
+
+def update(lefts, rights, grad, w, m, v, most, part=0, parts=1, so_far=()):
+    shards = len(lefts)
+    rows, height = lefts[0].shape
+    width = rights[0].shape[1] // parts
+    block = block_of(height, most)
     panel = pl.BlockSpec((block, width), lambda i: (i, part))
     shape = jax.ShapeDtypeStruct(w.shape, jnp.float32)
     return pl.pallas_call(
-        update_kernel,
+        functools.partial(update_kernel, shards),
         grid=(height // block,),
-        in_specs=[
-            pl.BlockSpec((rows, block), lambda i: (0, i)),
-            pl.BlockSpec((rows, width), lambda i: (0, part)),
-            panel,
-            panel,
-            panel,
-            panel,
-        ]
+        in_specs=[pl.BlockSpec((rows, block), lambda i: (0, i))] * shards
+        + [pl.BlockSpec((rows, width), lambda i: (0, part))] * shards
+        + [panel] * 4
         + [pl.BlockSpec(memory_space=pl.ANY)] * len(so_far),
         out_specs=[panel] * 3,
         out_shape=[shape] * 3,
-        input_output_aliases={6 + i: i for i in range(len(so_far))},
+        scratch_shapes=[pltpu.VMEM((block, width), jnp.float32)],
+        input_output_aliases={2 * shards + 4 + i: i for i in range(len(so_far))},
         compiler_params=pltpu.CompilerParams(vmem_limit_bytes=56 * 2**20),
         cost_estimate=pl.CostEstimate(
-            flops=2 * rows * height * width,
-            bytes_accessed=7 * 4 * height * width + 2 * rows * (height + width),
+            flops=2 * shards * rows * height * width,
+            bytes_accessed=7 * 4 * height * width + 2 * shards * rows * (height + width),
             transcendentals=2 * height * width,
         ),
-    )(left, right, grad, w, m, v, *so_far)
+    )(*lefts, *rights, grad, w, m, v, *so_far)
 
 
 def link_pairs(n, first, step):
@@ -142,10 +152,12 @@
     here = lax.axis_index(axis)
     came = {(0, 0): shard, (1, 0): shard}
     for step in range(1, n):
+        arrived = {}
         for links in (0, 1):
             pairs = link_pairs(n, links, step)
             if pairs:
-                came[links, step] = lax.ppermute(came[1 - links, step - 1], axis, pairs)
+                arrived[links, step] = lax.ppermute(came[1 - links, step - 1], axis, pairs)
+        came.update(lax.optimization_barrier(arrived))
     slots, owners = [shard], [here]
     tables = [arrivals(n, c) for c in range(n)]
     for slot in range(n - 1):
@@ -167,43 +179,55 @@
     return slots, owners
 
 
-def together(came, beside):
-    if beside:
-        came, _ = lax.optimization_barrier((came, beside.pop(0)()))
-    return came
-
-
-def halving_sum(part, axis, beside=None):
-    n = lax.axis_size(axis)
+def after(value, earlier):
+    if earlier is not None:
+        value, _ = lax.optimization_barrier((value, earlier))
+    return value
+
+
+def exchange(part, axis, mask, beside=None):
+    came = lax.ppermute(part, axis, [(i, i ^ mask) for i in range(lax.axis_size(axis))])
+    work = beside.pop(0) if beside else None
+    return after(came, work() if callable(work) else work)
+
+
+def row_sum(part, axis, beside=None):
     here = lax.axis_index(axis)
+    others = lax.axis_size(axis) // 2
+    half = part.shape[0] // 2
+    odd, place = here % 2, here // 2
+    kept = lax.dynamic_slice_in_dim(part, odd * half, half)
+    sent = lax.dynamic_slice_in_dim(part, (1 - odd) * half, half)
+    part = kept + exchange(sent, axis, 1, beside)
+    piece = half // others
+    total = lax.dynamic_slice_in_dim(part, place * piece, piece)
+    came = [
+        exchange(lax.dynamic_slice_in_dim(part, (place ^ other) * piece, piece), axis, 2 * other)
+        for other in range(1, others)
+    ]
+    work = beside.pop(0) if beside else None
+    came = after(came, work() if callable(work) else work)
+    return functools.reduce(jnp.add, came, total)
+
+
+def row_gather(part, axis, beside=None):
+    here = lax.axis_index(axis)
+    others = lax.axis_size(axis) // 2
+    odd, place = here % 2, here // 2
+    pieces = [part] + [exchange(part, axis, 2 * other) for other in range(1, others)]
+    work = beside.pop(0) if beside else None
+    pieces = after(pieces, work() if callable(work) else work)
     bit = 1
-    while bit < n:
-        half = part.shape[-2] // 2
-        high = (here // bit) % 2
-        kept = lax.dynamic_slice_in_dim(part, high * half, half, axis=-2)
-        sent = lax.dynamic_slice_in_dim(part, (1 - high) * half, half, axis=-2)
-        came = lax.ppermute(sent, axis, [(i, i ^ bit) for i in range(n)])
-        if bit > 1:
-            came = together(came, beside)
-        part = kept + came
+    while bit < others:
+        pieces = [
+            jnp.where((place // bit) % 2 == 1, pieces[i ^ bit], pieces[i]) for i in range(others)
+        ]
         bit *= 2
-    return part
-
-
-def doubling_gather(part, axis, beside=None):
-    n = lax.axis_size(axis)
-    here = lax.axis_index(axis)
-    bit = n // 2
-    while bit:
-        came = lax.ppermute(part, axis, [(i, i ^ bit) for i in range(n)])
-        came = together(came, beside)
-        part = jnp.where(
-            (here // bit) % 2 == 1,
-            jnp.concatenate([came, part], axis=-2),
-            jnp.concatenate([part, came], axis=-2),
-        )
-        bit //= 2
-    return part
+    part = jnp.concatenate(pieces)
+    came = exchange(part, axis, 1, beside)
+    return jnp.where(
+        odd == 1, jnp.concatenate([came, part]), jnp.concatenate([part, came])
+    )
 
 
 def response_codes(logratio, token_session, token_position, pad_mask):
@@ -239,7 +263,6 @@
 ):
     n = lax.axis_size("col")
     here = lax.axis_index("col")
-    token_slots, owners = line_gather(tokens, "col")
     codes = response_codes(logratio, token_session, token_position, pad_mask)
     codes = jnp.stack(
         [codes]
@@ -249,21 +272,18 @@
         ]
     )
     out_grad, codes = lax.optimization_barrier((out_grad, codes))
-    out_grad_slots, _ = line_gather(out_grad, "col")
     coeff = coefficients(codes)
     w_in16, w_out16 = lax.optimization_barrier(
         (w_in.astype(jnp.bfloat16), w_out.astype(jnp.bfloat16))
     )
 
-    def scaled(slot, after=None):
-        shift = (here - owners[slot] + n) % n
-        mine = lax.dynamic_index_in_dim(coeff, shift, 0, keepdims=False)
-        if after is not None:
-            mine, _ = lax.optimization_barrier((mine, after))
-        return (mine[:, None] * out_grad_slots[slot].astype(jnp.float32)).astype(jnp.bfloat16)
-
-    def pre_of(slot):
-        return jnp.dot(token_slots[slot], w_in16, preferred_element_type=jnp.float32)
+    def scaled(shard, owner, earlier=None):
+        mine = lax.dynamic_index_in_dim(coeff, (here - owner + n) % n, 0, keepdims=False)
+        mine = after(mine, earlier)
+        return (mine[:, None] * shard.astype(jnp.float32)).astype(jnp.bfloat16)
+
+    def pre_of(shard):
+        return jnp.dot(shard, w_in16, preferred_element_type=jnp.float32)
 
     def square(pre):
         positive = jnp.maximum(pre, 0.0)
@@ -272,20 +292,8 @@
     def chain(pre, back):
         return (back * 2.0 * jnp.maximum(pre, 0.0)).astype(jnp.bfloat16)
 
-    early = range(n - 2)
-    dys = [scaled(slot) for slot in range(n - 1)]
-    sums = lax.psum([(pre_of(slot), against(dys[slot], w_out16)) for slot in early], "row")
-    both = halving_sum(jnp.stack([pre_of(n - 2), against(dys[n - 2], w_out16)]), "row")
-    both = doubling_gather(jnp.stack([square(both[0]), chain(both[0], both[1])]), "row")
-    sums, both = lax.optimization_barrier((sums, both))
-    acts = [square(pre) for pre, _ in sums] + [both[0]]
-    dpres = [chain(pre, back) for pre, back in sums] + [both[1]]
-    grad_in = grad_sum(token_slots[:-1], dpres, 256)
-    grad_out = grad_sum(acts, dys, 128)
-
-    pre = halving_sum(pre_of(n - 1), "row")
-    act = doubling_gather(square(pre), "row")
-    dy = scaled(n - 1, (grad_in, grad_out, act))
+    token_slots, owners = line_gather(tokens, "col")
+    out_grad_slots, _ = line_gather(out_grad, "col")
     parts = 3
     outs_out = ()
 
@@ -293,18 +301,37 @@
         def run():
             nonlocal outs_out
             outs_out = update(
-                act, dy, grad_out, w_out, m_out, v_out, 256, part, parts, outs_out
+                acts[-2:], dys[-2:], grad_out, w_out, m_out, v_out, 128, part, parts, outs_out
             )
             return outs_out
 
         return run
 
-    beside = [update_part(part) for part in range(parts)]
-    back = halving_sum(against(dy, w_out16), "row", beside)
-    dpre = doubling_gather(chain(pre, back), "row", beside)
-    while beside:
-        beside.pop(0)()
-    outs_in = update(token_slots[-1], dpre, grad_in, w_in, m_in, v_in, 256)
+    waits = [x for pair in zip(token_slots[1:], out_grad_slots[1:]) for x in pair][:-1]
+    acts, dpres, dys = [], [], []
+    last = None
+    for slot in range(n):
+        pre = row_sum(after(pre_of(token_slots[slot]), last), "row")
+        latest = [out_grad_slots[n - 1]] if slot == n - 1 else None
+        acts.append(row_gather(square(pre), "row", latest))
+        if slot == n - 1:
+            break
+        last = (acts[-1], waits.pop(0))
+        dys.append(scaled(out_grad_slots[slot], owners[slot]))
+        back = row_sum(after(against(dys[slot], w_out16), last), "row")
+        dpres.append(row_gather(chain(pre, back), "row"))
+        last = (dpres[-1], waits.pop(0) if waits else ())
+
+    grad_in = grad_sum(token_slots[:-2], dpres[:-1], 256)
+    grad_out = grad_sum(acts[:-2], dys[:-1], 128)
+
+    dys.append(scaled(out_grad_slots[n - 1], owners[n - 1], (grad_in, grad_out, acts)))
+    work = [None] + [update_part(part) for part in range(parts)]
+    back = row_sum(against(dys[n - 1], w_out16), "row", work)
+    dpres.append(row_gather(chain(pre, back), "row", work))
+    while work:
+        work.pop(0)()
+    outs_in = update(token_slots[-2:], dpres[-2:], grad_in, w_in, m_in, v_in, 128)
     return (*outs_in, *outs_out)
 
 

time: 420 us -> 399 us (0.950)
  starting transfers between devices: 39.6 us -> 80 us
  waiting for transfers between devices: 227 us -> 195 us
  other arithmetic: 35.3 us -> 17.8 us
  between operations: 16.6 us -> 4.19 us
  Pallas kernels: 66.6 us -> 77.9 us
  local copies, waits for them, and re-layouts: 17.7 us -> 8.5 us
    psum x1 -> x0, waiting for transfers between devices: 40.5 us -> none  [on_device(): lax.psum([(pre_of(slot), against(dys[slot], w_out16)) for slot in early],...]
    ppermute x28 -> x74, starting transfers between devices: 34.8 us -> 72.1 us  [the longest x64 59.3 us: exchange(): lax.ppermute(part, axis, [(i, i ^ mask) for i in range(lax.axis_size(axis...]
    ppermute x28 -> x74, waiting for transfers between devices: 167 us -> 195 us  [the longest x10 127 us: line_gather(): arrived[links, step] = lax.ppermute(came[1 - links, step - 1], axis, pairs)]
    ppermute x3, waiting for transfers between devices: 19.1 us -> 0.01 us  [on_device(): lax.ppermute(codes, 'col', [(i, (i + shift) % n) for i in range(n)])]
    pallas_call x4, Pallas kernels: 49.8 us -> 61.7 us  [update(): pl.pallas_call(functools.partial(update_kernel, shards), grid=(height //...]
    select_n x9 -> x8, other arithmetic: 13 us -> 3.88 us  [row_gather(): jnp.where(odd == 1, jnp.concatenate([came, part]), jnp.concatenate([part,...]
    unnamed x58 -> x66, local copies, waits for them, and re-layouts: 10.2 us -> 4.63 us
    convert_element_type x4, other arithmetic: 6.54 us -> 1.62 us  [scaled(): return (mine[:, None] * shard.astype(jnp.float32)).astype(jnp.bfloat16)]
  transfers between devices with their start and end apart: 32 -> 77, of which waited for: 15 -> 43; matrix products, arithmetic and copies ran while one was open for 13% -> 7% of each run, Pallas kernels for 11% -> 12%
where the time goes in v4:
time: 399 us; the launch traced here: 397 us
  waiting for transfers between devices  195 us (49%)
  starting transfers between devices  80 us (20%)
  Pallas kernels  77.9 us (20%)
  other arithmetic  17.8 us (4%)
  matrix products  13.9 us (3%)
  local copies, waits for them, and re-layouts  8.5 us (2%)
  between operations  4.19 us (1%)
    ppermute x10, waiting for transfers between devices, line_gather(): arrived[links, step] = lax.ppermute(came[1 - links, step - 1], axis, pairs)  127 us
    ppermute x64, waiting for transfers between devices, exchange(): lax.ppermute(part, axis, [(i, i ^ mask) for i in range(lax.axis_size(axis...  68.5 us
    pallas_call x4, Pallas kernels, update(): pl.pallas_call(functools.partial(update_kernel, shards), grid=(height //...  61.7 us
    ppermute x64, starting transfers between devices, exchange(): lax.ppermute(part, axis, [(i, i ^ mask) for i in range(lax.axis_size(axis...  59.3 us
    pallas_call x2, Pallas kernels, grad_sum(): pl.pallas_call(functools.partial(grad_kernel, parts), grid=(height // blo...  16.2 us
    ppermute x10, starting transfers between devices, line_gather(): arrived[links, step] = lax.ppermute(came[1 - links, step - 1], axis, pairs)  12.8 us
  transfers between devices with their start and end apart: 77, of which 43 were waited for; matrix products, arithmetic and copies ran while one was open for 7% of the time, Pallas kernels for 12%

profile of v4, /device:TPU:0, one launch (start us, length us, event | category | flops | bytes accessed | tf_op | source)
XLA Modules:
  0.0 397.5 jit_solution(9700553705220408780)
XLA Ops:
  1.4 4.1 %collective-permute-start.6 = (f32[2,384]{1,0:T(2,128)S(1)}, f32[2,384]{1,0:T(2,128)S(1)}, u32[]{:S(2)}, u32[]{:S(2)}) collective-permute-start(f32[2,384]{1,0:T(2,128)S(1)} %get-tuple-element.215), channel_id=1, source_target_pairs={{0,2},{1,3},{2,0},{3,1},{4,6},{5,7},{6,4},{7,5},{8,10},{9,11},{10,... | collective-permute-start | bytes 9224 | tf_op jit(solution)/shard_map/ppermute | solution.py:270
  13.1 3.5 convert_element_type.81
  32.4 3.2 collective-permute-done.13
  35.5 3.4 collective-permute-done.15
  60.5 3.0 collective-permute-done.23
  72.5 3.0 fusion.18
  75.6 22.7 %collective-permute-done.8 = bf16[384,2304]{1,0:T(8,128)(2,1)S(1)} collective-permute-done((bf16[384,2304]{1,0:T(8,128)(2,1)S(1)}, bf16[384,2304]{1,0:T(8,128)(2,1)S(1)}, u32[]{:S(2)}, u32[]{:S(2)}) %collective-permute-start.8) | collective-permute-done | bytes 1769504 | tf_op jit(solution)/shard_map/ppermute | solution.py:159
  109.8 3.8 collective-permute-done.31
  120.1 25.1 %collective-permute-done.2 = bf16[384,2304]{1,0:T(8,128)(2,1)S(1)} collective-permute-done((bf16[384,2304]{1,0:T(8,128)(2,1)}, bf16[384,2304]{1,0:T(8,128)(2,1)S(1)}, u32[]{:S(2)}, u32[]{:S(2)}) %collective-permute-start.2) | collective-permute-done | bytes 1769504 | tf_op jit(solution)/shard_map/ppermute | solution.py:159
  154.8 3.2 collective-permute-done.37
  158.0 3.4 collective-permute-done.39
  167.9 23.4 %collective-permute-done.10 = bf16[384,2304]{1,0:T(8,128)(2,1)S(1)} collective-permute-done((bf16[384,2304]{1,0:T(8,128)(2,1)S(1)}, bf16[384,2304]{1,0:T(8,128)(2,1)S(1)}, u32[]{:S(2)}, u32[]{:S(2)}) %collective-permute-start.10) | collective-permute-done | bytes 1769504 | tf_op jit(solution)/shard_map/ppermute | solution.py:159
  199.2 3.2 collective-permute-done.45
  202.4 3.4 collective-permute-done.47
  212.4 25.5 %collective-permute-done.4 = bf16[384,2304]{1,0:T(8,128)(2,1)S(1)} collective-permute-done((bf16[384,2304]{1,0:T(8,128)(2,1)S(1)}, bf16[384,2304]{1,0:T(8,128)(2,1)S(1)}, u32[]{:S(2)}, u32[]{:S(2)}) %collective-permute-start.4) | collective-permute-done | bytes 1769504 | tf_op jit(solution)/shard_map/ppermute | solution.py:159
  246.6 3.2 collective-permute-done.53
  249.8 3.4 collective-permute-done.55
  270.0 28.6 %collective-permute-done.67 = bf16[384,2304]{1,0:T(8,128)(2,1)S(1)} collective-permute-done((bf16[384,2304]{1,0:T(8,128)(2,1)S(1)}, bf16[384,2304]{1,0:T(8,128)(2,1)S(1)}, u32[]{:S(2)}, u32[]{:S(2)}) %collective-permute-start.67) | collective-permute-done | bytes 1769504 | tf_op jit(solution)/shard_map/ppermute | solution.py:159
  305.6 6.5 %shard_map.191.refs_4_ = f32[768,2304]{1,0:T(8,128)} custom-call(bf16[384,768]{1,0:T(8,128)(2,1)S(1)} %broadcast_select_fusion.11.refs_0_, bf16[384,768]{1,0:T(8,128)(2,1)S(1)} %broadcast_select_fusion.9.refs_1_, bf16[384,2304]{1,0:T(8,128)(2,1)S(1)} %multiply_convert_fusion.1.refs_2_, bf16[384,2304]{1,0:T(8,128)(2,1)S(1)} %multiply_convert_fusion.2.refs_3_), custom_call_target="tpu_custom_call" | custom-call | flops 2717908992 | bytes 11796480 | tf_op jit(solution)/shard_map/pallas_call | solution.py:69
  312.1 9.8 %shard_map.190.refs_4_ = f32[2304,768]{1,0:T(8,128)} custom-call(bf16[384,2304]{1,0:T(8,128)(2,1)S(1)} %copy-done.1, bf16[384,2304]{1,0:T(8,128)(2,1)} %collective-permute-done.refs_1_, bf16[384,768]{1,0:T(8,128)(2,1)S(1)} %broadcast_select_fusion.10.refs_2_, bf16[384,768]{1,0:T(8,128)(2,1)S(1)} %broadcast_select_fusion.8.refs_3_), custom_call_target="tpu_custom_call" | custom-call | flops 2717908992 | bytes 11796480 | tf_op jit(solution)/shard_map/pallas_call | solution.py:69
  330.7 10.8 %shard_map.192 = (f32[768,2304]{1,0:T(8,128)}, f32[768,2304]{1,0:T(8,128)}, f32[768,2304]{1,0:T(8,128)}) custom-call(bf16[384,768]{1,0:T(8,128)(2,1)} %broadcast_select_fusion.7.refs_0_, bf16[384,768]{1,0:T(8,128)(2,1)} %broadcast_select_fusion.5.refs_1_, bf16[384,2304]{1,0:T(8,128)(2,1)} %copy-done.3, bf16[384,2304]{1,0:T(8,128)(2,1)} %copy-done.4, ...), custom_call_target="tpu_custom_call" | custom-call | flops 905969664 | bytes 18874368 | tf_op jit(solution)/shard_map/pallas_call | solution.py:111
  345.2 10.8 %shard_map.193 = (f32[768,2304]{1,0:T(8,128)}, f32[768,2304]{1,0:T(8,128)}, f32[768,2304]{1,0:T(8,128)}) custom-call(bf16[384,768]{1,0:T(8,128)(2,1)} %broadcast_select_fusion.7.refs_0_, bf16[384,768]{1,0:T(8,128)(2,1)} %broadcast_select_fusion.5.refs_1_, bf16[384,2304]{1,0:T(8,128)(2,1)} %copy-done.3, ...), custom_call_target="tpu_custom_call", output_to_operand_aliasing={{0}: (8, {}), {1}: (9, {}), {2}: (10, {})} | custom-call | flops 905969664 | bytes 18874368 | tf_op jit(solution)/shard_map/pallas_call | solution.py:111
  356.3 10.8 %shard_map.194 = (f32[768,2304]{1,0:T(8,128)}, f32[768,2304]{1,0:T(8,128)}, f32[768,2304]{1,0:T(8,128)}) custom-call(bf16[384,768]{1,0:T(8,128)(2,1)} %broadcast_select_fusion.7.refs_0_, bf16[384,768]{1,0:T(8,128)(2,1)} %broadcast_select_fusion.5.refs_1_, bf16[384,2304]{1,0:T(8,128)(2,1)} %copy-done.3, ...), custom_call_target="tpu_custom_call", output_to_operand_aliasing={{0}: (8, {}), {1}: (9, {}), {2}: (10, {})} | custom-call | flops 905969664 | bytes 18874368 | tf_op jit(solution)/shard_map/pallas_call | solution.py:111
  368.1 29.3 %shard_map.195 = (f32[2304,768]{1,0:T(8,128)}, f32[2304,768]{1,0:T(8,128)}, f32[2304,768]{1,0:T(8,128)}) custom-call(bf16[384,2304]{1,0:T(8,128)(2,1)} %copy-done.5, bf16[384,2304]{1,0:T(8,128)(2,1)} %copy-done.6, bf16[384,768]{1,0:T(8,128)(2,1)} %broadcast_select_fusion.6.refs_2_, bf16[384,768]{1,0:T(8,128)(2,1)} %broadcast_select_fusion.4.refs_3_, ...), custom_call_target="tpu_custom_call" | custom-call | flops 2717908992 | bytes 54263808 | tf_op jit(solution)/shard_map/pallas_call | solution.py:111
  (340 shorter events, 146.1 us)
Async XLA Ops:
  1.4 24.0 %collective-permute-start.6 = (f32[2,384]{1,0:T(2,128)S(1)}, f32[2,384]{1,0:T(2,128)S(1)}, u32[]{:S(2)}, u32[]{:S(2)}) collective-permute-start(f32[2,384]{1,0:T(2,128)S(1)} %get-tuple-element.215), channel_id=1, source_target_pairs={{0,2},{1,3},{2,0},{3,1},{4,6},{5,7},{6,4},{7,5},{8,10},{9,11},{10,... | collective-permute-start | bytes 9224 | tf_op jit(solution)/shard_map/ppermute | solution.py:270
  5.5 20.0 %collective-permute-start.5 = (f32[2,384]{1,0:T(2,128)S(1)}, f32[2,384]{1,0:T(2,128)S(1)}, u32[]{:S(2)}, u32[]{:S(2)}) collective-permute-start(f32[2,384]{1,0:T(2,128)S(1)} %get-tuple-element.215), channel_id=1, source_target_pairs={{0,1},{1,2},{2,3},{3,0},{4,5},{5,6},{6,7},{7,4},{8,9},{9,10},{10,1... | collective-permute-start | bytes 9224 | tf_op jit(solution)/shard_map/ppermute | solution.py:270
  9.4 40.4 %collective-permute-start.1 = (bf16[384,2304]{1,0:T(8,128)(2,1)}, bf16[384,2304]{1,0:T(8,128)(2,1)}, u32[]{:S(2)}, u32[]{:S(2)}) collective-permute-start(bf16[384,2304]{1,0:T(8,128)(2,1)} %refs_0_.1), channel_id=1, source_target_pairs={{1,2},{2,1},{5,6},{6,5},{9,10},{10,9},{13,14},{14,13},{17,18},{18,... | collective-permute-start | bytes 5308424 | tf_op jit(solution)/shard_map/ppermute | solution.py:159
  11.2 39.8 %collective-permute-start = (bf16[384,2304]{1,0:T(8,128)(2,1)}, bf16[384,2304]{1,0:T(8,128)(2,1)}, u32[]{:S(2)}, u32[]{:S(2)}) collective-permute-start(bf16[384,2304]{1,0:T(8,128)(2,1)} %refs_0_.1), channel_id=1, source_target_pairs={{0,1},{1,0},{2,3},{3,2},{4,5},{5,4},{6,7},{7,6},{8,9},{9,8},{10,11... | collective-permute-start | bytes 5308424 | tf_op jit(solution)/shard_map/ppermute | solution.py:159
  57.6 40.6 %collective-permute-start.8 = (bf16[384,2304]{1,0:T(8,128)(2,1)S(1)}, bf16[384,2304]{1,0:T(8,128)(2,1)S(1)}, u32[]{:S(2)}, u32[]{:S(2)}) collective-permute-start(bf16[384,2304]{1,0:T(8,128)(2,1)S(1)} %copy-done.13), channel_id=1, source_target_pairs={{0,1},{1,0},{2,3},{3,2},{4,5},{5,4},{6,7},{7,6},{8,9},{9,8},{10,11... | collective-permute-start | bytes 5308424 | tf_op jit(solution)/shard_map/ppermute | solution.py:159
  72.4 25.8 %collective-permute-start.27 = (bf16[192,768]{1,0:T(8,128)(2,1)S(1)}, bf16[192,768]{1,0:T(8,128)(2,1)S(1)}, u32[]{:S(2)}, u32[]{:S(2)}) collective-permute-start(bf16[192,768]{1,0:T(8,128)(2,1)S(1)} %pad_maximum_fusion.1), channel_id=1, source_target_pairs={{0,4},{4,0},{8,12},{12,8},{16,20},{20,16},{24,28},{28,24},{1,5},{5... | collective-permute-start | bytes 884744 | tf_op jit(solution)/shard_map/ppermute | solution.py:189
  99.5 45.8 %collective-permute-start.3 = (bf16[384,2304]{1,0:T(8,128)(2,1)}, bf16[384,2304]{1,0:T(8,128)(2,1)S(1)}, u32[]{:S(2)}, u32[]{:S(2)}) collective-permute-start(bf16[384,2304]{1,0:T(8,128)(2,1)} %collective-permute-done.refs_1_), channel_id=1, source_target_pairs={{1,2},{2,1},{5,6},{6,5},{9,10},{10,9},{13,14},{14,13},{17,18},{18,... | collective-permute-start | bytes 5308424 | tf_op jit(solution)/shard_map/ppermute | solution.py:159
  100.4 44.9 %collective-permute-start.2 = (bf16[384,2304]{1,0:T(8,128)(2,1)}, bf16[384,2304]{1,0:T(8,128)(2,1)S(1)}, u32[]{:S(2)}, u32[]{:S(2)}) collective-permute-start(bf16[384,2304]{1,0:T(8,128)(2,1)} %collective-permute-done.1), channel_id=1, source_target_pairs={{1,0},{2,3},{5,4},{6,7},{9,8},{10,11},{13,12},{14,15},{17,16},{18,... | collective-permute-start | bytes 5308424 | tf_op jit(solution)/shard_map/ppermute | solution.py:159
  115.0 30.3 %collective-permute-start.34 = (bf16[48,768]{1,0:T(8,128)(2,1)S(1)}, bf16[48,768]{1,0:T(8,128)(2,1)S(1)}, u32[]{:S(2)}, u32[]{:S(2)}) collective-permute-start(bf16[48,768]{1,0:T(8,128)(2,1)S(1)} %get-tuple-element.152), channel_id=1, source_target_pairs={{0,8},{4,12},{8,0},{12,4},{16,24},{20,28},{24,16},{28,20},{1,9},{5... | collective-permute-start | bytes 221192 | tf_op jit(solution)/shard_map/ppermute | solution.py:189
  116.6 28.7 %collective-permute-start.33 = (bf16[48,768]{1,0:T(8,128)(2,1)S(1)}, bf16[48,768]{1,0:T(8,128)(2,1)S(1)}, u32[]{:S(2)}, u32[]{:S(2)}) collective-permute-start(bf16[48,768]{1,0:T(8,128)(2,1)S(1)} %get-tuple-element.152), channel_id=1, source_target_pairs={{0,16},{4,20},{8,24},{12,28},{16,0},{20,4},{24,8},{28,12},{1,17},{... | collective-permute-start | bytes 221192 | tf_op jit(solution)/shard_map/ppermute | solution.py:189
  117.1 28.2 %collective-permute-start.32 = (bf16[48,768]{1,0:T(8,128)(2,1)S(1)}, bf16[48,768]{1,0:T(8,128)(2,1)S(1)}, u32[]{:S(2)}, u32[]{:S(2)}) collective-permute-start(bf16[48,768]{1,0:T(8,128)(2,1)S(1)} %get-tuple-element.152), channel_id=1, source_target_pairs={{0,24},{4,28},{8,16},{12,20},{16,8},{20,12},{24,0},{28,4},{1,25},{... | collective-permute-start | bytes 221192 | tf_op jit(solution)/shard_map/ppermute | solution.py:189
  148.7 42.7 %collective-permute-start.10 = (bf16[384,2304]{1,0:T(8,128)(2,1)S(1)}, bf16[384,2304]{1,0:T(8,128)(2,1)S(1)}, u32[]{:S(2)}, u32[]{:S(2)}) collective-permute-start(bf16[384,2304]{1,0:T(8,128)(2,1)S(1)} %copy-done.15), channel_id=1, source_target_pairs={{1,0},{2,3},{5,4},{6,7},{9,8},{10,11},{13,12},{14,15},{17,16},{18,... | collective-permute-start | bytes 5308424 | tf_op jit(solution)/shard_map/ppermute | solution.py:159
  150.1 41.2 %collective-permute-start.11 = (bf16[384,2304]{1,0:T(8,128)(2,1)S(1)}, bf16[384,2304]{1,0:T(8,128)(2,1)S(1)}, u32[]{:S(2)}, u32[]{:S(2)}) collective-permute-start(bf16[384,2304]{1,0:T(8,128)(2,1)S(1)} %copy-done.17), channel_id=1, source_target_pairs={{1,2},{2,1},{5,6},{6,5},{9,10},{10,9},{13,14},{14,13},{17,18},{18,... | collective-permute-start | bytes 5308424 | tf_op jit(solution)/shard_map/ppermute | solution.py:159
  162.8 28.6 %collective-permute-start.42 = (bf16[48,768]{1,0:T(8,128)(2,1)S(1)}, bf16[48,768]{1,0:T(8,128)(2,1)S(1)}, u32[]{:S(2)}, u32[]{:S(2)}) collective-permute-start(bf16[48,768]{1,0:T(8,128)(2,1)S(1)} %multiply_convert_fusion.8), channel_id=1, source_target_pairs={{0,8},{4,12},{8,0},{12,4},{16,24},{20,28},{24,16},{28,20},{1,9},{5... | collective-permute-start | bytes 221192 | tf_op jit(solution)/shard_map/ppermute | solution.py:189
  163.6 27.8 %collective-permute-start.41 = (bf16[48,768]{1,0:T(8,128)(2,1)S(1)}, bf16[48,768]{1,0:T(8,128)(2,1)S(1)}, u32[]{:S(2)}, u32[]{:S(2)}) collective-permute-start(bf16[48,768]{1,0:T(8,128)(2,1)S(1)} %multiply_convert_fusion.8), channel_id=1, source_target_pairs={{0,16},{4,20},{8,24},{12,28},{16,0},{20,4},{24,8},{28,12},{1,17},{... | collective-permute-start | bytes 221192 | tf_op jit(solution)/shard_map/ppermute | solution.py:189
  164.1 27.3 %collective-permute-start.40 = (bf16[48,768]{1,0:T(8,128)(2,1)S(1)}, bf16[48,768]{1,0:T(8,128)(2,1)S(1)}, u32[]{:S(2)}, u32[]{:S(2)}) collective-permute-start(bf16[48,768]{1,0:T(8,128)(2,1)S(1)} %multiply_convert_fusion.8), channel_id=1, source_target_pairs={{0,24},{4,28},{8,16},{12,20},{16,8},{20,12},{24,0},{28,4},{1,25},{... | collective-permute-start | bytes 221192 | tf_op jit(solution)/shard_map/ppermute | solution.py:189
  193.7 44.2 %collective-permute-start.4 = (bf16[384,2304]{1,0:T(8,128)(2,1)S(1)}, bf16[384,2304]{1,0:T(8,128)(2,1)S(1)}, u32[]{:S(2)}, u32[]{:S(2)}) collective-permute-start(bf16[384,2304]{1,0:T(8,128)(2,1)S(1)} %collective-permute-done.3), channel_id=1, source_target_pairs={{1,0},{2,3},{5,4},{6,7},{9,8},{10,11},{13,12},{14,15},{17,16},{18,... | collective-permute-start | bytes 5308424 | tf_op jit(solution)/shard_map/ppermute | solution.py:159
  207.3 30.6 %collective-permute-start.50 = (bf16[48,768]{1,0:T(8,128)(2,1)S(1)}, bf16[48,768]{1,0:T(8,128)(2,1)S(1)}, u32[]{:S(2)}, u32[]{:S(2)}) collective-permute-start(bf16[48,768]{1,0:T(8,128)(2,1)S(1)} %get-tuple-element.132), channel_id=1, source_target_pairs={{0,8},{4,12},{8,0},{12,4},{16,24},{20,28},{24,16},{28,20},{1,9},{5... | collective-permute-start | bytes 221192 | tf_op jit(solution)/shard_map/ppermute | solution.py:189
  208.0 29.8 %collective-permute-start.49 = (bf16[48,768]{1,0:T(8,128)(2,1)S(1)}, bf16[48,768]{1,0:T(8,128)(2,1)S(1)}, u32[]{:S(2)}, u32[]{:S(2)}) collective-permute-start(bf16[48,768]{1,0:T(8,128)(2,1)S(1)} %get-tuple-element.132), channel_id=1, source_target_pairs={{0,16},{4,20},{8,24},{12,28},{16,0},{20,4},{24,8},{28,12},{1,17},{... | collective-permute-start | bytes 221192 | tf_op jit(solution)/shard_map/ppermute | solution.py:189
  208.6 29.3 %collective-permute-start.48 = (bf16[48,768]{1,0:T(8,128)(2,1)S(1)}, bf16[48,768]{1,0:T(8,128)(2,1)S(1)}, u32[]{:S(2)}, u32[]{:S(2)}) collective-permute-start(bf16[48,768]{1,0:T(8,128)(2,1)S(1)} %get-tuple-element.132), channel_id=1, source_target_pairs={{0,24},{4,28},{8,16},{12,20},{16,8},{20,12},{24,0},{28,4},{1,25},{... | collective-permute-start | bytes 221192 | tf_op jit(solution)/shard_map/ppermute | solution.py:189
  258.2 40.5 %collective-permute-start.67 = (bf16[384,2304]{1,0:T(8,128)(2,1)S(1)}, bf16[384,2304]{1,0:T(8,128)(2,1)S(1)}, u32[]{:S(2)}, u32[]{:S(2)}) collective-permute-start(bf16[384,2304]{1,0:T(8,128)(2,1)S(1)} %collective-permute-done.11), channel_id=1, source_target_pairs={{1,0},{2,3},{5,4},{6,7},{9,8},{10,11},{13,12},{14,15},{17,16},{18,... | collective-permute-start | bytes 5308424 | tf_op jit(solution)/shard_map/ppermute | solution.py:159
  266.4 32.2 %collective-permute-start.61 = (f32[48,768]{1,0:T(8,128)S(1)}, f32[48,768]{1,0:T(8,128)S(1)}, u32[]{:S(2)}, u32[]{:S(2)}) collective-permute-start(f32[48,768]{1,0:T(8,128)S(1)} %get-tuple-element.175), channel_id=1, source_target_pairs={{0,8},{4,12},{8,0},{12,4},{16,24},{20,28},{24,16},{28,20},{1,9},{5... | collective-permute-start | bytes 442376 | tf_op jit(solution)/shard_map/ppermute | solution.py:189
  267.8 30.8 %collective-permute-start.63 = (f32[48,768]{1,0:T(8,128)S(1)}, f32[48,768]{1,0:T(8,128)S(1)}, u32[]{:S(2)}, u32[]{:S(2)}) collective-permute-start(f32[48,768]{1,0:T(8,128)S(1)} %get-tuple-element.176), channel_id=1, source_target_pairs={{0,24},{4,28},{8,16},{12,20},{16,8},{20,12},{24,0},{28,4},{1,25},{... | collective-permute-start | bytes 442376 | tf_op jit(solution)/shard_map/ppermute | solution.py:189
  269.5 29.2 %collective-permute-start.62 = (f32[48,768]{1,0:T(8,128)S(1)}, f32[48,768]{1,0:T(8,128)S(1)}, u32[]{:S(2)}, u32[]{:S(2)}) collective-permute-start(f32[48,768]{1,0:T(8,128)S(1)} %get-tuple-element.177), channel_id=1, source_target_pairs={{0,16},{4,20},{8,24},{12,28},{16,0},{20,4},{24,8},{28,12},{1,17},{... | collective-permute-start | bytes 442376 | tf_op jit(solution)/shard_map/ppermute | solution.py:189
  (74 other events, 595.1 us)

commit v5 on v4

--- a/solution.py
+++ b/solution.py
@@ -82,50 +82,37 @@
     )(*lefts, *rights)
 
 
-def update_kernel(shards, *refs):
-    lefts, rights = refs[:shards], refs[shards : 2 * shards]
-    grad, w, m, v = refs[2 * shards : 2 * shards + 4]
-    new_w, new_m, new_v, total = refs[-4:]
-    summed = grad[...]
-    for left, right in zip(lefts, rights):
-        summed += over_rows(left[...], right[...])
-    total[...] = summed
-
-    def eight_rows(i, carry):
-        rows = pl.ds(pl.multiple_of(8 * i, 8), 8)
-        new_w[rows, :], new_m[rows, :], new_v[rows, :] = adamw(
-            w[rows, :], m[rows, :], v[rows, :], total[rows, :]
-        )
-        return carry
-
-    lax.fori_loop(0, total.shape[0] // 8, eight_rows, 0, unroll=2)
-
-
-def update(lefts, rights, grad, w, m, v, most, part=0, parts=1, so_far=()):
-    shards = len(lefts)
-    rows, height = lefts[0].shape
-    width = rights[0].shape[1] // parts
+def update_kernel(left, right, grad, w, m, v, *refs):
+    new_w, new_m, new_v = refs[-3:]
+    total = grad[...] + over_rows(left[...], right[...])
+    new_w[...], new_m[...], new_v[...] = adamw(w[...], m[...], v[...], total)
+
+
+def update(left, right, grad, w, m, v, most, part=0, parts=1, so_far=()):
+    rows, height = left.shape
+    width = right.shape[1] // parts
     block = block_of(height, most)
     panel = pl.BlockSpec((block, width), lambda i: (i, part))
     shape = jax.ShapeDtypeStruct(w.shape, jnp.float32)
     return pl.pallas_call(
-        functools.partial(update_kernel, shards),
+        update_kernel,
         grid=(height // block,),
-        in_specs=[pl.BlockSpec((rows, block), lambda i: (0, i))] * shards
-        + [pl.BlockSpec((rows, width), lambda i: (0, part))] * shards
+        in_specs=[
+            pl.BlockSpec((rows, block), lambda i: (0, i)),
+            pl.BlockSpec((rows, width), lambda i: (0, part)),
+        ]
         + [panel] * 4
         + [pl.BlockSpec(memory_space=pl.ANY)] * len(so_far),
         out_specs=[panel] * 3,
         out_shape=[shape] * 3,
-        scratch_shapes=[pltpu.VMEM((block, width), jnp.float32)],
-        input_output_aliases={2 * shards + 4 + i: i for i in range(len(so_far))},
+        input_output_aliases={6 + i: i for i in range(len(so_far))},
         compiler_params=pltpu.CompilerParams(vmem_limit_bytes=56 * 2**20),
         cost_estimate=pl.CostEstimate(
-            flops=2 * shards * rows * height * width,
-            bytes_accessed=7 * 4 * height * width + 2 * shards * rows * (height + width),
+            flops=2 * rows * height * width,
+            bytes_accessed=7 * 4 * height * width + 2 * rows * (height + width),
             transcendentals=2 * height * width,
         ),
-    )(*lefts, *rights, grad, w, m, v, *so_far)
+    )(left, right, grad, w, m, v, *so_far)
 
 
 def link_pairs(n, first, step):
@@ -176,7 +163,7 @@
                 choice = jnp.where(mine, came[source], choice)
         slots.append(choice)
         owners.append(jnp.array(origins, dtype=jnp.int32)[here])
-    return slots, owners
+    return slots, owners, [[came[at] for at in came if at[1] == step] for step in range(n)]
 
 
 def after(value, earlier):
@@ -194,27 +181,27 @@
 def row_sum(part, axis, beside=None):
     here = lax.axis_index(axis)
     others = lax.axis_size(axis) // 2
-    half = part.shape[0] // 2
+    half = part.shape[-2] // 2
     odd, place = here % 2, here // 2
-    kept = lax.dynamic_slice_in_dim(part, odd * half, half)
-    sent = lax.dynamic_slice_in_dim(part, (1 - odd) * half, half)
+    kept = lax.dynamic_slice_in_dim(part, odd * half, half, axis=-2)
+    sent = lax.dynamic_slice_in_dim(part, (1 - odd) * half, half, axis=-2)
     part = kept + exchange(sent, axis, 1, beside)
     piece = half // others
-    total = lax.dynamic_slice_in_dim(part, place * piece, piece)
-    came = [
-        exchange(lax.dynamic_slice_in_dim(part, (place ^ other) * piece, piece), axis, 2 * other)
-        for other in range(1, others)
-    ]
+
+    def piece_of(which):
+        return lax.dynamic_slice_in_dim(part, which * piece, piece, axis=-2)
+
+    came = [exchange(piece_of(place ^ d), axis, 2 * d) for d in range(1, others)]
     work = beside.pop(0) if beside else None
     came = after(came, work() if callable(work) else work)
-    return functools.reduce(jnp.add, came, total)
+    return functools.reduce(jnp.add, came, piece_of(place))
 
 
 def row_gather(part, axis, beside=None):
     here = lax.axis_index(axis)
     others = lax.axis_size(axis) // 2
     odd, place = here % 2, here // 2
-    pieces = [part] + [exchange(part, axis, 2 * other) for other in range(1, others)]
+    pieces = [part] + [exchange(part, axis, 2 * d) for d in range(1, others)]
     work = beside.pop(0) if beside else None
     pieces = after(pieces, work() if callable(work) else work)
     bit = 1
@@ -223,10 +210,12 @@
             jnp.where((place // bit) % 2 == 1, pieces[i ^ bit], pieces[i]) for i in range(others)
         ]
         bit *= 2
-    part = jnp.concatenate(pieces)
+    part = jnp.concatenate(pieces, axis=-2)
     came = exchange(part, axis, 1, beside)
     return jnp.where(
-        odd == 1, jnp.concatenate([came, part]), jnp.concatenate([part, came])
+        odd == 1,
+        jnp.concatenate([came, part], axis=-2),
+        jnp.concatenate([part, came], axis=-2),
     )
 
 
@@ -292,46 +281,54 @@
     def chain(pre, back):
         return (back * 2.0 * jnp.maximum(pre, 0.0)).astype(jnp.bfloat16)
 
-    token_slots, owners = line_gather(tokens, "col")
-    out_grad_slots, _ = line_gather(out_grad, "col")
-    parts = 3
+    token_slots, owners, tokens_came = line_gather(tokens, "col")
+    out_grad_slots, _, out_grads_came = line_gather(out_grad, "col")
+    parts = next(p for p in (2, 3, 1) if w_out.shape[1] % (128 * p) == 0)
     outs_out = ()
 
     def update_part(part):
         def run():
             nonlocal outs_out
             outs_out = update(
-                acts[-2:], dys[-2:], grad_out, w_out, m_out, v_out, 128, part, parts, outs_out
+                acts[-1], dys[-1], grad_out, w_out, m_out, v_out, 128, part, parts, outs_out
             )
             return outs_out
 
         return run
 
-    waits = [x for pair in zip(token_slots[1:], out_grad_slots[1:]) for x in pair][:-1]
-    acts, dpres, dys = [], [], []
-    last = None
-    for slot in range(n):
-        pre = row_sum(after(pre_of(token_slots[slot]), last), "row")
-        latest = [out_grad_slots[n - 1]] if slot == n - 1 else None
-        acts.append(row_gather(square(pre), "row", latest))
-        if slot == n - 1:
-            break
-        last = (acts[-1], waits.pop(0))
-        dys.append(scaled(out_grad_slots[slot], owners[slot]))
-        back = row_sum(after(against(dys[slot], w_out16), last), "row")
-        dpres.append(row_gather(chain(pre, back), "row"))
-        last = (dpres[-1], waits.pop(0) if waits else ())
-
-    grad_in = grad_sum(token_slots[:-2], dpres[:-1], 256)
-    grad_out = grad_sum(acts[:-2], dys[:-1], 128)
-
-    dys.append(scaled(out_grad_slots[n - 1], owners[n - 1], (grad_in, grad_out, acts)))
+    dys = [scaled(out_grad, here)]
+    pre = row_sum(pre_of(tokens), "row")
+    acts, dpres = [row_gather(square(pre), "row")], []
+    both = jnp.stack([against(dys[0], w_out16), pre_of(token_slots[1])])
+    both = row_sum(after(both, (acts[0], tokens_came[1])), "row")
+    both, pre = jnp.stack([chain(pre, both[0]), square(both[1])]), both[1]
+    last = both = row_gather(both, "row")
+    acts.append(both[1])
+    dpres.append(both[0])
+    for slot in range(1, n):
+        if slot > 1:
+            last = (last, tokens_came[slot])
+            beside, latest = None, None
+            if slot == n - 1:
+                grad_in = grad_sum(token_slots[:-1], dpres, 256)
+                grad_out = grad_sum(acts, dys, 128)
+                beside, latest = [None, (grad_in, grad_out)], [out_grads_came[slot]]
+            pre = row_sum(after(pre_of(token_slots[slot]), last), "row", beside)
+            last = row_gather(square(pre), "row", latest)
+            acts.append(last)
+        if slot < n - 1:
+            dys.append(scaled(out_grad_slots[slot], owners[slot]))
+            back = after(against(dys[slot], w_out16), (last, out_grads_came[slot]))
+            last = row_gather(chain(pre, row_sum(back, "row")), "row")
+            dpres.append(last)
+
+    dys.append(scaled(out_grad_slots[n - 1], owners[n - 1], acts[-1]))
     work = [None] + [update_part(part) for part in range(parts)]
     back = row_sum(against(dys[n - 1], w_out16), "row", work)
     dpres.append(row_gather(chain(pre, back), "row", work))
     while work:
         work.pop(0)()
-    outs_in = update(token_slots[-2:], dpres[-2:], grad_in, w_in, m_in, v_in, 128)
+    outs_in = update(token_slots[-1], dpres[-1], grad_in, w_in, m_in, v_in, 256)
     return (*outs_in, *outs_out)
 
 

time: 399 us -> 330 us (0.83)
  waiting for transfers between devices: 195 us -> 141 us
  Pallas kernels: 77.9 us -> 65.4 us
  starting transfers between devices: 80 us -> 74.5 us
    ppermute x10, waiting for transfers between devices: 127 us -> 91.7 us  [line_gather(): arrived[links, step] = lax.ppermute(came[1 - links, step - 1], axis, pairs)]
    ppermute x64 -> x56, waiting for transfers between devices: 68.5 us -> 49.1 us  [exchange(): lax.ppermute(part, axis, [(i, i ^ mask) for i in range(lax.axis_size(axis...]
    pallas_call x4 -> x3, Pallas kernels: 61.7 us -> 46.5 us  [update(): pl.pallas_call(update_kernel, grid=(height // block,), in_specs=[pl.Block...]
    ppermute x64 -> x56, starting transfers between devices: 59.3 us -> 52.7 us  [exchange(): lax.ppermute(part, axis, [(i, i ^ mask) for i in range(lax.axis_size(axis...]
  transfers between devices with their start and end apart: 77 -> 69, of which waited for: 43 -> 31; matrix products, arithmetic and copies ran while one was open for 7% -> 9% of each run, Pallas kernels for 12% -> 13%
where the time goes in v5:
time: 330 us
  waiting for transfers between devices  141 us (43%)
  starting transfers between devices  74.5 us (23%)
  Pallas kernels  65.4 us (20%)
  other arithmetic  21.2 us (6%)
  matrix products  13.9 us (4%)
  local copies, waits for them, and re-layouts  9.76 us (3%)
  between operations  4.02 us (1%)
    ppermute x10, waiting for transfers between devices, line_gather(): arrived[links, step] = lax.ppermute(came[1 - links, step - 1], axis, pairs)  91.7 us
    ppermute x56, starting transfers between devices, exchange(): lax.ppermute(part, axis, [(i, i ^ mask) for i in range(lax.axis_size(axis...  52.7 us
    ppermute x56, waiting for transfers between devices, exchange(): lax.ppermute(part, axis, [(i, i ^ mask) for i in range(lax.axis_size(axis...  49.1 us
    pallas_call x3, Pallas kernels, update(): pl.pallas_call(update_kernel, grid=(height // block,), in_specs=[pl.Block...  46.5 us
    pallas_call x2, Pallas kernels, grad_sum(): pl.pallas_call(functools.partial(grad_kernel, parts), grid=(height // blo...  18.9 us
    ppermute x10, starting transfers between devices, line_gather(): arrived[links, step] = lax.ppermute(came[1 - links, step - 1], axis, pairs)  13.8 us
    ppermute x3, starting transfers between devices, on_device(): lax.ppermute(codes, 'col', [(i, (i + shift) % n) for i in range(n)])  7.93 us
    dot_general x4, matrix products, pre_of(): return jnp.dot(shard, w_in16, preferred_element_type=jnp.float32)  7.62 us
  transfers between devices with their start and end apart: 69, of which 31 were waited for; matrix products, arithmetic and copies ran while one was open for 9% of the time, Pallas kernels for 13%

profile of v5, /device:TPU:0, one launch (start us, length us, event | category | flops | bytes accessed | tf_op | source)
XLA Modules:
  0.0 329.6 jit_solution(15258327827017698102)
XLA Ops:
  1.4 4.1 %collective-permute-start.6 = (f32[2,384]{1,0:T(2,128)S(1)}, f32[2,384]{1,0:T(2,128)S(1)}, u32[]{:S(2)}, u32[]{:S(2)}) collective-permute-start(f32[2,384]{1,0:T(2,128)S(1)} %get-tuple-element.196), channel_id=1, source_target_pairs={{0,2},{1,3},{2,0},{3,1},{4,6},{5,7},{6,4},{7,5},{8,10},{9,11},{10,... | collective-permute-start | bytes 9224 | tf_op jit(solution)/shard_map/ppermute | solution.py:259
  7.1 2.2 collective-permute-start.7
  13.1 3.5 %convert_element_type.80 = bf16[2304,768]{1,0:T(8,128)(2,1)S(1)} convert(f32[2304,768]{1,0:T(8,128)} %w.5) | non-fusion elementwise | flops 1769472 | bytes 10616832 | tf_op jit(solution)/shard_map/convert_element_type | solution.py:266
  18.2 2.1 convert_element_type.81
  32.4 3.2 collective-permute-done.13
  35.5 3.4 %collective-permute-done.15 = f32[48,768]{1,0:T(8,128)S(1)} collective-permute-done((f32[48,768]{1,0:T(8,128)S(1)}, f32[48,768]{1,0:T(8,128)S(1)}, u32[]{:S(2)}, u32[]{:S(2)}) %collective-permute-start.15) | collective-permute-done | bytes 147488 | tf_op jit(solution)/shard_map/ppermute | solution.py:176
  51.1 3.0 convolution_bitcast_fusion
  55.2 3.2 collective-permute-start.8
  59.8 1.9 collective-permute-start.23
  62.2 6.4 %collective-permute-done.21 = f32[2,48,768]{2,1,0:T(8,128)S(1)} collective-permute-done((f32[2,48,768]{2,1,0:T(8,128)S(1)}, f32[2,48,768]{2,1,0:T(8,128)S(1)}, u32[]{:S(2)}, u32[]{:S(2)}) %collective-permute-start.21) | collective-permute-done | bytes 294944 | tf_op jit(solution)/shard_map/ppermute | solution.py:176
  68.6 6.1 %collective-permute-done.23 = f32[2,48,768]{2,1,0:T(8,128)S(1)} collective-permute-done((f32[2,48,768]{2,1,0:T(8,128)S(1)}, f32[2,48,768]{2,1,0:T(8,128)S(1)}, u32[]{:S(2)}, u32[]{:S(2)}) %collective-permute-start.23) | collective-permute-done | bytes 294944 | tf_op jit(solution)/shard_map/ppermute | solution.py:176
  81.8 15.4 %collective-permute-done.8 = bf16[384,2304]{1,0:T(8,128)(2,1)S(1)} collective-permute-done((bf16[384,2304]{1,0:T(8,128)(2,1)S(1)}, bf16[384,2304]{1,0:T(8,128)(2,1)S(1)}, u32[]{:S(2)}, u32[]{:S(2)}) %collective-permute-start.8) | collective-permute-done | bytes 1769504 | tf_op jit(solution)/shard_map/ppermute | solution.py:146
  110.4 28.1 %collective-permute-done.2 = bf16[384,2304]{1,0:T(8,128)(2,1)} collective-permute-done((bf16[384,2304]{1,0:T(8,128)(2,1)}, bf16[384,2304]{1,0:T(8,128)(2,1)}, u32[]{:S(2)}, u32[]{:S(2)}) %collective-permute-start.2) | collective-permute-done | bytes 1769504 | tf_op jit(solution)/shard_map/ppermute | solution.py:146
  147.4 2.0 collective-permute-done.32
  157.4 22.2 %collective-permute-done.10 = bf16[384,2304]{1,0:T(8,128)(2,1)S(1)} collective-permute-done((bf16[384,2304]{1,0:T(8,128)(2,1)}, bf16[384,2304]{1,0:T(8,128)(2,1)S(1)}, u32[]{:S(2)}, u32[]{:S(2)}) %collective-permute-start.10) | collective-permute-done | bytes 1769504 | tf_op jit(solution)/shard_map/ppermute | solution.py:146
  185.9 2.4 collective-permute-done.40
  197.7 25.6 %collective-permute-done.4 = bf16[384,2304]{1,0:T(8,128)(2,1)S(1)} collective-permute-done((bf16[384,2304]{1,0:T(8,128)(2,1)}, bf16[384,2304]{1,0:T(8,128)(2,1)S(1)}, u32[]{:S(2)}, u32[]{:S(2)}) %collective-permute-start.4) | collective-permute-done | bytes 1769504 | tf_op jit(solution)/shard_map/ppermute | solution.py:146
  228.2 2.4 collective-permute-done.48
  234.4 8.1 %shard_map.191.grad = f32[768,2304]{1,0:T(8,128)} custom-call(bf16[384,768]{1,0:T(8,128)(2,1)S(1)} %copy-done, bf16[384,768]{1,0:T(8,128)(2,1)S(1)} %get-tuple-element.156.refs_1_, bf16[384,768]{1,0:T(8,128)(2,1)S(1)} %broadcast_select_fusion.6.refs_2_, bf16[384,2304]{1,0:T(8,128)(2,1)S(1)} %multiply_convert_fusion.1.refs_3_, ...), custom_call_target="tpu_custom_call" | custom-call | flops 4076863488 | bytes 14155776 | tf_op jit(solution)/shard_map/pallas_call | solution.py:69
  247.4 10.8 %shard_map.190.grad = f32[2304,768]{1,0:T(8,128)} custom-call(bf16[384,2304]{1,0:T(8,128)(2,1)S(1)} %copy-done.2, bf16[384,2304]{1,0:T(8,128)(2,1)} %collective-permute-done.refs_1_, bf16[384,2304]{1,0:T(8,128)(2,1)S(1)} %broadcast_select_fusion.refs_2_, bf16[384,768]{1,0:T(8,128)(2,1)S(1)} %get-tuple-element.157.refs_3_, ...), custom_call_target="tpu_custom_call" | custom-call | flops 4076863488 | bytes 14155776 | tf_op jit(solution)/shard_map/pallas_call | solution.py:69
  261.8 2.4 collective-permute-done.58
  276.5 12.0 %shard_map.192 = (f32[768,2304]{1,0:T(8,128)}, f32[768,2304]{1,0:T(8,128)}, f32[768,2304]{1,0:T(8,128)}) custom-call(bf16[384,768]{1,0:T(8,128)(2,1)} %broadcast_select_fusion.4.left, bf16[384,2304]{1,0:T(8,128)(2,1)} %copy-done.4, f32[768,2304]{1,0:T(8,128)} %shard_map.191.grad, f32[768,2304]{1,0:T(8,128)} %w.4, f32[768,2304]{1,0:T(8,128)} %m.4, f32[768,2304]{1,0:T(8,128)} %v.4), custom_call_target="tpu_custom_call" | custom-call | flops 679477248 | bytes 26247168 | tf_op jit(solution)/shard_map/pallas_call | solution.py:97
  292.2 12.0 %shard_map.193 = (f32[768,2304]{1,0:T(8,128)}, f32[768,2304]{1,0:T(8,128)}, f32[768,2304]{1,0:T(8,128)}) custom-call(bf16[384,768]{1,0:T(8,128)(2,1)} %broadcast_select_fusion.4.left, bf16[384,2304]{1,0:T(8,128)(2,1)} %copy-done.4, f32[768,2304]{1,0:T(8,128)} %shard_map.191.grad, ...), custom_call_target="tpu_custom_call", output_to_operand_aliasing={{0}: (6, {}), {1}: (7, {}), {2}: (8, {})} | custom-call | flops 679477248 | bytes 26247168 | tf_op jit(solution)/shard_map/pallas_call | solution.py:97
  307.2 22.4 %shard_map.194 = (f32[2304,768]{1,0:T(8,128)}, f32[2304,768]{1,0:T(8,128)}, f32[2304,768]{1,0:T(8,128)}) custom-call(bf16[384,2304]{1,0:T(8,128)(2,1)} %copy-done.5, bf16[384,768]{1,0:T(8,128)(2,1)} %broadcast_select_fusion.3.right, f32[2304,768]{1,0:T(8,128)} %shard_map.190.grad, f32[2304,768]{1,0:T(8,128)} %w.5, f32[2304,768]{1,0:T(8,128)} %m.5, f32[2304,768]{1,0:T(8,128)} %v.5), custom_call_target="tpu_custom_call" | custom-call | flops 1358954496 | bytes 51904512 | tf_op jit(solution)/shard_map/pallas_call | solution.py:97
  (314 shorter events, 120.4 us)
Async XLA Ops:
  1.4 24.0 %collective-permute-start.6 = (f32[2,384]{1,0:T(2,128)S(1)}, f32[2,384]{1,0:T(2,128)S(1)}, u32[]{:S(2)}, u32[]{:S(2)}) collective-permute-start(f32[2,384]{1,0:T(2,128)S(1)} %get-tuple-element.196), channel_id=1, source_target_pairs={{0,2},{1,3},{2,0},{3,1},{4,6},{5,7},{6,4},{7,5},{8,10},{9,11},{10,... | collective-permute-start | bytes 9224 | tf_op jit(solution)/shard_map/ppermute | solution.py:259
  5.5 20.0 %collective-permute-start.5 = (f32[2,384]{1,0:T(2,128)S(1)}, f32[2,384]{1,0:T(2,128)S(1)}, u32[]{:S(2)}, u32[]{:S(2)}) collective-permute-start(f32[2,384]{1,0:T(2,128)S(1)} %get-tuple-element.196), channel_id=1, source_target_pairs={{0,1},{1,2},{2,3},{3,0},{4,5},{5,6},{6,7},{7,4},{8,9},{9,10},{10,1... | collective-permute-start | bytes 9224 | tf_op jit(solution)/shard_map/ppermute | solution.py:259
  9.4 41.3 %collective-permute-start.1 = (bf16[384,2304]{1,0:T(8,128)(2,1)}, bf16[384,2304]{1,0:T(8,128)(2,1)}, u32[]{:S(2)}, u32[]{:S(2)}) collective-permute-start(bf16[384,2304]{1,0:T(8,128)(2,1)} %refs_0_.1), channel_id=1, source_target_pairs={{1,2},{2,1},{5,6},{6,5},{9,10},{10,9},{13,14},{14,13},{17,18},{18,... | collective-permute-start | bytes 5308424 | tf_op jit(solution)/shard_map/ppermute | solution.py:146
  11.2 39.8 %collective-permute-start = (bf16[384,2304]{1,0:T(8,128)(2,1)}, bf16[384,2304]{1,0:T(8,128)(2,1)}, u32[]{:S(2)}, u32[]{:S(2)}) collective-permute-start(bf16[384,2304]{1,0:T(8,128)(2,1)} %refs_0_.1), channel_id=1, source_target_pairs={{0,1},{1,0},{2,3},{3,2},{4,5},{5,4},{6,7},{7,6},{8,9},{9,8},{10,11... | collective-permute-start | bytes 5308424 | tf_op jit(solution)/shard_map/ppermute | solution.py:146
  54.4 26.1 %collective-permute-start.9 = (bf16[384,2304]{1,0:T(8,128)(2,1)S(1)}, bf16[384,2304]{1,0:T(8,128)(2,1)S(1)}, u32[]{:S(2)}, u32[]{:S(2)}) collective-permute-start(bf16[384,2304]{1,0:T(8,128)(2,1)S(1)} %copy-done.14), channel_id=1, source_target_pairs={{1,2},{2,1},{5,6},{6,5},{9,10},{10,9},{13,14},{14,13},{17,18},{18,... | collective-permute-start | bytes 5308424 | tf_op jit(solution)/shard_map/ppermute | solution.py:146
  55.2 42.0 %collective-permute-start.8 = (bf16[384,2304]{1,0:T(8,128)(2,1)S(1)}, bf16[384,2304]{1,0:T(8,128)(2,1)S(1)}, u32[]{:S(2)}, u32[]{:S(2)}) collective-permute-start(bf16[384,2304]{1,0:T(8,128)(2,1)S(1)} %copy-done.14), channel_id=1, source_target_pairs={{0,1},{1,0},{2,3},{3,2},{4,5},{5,4},{6,7},{7,6},{8,9},{9,8},{10,11... | collective-permute-start | bytes 5308424 | tf_op jit(solution)/shard_map/ppermute | solution.py:146
  77.0 22.2 %collective-permute-start.26 = (bf16[2,48,768]{2,1,0:T(8,128)(2,1)S(1)}, bf16[2,48,768]{2,1,0:T(8,128)(2,1)S(1)}, u32[]{:S(2)}, u32[]{:S(2)}) collective-permute-start(bf16[2,48,768]{2,1,0:T(8,128)(2,1)S(1)} %pad_maximum_fusion.8), channel_id=1, source_target_pairs={{0,8},{4,12},{8,0},{12,4},{16,24},{20,28},{24,16},{28,20},{1,9},{5... | collective-permute-start | bytes 442376 | tf_op jit(solution)/shard_map/ppermute | solution.py:176
  78.3 20.9 %collective-permute-start.25 = (bf16[2,48,768]{2,1,0:T(8,128)(2,1)S(1)}, bf16[2,48,768]{2,1,0:T(8,128)(2,1)S(1)}, u32[]{:S(2)}, u32[]{:S(2)}) collective-permute-start(bf16[2,48,768]{2,1,0:T(8,128)(2,1)S(1)} %pad_maximum_fusion.8), channel_id=1, source_target_pairs={{0,16},{4,20},{8,24},{12,28},{16,0},{20,4},{24,8},{28,12},{1,17},{... | collective-permute-start | bytes 442376 | tf_op jit(solution)/shard_map/ppermute | solution.py:176
  78.8 20.4 %collective-permute-start.24 = (bf16[2,48,768]{2,1,0:T(8,128)(2,1)S(1)}, bf16[2,48,768]{2,1,0:T(8,128)(2,1)S(1)}, u32[]{:S(2)}, u32[]{:S(2)}) collective-permute-start(bf16[2,48,768]{2,1,0:T(8,128)(2,1)S(1)} %pad_maximum_fusion.8), channel_id=1, source_target_pairs={{0,24},{4,28},{8,16},{12,20},{16,8},{20,12},{24,0},{28,4},{1,25},{... | collective-permute-start | bytes 442376 | tf_op jit(solution)/shard_map/ppermute | solution.py:176
  80.5 57.9 %collective-permute-start.2 = (bf16[384,2304]{1,0:T(8,128)(2,1)}, bf16[384,2304]{1,0:T(8,128)(2,1)}, u32[]{:S(2)}, u32[]{:S(2)}) collective-permute-start(bf16[384,2304]{1,0:T(8,128)(2,1)} %collective-permute-done.1), channel_id=1, source_target_pairs={{1,0},{2,3},{5,4},{6,7},{9,8},{10,11},{13,12},{14,15},{17,16},{18,... | collective-permute-start | bytes 5308424 | tf_op jit(solution)/shard_map/ppermute | solution.py:146
  97.3 42.5 %collective-permute-start.3 = (bf16[384,2304]{1,0:T(8,128)(2,1)}, bf16[384,2304]{1,0:T(8,128)(2,1)}, u32[]{:S(2)}, u32[]{:S(2)}) collective-permute-start(bf16[384,2304]{1,0:T(8,128)(2,1)} %collective-permute-done.refs_1_), channel_id=1, source_target_pairs={{1,2},{2,1},{5,6},{6,5},{9,10},{10,9},{13,14},{14,13},{17,18},{18,... | collective-permute-start | bytes 5308424 | tf_op jit(solution)/shard_map/ppermute | solution.py:146
  106.8 33.8 %collective-permute-start.29 = (f32[48,768]{1,0:T(8,128)}, f32[48,768]{1,0:T(8,128)}, u32[]{:S(2)}, u32[]{:S(2)}) collective-permute-start(f32[48,768]{1,0:T(8,128)} %get-tuple-element.173), channel_id=1, source_target_pairs={{0,8},{4,12},{8,0},{12,4},{16,24},{20,28},{24,16},{28,20},{1,9},{5... | collective-permute-start | bytes 442376 | tf_op jit(solution)/shard_map/ppermute | solution.py:176
  108.1 32.6 %collective-permute-start.31 = (f32[48,768]{1,0:T(8,128)}, f32[48,768]{1,0:T(8,128)}, u32[]{:S(2)}, u32[]{:S(2)}) collective-permute-start(f32[48,768]{1,0:T(8,128)} %get-tuple-element.174), channel_id=1, source_target_pairs={{0,24},{4,28},{8,16},{12,20},{16,8},{20,12},{24,0},{28,4},{1,25},{... | collective-permute-start | bytes 442376 | tf_op jit(solution)/shard_map/ppermute | solution.py:176
  109.8 30.9 %collective-permute-start.30 = (f32[48,768]{1,0:T(8,128)}, f32[48,768]{1,0:T(8,128)}, u32[]{:S(2)}, u32[]{:S(2)}) collective-permute-start(f32[48,768]{1,0:T(8,128)} %get-tuple-element.175), channel_id=1, source_target_pairs={{0,16},{4,20},{8,24},{12,28},{16,0},{20,4},{24,8},{28,12},{1,17},{... | collective-permute-start | bytes 442376 | tf_op jit(solution)/shard_map/ppermute | solution.py:176
  138.4 41.2 %collective-permute-start.10 = (bf16[384,2304]{1,0:T(8,128)(2,1)}, bf16[384,2304]{1,0:T(8,128)(2,1)S(1)}, u32[]{:S(2)}, u32[]{:S(2)}) collective-permute-start(bf16[384,2304]{1,0:T(8,128)(2,1)} %copy-done.15), channel_id=1, source_target_pairs={{1,0},{2,3},{5,4},{6,7},{9,8},{10,11},{13,12},{14,15},{17,16},{18,... | collective-permute-start | bytes 5308424 | tf_op jit(solution)/shard_map/ppermute | solution.py:146
  139.7 41.1 %collective-permute-start.11 = (bf16[384,2304]{1,0:T(8,128)(2,1)}, bf16[384,2304]{1,0:T(8,128)(2,1)S(1)}, u32[]{:S(2)}, u32[]{:S(2)}) collective-permute-start(bf16[384,2304]{1,0:T(8,128)(2,1)} %copy-done.17), channel_id=1, source_target_pairs={{1,2},{2,1},{5,6},{6,5},{9,10},{10,9},{13,14},{14,13},{17,18},{18,... | collective-permute-start | bytes 5308424 | tf_op jit(solution)/shard_map/ppermute | solution.py:146
  153.8 27.1 %collective-permute-start.37 = (f32[48,768]{1,0:T(8,128)S(1)}, f32[48,768]{1,0:T(8,128)S(1)}, u32[]{:S(2)}, u32[]{:S(2)}) collective-permute-start(f32[48,768]{1,0:T(8,128)S(1)} %get-tuple-element.170), channel_id=1, source_target_pairs={{0,8},{4,12},{8,0},{12,4},{16,24},{20,28},{24,16},{28,20},{1,9},{5... | collective-permute-start | bytes 442376 | tf_op jit(solution)/shard_map/ppermute | solution.py:176
  155.4 25.5 %collective-permute-start.39 = (f32[48,768]{1,0:T(8,128)S(1)}, f32[48,768]{1,0:T(8,128)S(1)}, u32[]{:S(2)}, u32[]{:S(2)}) collective-permute-start(f32[48,768]{1,0:T(8,128)S(1)} %get-tuple-element.171), channel_id=1, source_target_pairs={{0,24},{4,28},{8,16},{12,20},{16,8},{20,12},{24,0},{28,4},{1,25},{... | collective-permute-start | bytes 442376 | tf_op jit(solution)/shard_map/ppermute | solution.py:176
  155.9 25.1 %collective-permute-start.38 = (f32[48,768]{1,0:T(8,128)S(1)}, f32[48,768]{1,0:T(8,128)S(1)}, u32[]{:S(2)}, u32[]{:S(2)}) collective-permute-start(f32[48,768]{1,0:T(8,128)S(1)} %get-tuple-element.172), channel_id=1, source_target_pairs={{0,16},{4,20},{8,24},{12,28},{16,0},{20,4},{24,8},{28,12},{1,17},{... | collective-permute-start | bytes 442376 | tf_op jit(solution)/shard_map/ppermute | solution.py:176
  179.6 43.6 %collective-permute-start.4 = (bf16[384,2304]{1,0:T(8,128)(2,1)}, bf16[384,2304]{1,0:T(8,128)(2,1)S(1)}, u32[]{:S(2)}, u32[]{:S(2)}) collective-permute-start(bf16[384,2304]{1,0:T(8,128)(2,1)} %collective-permute-done.3), channel_id=1, source_target_pairs={{1,0},{2,3},{5,4},{6,7},{9,8},{10,11},{13,12},{14,15},{17,16},{18,... | collective-permute-start | bytes 5308424 | tf_op jit(solution)/shard_map/ppermute | solution.py:146
  192.8 30.4 %collective-permute-start.45 = (f32[48,768]{1,0:T(8,128)S(1)}, f32[48,768]{1,0:T(8,128)S(1)}, u32[]{:S(2)}, u32[]{:S(2)}) collective-permute-start(f32[48,768]{1,0:T(8,128)S(1)} %get-tuple-element.167), channel_id=1, source_target_pairs={{0,8},{4,12},{8,0},{12,4},{16,24},{20,28},{24,16},{28,20},{1,9},{5... | collective-permute-start | bytes 442376 | tf_op jit(solution)/shard_map/ppermute | solution.py:176
  194.4 28.9 %collective-permute-start.47 = (f32[48,768]{1,0:T(8,128)S(1)}, f32[48,768]{1,0:T(8,128)S(1)}, u32[]{:S(2)}, u32[]{:S(2)}) collective-permute-start(f32[48,768]{1,0:T(8,128)S(1)} %get-tuple-element.168), channel_id=1, source_target_pairs={{0,24},{4,28},{8,16},{12,20},{16,8},{20,12},{24,0},{28,4},{1,25},{... | collective-permute-start | bytes 442376 | tf_op jit(solution)/shard_map/ppermute | solution.py:176
  194.9 28.4 %collective-permute-start.46 = (f32[48,768]{1,0:T(8,128)S(1)}, f32[48,768]{1,0:T(8,128)S(1)}, u32[]{:S(2)}, u32[]{:S(2)}) collective-permute-start(f32[48,768]{1,0:T(8,128)S(1)} %get-tuple-element.169), channel_id=1, source_target_pairs={{0,16},{4,20},{8,24},{12,28},{16,0},{20,4},{24,8},{28,12},{1,17},{... | collective-permute-start | bytes 442376 | tf_op jit(solution)/shard_map/ppermute | solution.py:176
  196.4 65.4 %collective-permute-start.59 = (bf16[384,2304]{1,0:T(8,128)(2,1)S(1)}, bf16[384,2304]{1,0:T(8,128)(2,1)S(1)}, u32[]{:S(2)}, u32[]{:S(2)}) collective-permute-start(bf16[384,2304]{1,0:T(8,128)(2,1)S(1)} %collective-permute-done.11), channel_id=1, source_target_pairs={{1,0},{2,3},{5,4},{6,7},{9,8},{10,11},{13,12},{14,15},{17,16},{18,... | collective-permute-start | bytes 5308424 | tf_op jit(solution)/shard_map/ppermute | solution.py:146
  (67 other events, 446.7 us)

commit v6 on v5

--- a/solution.py
+++ b/solution.py
@@ -82,37 +82,60 @@
     )(*lefts, *rights)
 
 
-def update_kernel(left, right, grad, w, m, v, *refs):
-    new_w, new_m, new_v = refs[-3:]
-    total = grad[...] + over_rows(left[...], right[...])
-    new_w[...], new_m[...], new_v[...] = adamw(w[...], m[...], v[...], total)
-
-
-def update(left, right, grad, w, m, v, most, part=0, parts=1, so_far=()):
-    rows, height = left.shape
-    width = right.shape[1] // parts
+def update_kernel(shards, *refs):
+    lefts, rights = refs[:shards], refs[shards : 2 * shards]
+    grad, w, m, v = refs[2 * shards : 2 * shards + 4]
+    new_w, new_m, new_v, late = refs[-4:]
+    height = lefts[0].shape[1]
+    block = w.shape[0]
+    step = pl.program_id(0)
+
+    @pl.when(step == 0)
+    def _():
+        span = block_of(height, 768)
+        for at in range(0, height, span):
+            columns = slice(at, at + span)
+            total = over_rows(lefts[0][:, columns], rights[0][...])
+            for left, right in zip(lefts[1:], rights[1:]):
+                total += over_rows(left[:, columns], right[...])
+            late[columns, :] = total
+
+    def some_rows(i, carry):
+        rows = pl.ds(pl.multiple_of(16 * i, 16), 16)
+        late_rows = pl.ds(pl.multiple_of(step * block + 16 * i, 16), 16)
+        new_w[rows, :], new_m[rows, :], new_v[rows, :] = adamw(
+            w[rows, :], m[rows, :], v[rows, :], grad[rows, :] + late[late_rows, :]
+        )
+        return carry
+
+    lax.fori_loop(0, block // 16, some_rows, 0, unroll=4)
+
+
+def update(lefts, rights, grad, w, m, v, most, part=0, parts=1, so_far=()):
+    shards = len(lefts)
+    rows, height = lefts[0].shape
+    width = rights[0].shape[1] // parts
     block = block_of(height, most)
     panel = pl.BlockSpec((block, width), lambda i: (i, part))
     shape = jax.ShapeDtypeStruct(w.shape, jnp.float32)
     return pl.pallas_call(
-        update_kernel,
+        functools.partial(update_kernel, shards),
         grid=(height // block,),
-        in_specs=[
-            pl.BlockSpec((rows, block), lambda i: (0, i)),
-            pl.BlockSpec((rows, width), lambda i: (0, part)),
-        ]
+        in_specs=[pl.BlockSpec((rows, height), lambda i: (0, 0))] * shards
+        + [pl.BlockSpec((rows, width), lambda i: (0, part))] * shards
         + [panel] * 4
         + [pl.BlockSpec(memory_space=pl.ANY)] * len(so_far),
         out_specs=[panel] * 3,
         out_shape=[shape] * 3,
-        input_output_aliases={6 + i: i for i in range(len(so_far))},
+        scratch_shapes=[pltpu.VMEM((height, width), jnp.float32)],
+        input_output_aliases={2 * shards + 4 + i: i for i in range(len(so_far))},
         compiler_params=pltpu.CompilerParams(vmem_limit_bytes=56 * 2**20),
         cost_estimate=pl.CostEstimate(
-            flops=2 * rows * height * width,
-            bytes_accessed=7 * 4 * height * width + 2 * rows * (height + width),
+            flops=2 * shards * rows * height * width,
+            bytes_accessed=7 * 4 * height * width + 2 * shards * rows * (height + width),
             transcendentals=2 * height * width,
         ),
-    )(left, right, grad, w, m, v, *so_far)
+    )(*lefts, *rights, grad, w, m, v, *so_far)
 
 
 def link_pairs(n, first, step):
@@ -290,7 +313,7 @@
         def run():
             nonlocal outs_out
             outs_out = update(
-                acts[-1], dys[-1], grad_out, w_out, m_out, v_out, 128, part, parts, outs_out
+                acts[-2:], dys[-2:], grad_out, w_out, m_out, v_out, 128, part, parts, outs_out
             )
             return outs_out
 
@@ -309,10 +332,12 @@
         if slot > 1:
             last = (last, tokens_came[slot])
             beside, latest = None, None
+            if slot == n - 2:
+                grad_in = grad_sum(token_slots[:slot], dpres, 256)
+                grad_out = grad_sum(acts, dys, 128)
+                beside = [None, (grad_in, grad_out)]
             if slot == n - 1:
-                grad_in = grad_sum(token_slots[:-1], dpres, 256)
-                grad_out = grad_sum(acts, dys, 128)
-                beside, latest = [None, (grad_in, grad_out)], [out_grads_came[slot]]
+                latest = [out_grads_came[slot]]
             pre = row_sum(after(pre_of(token_slots[slot]), last), "row", beside)
             last = row_gather(square(pre), "row", latest)
             acts.append(last)
@@ -328,7 +353,7 @@
     dpres.append(row_gather(chain(pre, back), "row", work))
     while work:
         work.pop(0)()
-    outs_in = update(token_slots[-1], dpres[-1], grad_in, w_in, m_in, v_in, 256)
+    outs_in = update(token_slots[-2:], dpres[-2:], grad_in, w_in, m_in, v_in, 256)
     return (*outs_in, *outs_out)
 
 

time: 330 us -> 334 us (1.012)
  Pallas kernels: 65.4 us -> 71.7 us
    ppermute x10, waiting for transfers between devices: 91.7 us -> 79.5 us  [line_gather(): arrived[links, step] = lax.ppermute(came[1 - links, step - 1], axis, pairs)]
    ppermute x56, waiting for transfers between devices: 49.1 us -> 59.5 us  [exchange(): lax.ppermute(part, axis, [(i, i ^ mask) for i in range(lax.axis_size(axis...]
    pallas_call x3, Pallas kernels: 46.5 us -> 55.3 us  [update(): pl.pallas_call(functools.partial(update_kernel, shards), grid=(height //...]
  transfers between devices with their start and end apart: 69 -> 69, of which waited for: 31 -> 34; matrix products, arithmetic and copies ran while one was open for 9% -> 9% of each run, Pallas kernels for 13% -> 13%
where the time goes in v6:
time: 334 us; the launch traced here: 333 us
  waiting for transfers between devices  139 us (42%)
  starting transfers between devices  74.6 us (22%)
  Pallas kernels  71.7 us (21%)
  other arithmetic  21.5 us (6%)
  matrix products  13.9 us (4%)
  local copies, waits for them, and re-layouts  8.73 us (3%)
  between operations  4.02 us (1%)
    ppermute x10, waiting for transfers between devices, line_gather(): arrived[links, step] = lax.ppermute(came[1 - links, step - 1], axis, pairs)  79.5 us
    ppermute x56, waiting for transfers between devices, exchange(): lax.ppermute(part, axis, [(i, i ^ mask) for i in range(lax.axis_size(axis...  59.5 us
    pallas_call x3, Pallas kernels, update(): pl.pallas_call(functools.partial(update_kernel, shards), grid=(height //...  55.3 us
    ppermute x56, starting transfers between devices, exchange(): lax.ppermute(part, axis, [(i, i ^ mask) for i in range(lax.axis_size(axis...  52.8 us
    pallas_call x2, Pallas kernels, grad_sum(): pl.pallas_call(functools.partial(grad_kernel, parts), grid=(height // blo...  16.4 us
    ppermute x10, starting transfers between devices, line_gather(): arrived[links, step] = lax.ppermute(came[1 - links, step - 1], axis, pairs)  13.8 us
    ppermute x3, starting transfers between devices, on_device(): lax.ppermute(codes, 'col', [(i, (i + shift) % n) for i in range(n)])  7.93 us
    dot_general x4, matrix products, pre_of(): return jnp.dot(shard, w_in16, preferred_element_type=jnp.float32)  7.63 us
  transfers between devices with their start and end apart: 69, of which 34 were waited for; matrix products, arithmetic and copies ran while one was open for 9% of the time, Pallas kernels for 13%

profile of v6, /device:TPU:0, one launch (start us, length us, event | category | flops | bytes accessed | tf_op | source)
XLA Modules:
  0.0 333.3 jit_solution(18377607963203913417)
XLA Ops:
  1.4 4.1 %collective-permute-start.6 = (f32[2,384]{1,0:T(2,128)S(1)}, f32[2,384]{1,0:T(2,128)S(1)}, u32[]{:S(2)}, u32[]{:S(2)}) collective-permute-start(f32[2,384]{1,0:T(2,128)S(1)} %get-tuple-element.196), channel_id=1, source_target_pairs={{0,2},{1,3},{2,0},{3,1},{4,6},{5,7},{6,4},{7,5},{8,10},{9,11},{10,... | collective-permute-start | bytes 9224 | tf_op jit(solution)/shard_map/ppermute | solution.py:282
  7.1 2.2 collective-permute-start.7
  13.1 3.5 %convert_element_type.82 = bf16[2304,768]{1,0:T(8,128)(2,1)S(1)} convert(f32[2304,768]{1,0:T(8,128)} %refs_5_.5) | non-fusion elementwise | flops 1769472 | bytes 10616832 | tf_op jit(solution)/shard_map/convert_element_type | solution.py:289
  18.2 2.1 convert_element_type.83
  32.4 3.2 collective-permute-done.13
  35.5 3.4 %collective-permute-done.15 = f32[48,768]{1,0:T(8,128)S(1)} collective-permute-done((f32[48,768]{1,0:T(8,128)S(1)}, f32[48,768]{1,0:T(8,128)S(1)}, u32[]{:S(2)}, u32[]{:S(2)}) %collective-permute-start.15) | collective-permute-done | bytes 147488 | tf_op jit(solution)/shard_map/ppermute | solution.py:199
  51.1 3.0 convolution_bitcast_fusion
  55.2 3.2 collective-permute-start.8
  62.3 6.4 %collective-permute-done.21 = f32[2,48,768]{2,1,0:T(8,128)S(1)} collective-permute-done((f32[2,48,768]{2,1,0:T(8,128)S(1)}, f32[2,48,768]{2,1,0:T(8,128)S(1)}, u32[]{:S(2)}, u32[]{:S(2)}) %collective-permute-start.21) | collective-permute-done | bytes 294944 | tf_op jit(solution)/shard_map/ppermute | solution.py:199
  68.7 6.1 %collective-permute-done.23 = f32[2,48,768]{2,1,0:T(8,128)S(1)} collective-permute-done((f32[2,48,768]{2,1,0:T(8,128)S(1)}, f32[2,48,768]{2,1,0:T(8,128)S(1)}, u32[]{:S(2)}, u32[]{:S(2)}) %collective-permute-start.23) | collective-permute-done | bytes 294944 | tf_op jit(solution)/shard_map/ppermute | solution.py:199
  81.8 15.4 %collective-permute-done.8 = bf16[384,2304]{1,0:T(8,128)(2,1)S(1)} collective-permute-done((bf16[384,2304]{1,0:T(8,128)(2,1)S(1)}, bf16[384,2304]{1,0:T(8,128)(2,1)S(1)}, u32[]{:S(2)}, u32[]{:S(2)}) %collective-permute-start.8) | collective-permute-done | bytes 1769504 | tf_op jit(solution)/shard_map/ppermute | solution.py:169
  110.4 28.1 %collective-permute-done.2 = bf16[384,2304]{1,0:T(8,128)(2,1)} collective-permute-done((bf16[384,2304]{1,0:T(8,128)(2,1)}, bf16[384,2304]{1,0:T(8,128)(2,1)}, u32[]{:S(2)}, u32[]{:S(2)}) %collective-permute-start.2) | collective-permute-done | bytes 1769504 | tf_op jit(solution)/shard_map/ppermute | solution.py:169
  147.4 2.0 collective-permute-done.32
  153.4 28.7 %collective-permute-done.10 = bf16[384,2304]{1,0:T(8,128)(2,1)S(1)} collective-permute-done((bf16[384,2304]{1,0:T(8,128)(2,1)}, bf16[384,2304]{1,0:T(8,128)(2,1)S(1)}, u32[]{:S(2)}, u32[]{:S(2)}) %collective-permute-start.10) | collective-permute-done | bytes 1769504 | tf_op jit(solution)/shard_map/ppermute | solution.py:169
  182.2 6.5 %shard_map.191.refs_4_ = f32[768,2304]{1,0:T(8,128)} custom-call(bf16[384,768]{1,0:T(8,128)(2,1)S(1)} %copy-done, bf16[384,768]{1,0:T(8,128)(2,1)S(1)} %get-tuple-element.156.refs_1_, bf16[384,2304]{1,0:T(8,128)(2,1)S(1)} %multiply_convert_fusion.1.refs_2_, bf16[384,2304]{1,0:T(8,128)(2,1)S(1)} %multiply_convert_fusion.2.refs_3_), custom_call_target="tpu_custom_call" | custom-call | flops 2717908992 | bytes 11796480 | tf_op jit(solution)/shard_map/pallas_call | solution.py:69
  192.4 9.9 %shard_map.190.refs_4_ = f32[2304,768]{1,0:T(8,128)} custom-call(bf16[384,2304]{1,0:T(8,128)(2,1)S(1)} %copy-done.2, bf16[384,2304]{1,0:T(8,128)(2,1)} %collective-permute-done.refs_1_, bf16[384,768]{1,0:T(8,128)(2,1)S(1)} %get-tuple-element.157.refs_2_, bf16[384,768]{1,0:T(8,128)(2,1)S(1)} %broadcast_select_fusion.7.refs_3_), custom_call_target="tpu_custom_call" | custom-call | flops 2717908992 | bytes 11796480 | tf_op jit(solution)/shard_map/pallas_call | solution.py:69
  207.3 2.4 collective-permute-done.40
  221.7 2.7 collective-permute-done.47
  243.0 3.2 collective-permute-done.53
  246.1 2.7 collective-permute-done.55
  253.8 6.8 %collective-permute-done.59 = bf16[384,2304]{1,0:T(8,128)(2,1)S(1)} collective-permute-done((bf16[384,2304]{1,0:T(8,128)(2,1)S(1)}, bf16[384,2304]{1,0:T(8,128)(2,1)S(1)}, u32[]{:S(2)}, u32[]{:S(2)}) %collective-permute-start.59) | collective-permute-done | bytes 1769504 | tf_op jit(solution)/shard_map/ppermute | solution.py:169
  271.4 14.3 %shard_map.192 = (f32[768,2304]{1,0:T(8,128)}, f32[768,2304]{1,0:T(8,128)}, f32[768,2304]{1,0:T(8,128)}) custom-call(bf16[384,768]{1,0:T(8,128)(2,1)} %broadcast_select_fusion.6.refs_0_, bf16[384,768]{1,0:T(8,128)(2,1)} %broadcast_select_fusion.4.refs_1_, bf16[384,2304]{1,0:T(8,128)(2,1)} %copy-done.4, bf16[384,2304]{1,0:T(8,128)(2,1)} %copy-done.5, ...), custom_call_target="tpu_custom_call" | custom-call | flops 1358954496 | bytes 27721728 | tf_op jit(solution)/shard_map/pallas_call | solution.py:121
  289.4 14.3 %shard_map.193 = (f32[768,2304]{1,0:T(8,128)}, f32[768,2304]{1,0:T(8,128)}, f32[768,2304]{1,0:T(8,128)}) custom-call(bf16[384,768]{1,0:T(8,128)(2,1)} %broadcast_select_fusion.6.refs_0_, bf16[384,768]{1,0:T(8,128)(2,1)} %broadcast_select_fusion.4.refs_1_, bf16[384,2304]{1,0:T(8,128)(2,1)} %copy-done.4, ...), custom_call_target="tpu_custom_call", output_to_operand_aliasing={{0}: (8, {}), {1}: (9, {}), {2}: (10, {})} | custom-call | flops 1358954496 | bytes 27721728 | tf_op jit(solution)/shard_map/pallas_call | solution.py:121
  306.6 26.7 %shard_map.194 = (f32[2304,768]{1,0:T(8,128)}, f32[2304,768]{1,0:T(8,128)}, f32[2304,768]{1,0:T(8,128)}) custom-call(bf16[384,2304]{1,0:T(8,128)(2,1)} %copy-done.6, bf16[384,2304]{1,0:T(8,128)(2,1)} %copy-done.7, bf16[384,768]{1,0:T(8,128)(2,1)} %broadcast_select_fusion.5.refs_2_, bf16[384,768]{1,0:T(8,128)(2,1)} %broadcast_select_fusion.3.refs_3_, ...), custom_call_target="tpu_custom_call" | custom-call | flops 2717908992 | bytes 54263808 | tf_op jit(solution)/shard_map/pallas_call | solution.py:121
  (314 shorter events, 128.3 us)
Async XLA Ops:
  1.4 24.0 %collective-permute-start.6 = (f32[2,384]{1,0:T(2,128)S(1)}, f32[2,384]{1,0:T(2,128)S(1)}, u32[]{:S(2)}, u32[]{:S(2)}) collective-permute-start(f32[2,384]{1,0:T(2,128)S(1)} %get-tuple-element.196), channel_id=1, source_target_pairs={{0,2},{1,3},{2,0},{3,1},{4,6},{5,7},{6,4},{7,5},{8,10},{9,11},{10,... | collective-permute-start | bytes 9224 | tf_op jit(solution)/shard_map/ppermute | solution.py:282
  5.5 20.0 %collective-permute-start.5 = (f32[2,384]{1,0:T(2,128)S(1)}, f32[2,384]{1,0:T(2,128)S(1)}, u32[]{:S(2)}, u32[]{:S(2)}) collective-permute-start(f32[2,384]{1,0:T(2,128)S(1)} %get-tuple-element.196), channel_id=1, source_target_pairs={{0,1},{1,2},{2,3},{3,0},{4,5},{5,6},{6,7},{7,4},{8,9},{9,10},{10,1... | collective-permute-start | bytes 9224 | tf_op jit(solution)/shard_map/ppermute | solution.py:282
  7.1 18.4 %collective-permute-start.7 = (f32[2,384]{1,0:T(2,128)S(1)}, f32[2,384]{1,0:T(2,128)S(1)}, u32[]{:S(2)}, u32[]{:S(2)}) collective-permute-start(f32[2,384]{1,0:T(2,128)S(1)} %get-tuple-element.196), channel_id=1, source_target_pairs={{0,3},{1,0},{2,1},{3,2},{4,7},{5,4},{6,5},{7,6},{8,11},{9,8},{10,9... | collective-permute-start | bytes 9224 | tf_op jit(solution)/shard_map/ppermute | solution.py:282
  9.4 41.3 %collective-permute-start.1 = (bf16[384,2304]{1,0:T(8,128)(2,1)}, bf16[384,2304]{1,0:T(8,128)(2,1)}, u32[]{:S(2)}, u32[]{:S(2)}) collective-permute-start(bf16[384,2304]{1,0:T(8,128)(2,1)} %refs_0_.1), channel_id=1, source_target_pairs={{1,2},{2,1},{5,6},{6,5},{9,10},{10,9},{13,14},{14,13},{17,18},{18,... | collective-permute-start | bytes 5308424 | tf_op jit(solution)/shard_map/ppermute | solution.py:169
  11.2 39.8 %collective-permute-start = (bf16[384,2304]{1,0:T(8,128)(2,1)}, bf16[384,2304]{1,0:T(8,128)(2,1)}, u32[]{:S(2)}, u32[]{:S(2)}) collective-permute-start(bf16[384,2304]{1,0:T(8,128)(2,1)} %refs_0_.1), channel_id=1, source_target_pairs={{0,1},{1,0},{2,3},{3,2},{4,5},{5,4},{6,7},{7,6},{8,9},{9,8},{10,11... | collective-permute-start | bytes 5308424 | tf_op jit(solution)/shard_map/ppermute | solution.py:169
  54.5 26.1 %collective-permute-start.9 = (bf16[384,2304]{1,0:T(8,128)(2,1)S(1)}, bf16[384,2304]{1,0:T(8,128)(2,1)S(1)}, u32[]{:S(2)}, u32[]{:S(2)}) collective-permute-start(bf16[384,2304]{1,0:T(8,128)(2,1)S(1)} %copy-done.16), channel_id=1, source_target_pairs={{1,2},{2,1},{5,6},{6,5},{9,10},{10,9},{13,14},{14,13},{17,18},{18,... | collective-permute-start | bytes 5308424 | tf_op jit(solution)/shard_map/ppermute | solution.py:169
  55.2 42.0 %collective-permute-start.8 = (bf16[384,2304]{1,0:T(8,128)(2,1)S(1)}, bf16[384,2304]{1,0:T(8,128)(2,1)S(1)}, u32[]{:S(2)}, u32[]{:S(2)}) collective-permute-start(bf16[384,2304]{1,0:T(8,128)(2,1)S(1)} %copy-done.16), channel_id=1, source_target_pairs={{0,1},{1,0},{2,3},{3,2},{4,5},{5,4},{6,7},{7,6},{8,9},{9,8},{10,11... | collective-permute-start | bytes 5308424 | tf_op jit(solution)/shard_map/ppermute | solution.py:169
  77.0 22.2 %collective-permute-start.26 = (bf16[2,48,768]{2,1,0:T(8,128)(2,1)S(1)}, bf16[2,48,768]{2,1,0:T(8,128)(2,1)S(1)}, u32[]{:S(2)}, u32[]{:S(2)}) collective-permute-start(bf16[2,48,768]{2,1,0:T(8,128)(2,1)S(1)} %pad_maximum_fusion.8), channel_id=1, source_target_pairs={{0,8},{4,12},{8,0},{12,4},{16,24},{20,28},{24,16},{28,20},{1,9},{5... | collective-permute-start | bytes 442376 | tf_op jit(solution)/shard_map/ppermute | solution.py:199
  78.3 20.9 %collective-permute-start.25 = (bf16[2,48,768]{2,1,0:T(8,128)(2,1)S(1)}, bf16[2,48,768]{2,1,0:T(8,128)(2,1)S(1)}, u32[]{:S(2)}, u32[]{:S(2)}) collective-permute-start(bf16[2,48,768]{2,1,0:T(8,128)(2,1)S(1)} %pad_maximum_fusion.8), channel_id=1, source_target_pairs={{0,16},{4,20},{8,24},{12,28},{16,0},{20,4},{24,8},{28,12},{1,17},{... | collective-permute-start | bytes 442376 | tf_op jit(solution)/shard_map/ppermute | solution.py:199
  78.8 20.4 %collective-permute-start.24 = (bf16[2,48,768]{2,1,0:T(8,128)(2,1)S(1)}, bf16[2,48,768]{2,1,0:T(8,128)(2,1)S(1)}, u32[]{:S(2)}, u32[]{:S(2)}) collective-permute-start(bf16[2,48,768]{2,1,0:T(8,128)(2,1)S(1)} %pad_maximum_fusion.8), channel_id=1, source_target_pairs={{0,24},{4,28},{8,16},{12,20},{16,8},{20,12},{24,0},{28,4},{1,25},{... | collective-permute-start | bytes 442376 | tf_op jit(solution)/shard_map/ppermute | solution.py:199
  80.6 57.9 %collective-permute-start.2 = (bf16[384,2304]{1,0:T(8,128)(2,1)}, bf16[384,2304]{1,0:T(8,128)(2,1)}, u32[]{:S(2)}, u32[]{:S(2)}) collective-permute-start(bf16[384,2304]{1,0:T(8,128)(2,1)} %collective-permute-done.1), channel_id=1, source_target_pairs={{1,0},{2,3},{5,4},{6,7},{9,8},{10,11},{13,12},{14,15},{17,16},{18,... | collective-permute-start | bytes 5308424 | tf_op jit(solution)/shard_map/ppermute | solution.py:169
  97.3 42.5 %collective-permute-start.3 = (bf16[384,2304]{1,0:T(8,128)(2,1)}, bf16[384,2304]{1,0:T(8,128)(2,1)}, u32[]{:S(2)}, u32[]{:S(2)}) collective-permute-start(bf16[384,2304]{1,0:T(8,128)(2,1)} %collective-permute-done.refs_1_), channel_id=1, source_target_pairs={{1,2},{2,1},{5,6},{6,5},{9,10},{10,9},{13,14},{14,13},{17,18},{18,... | collective-permute-start | bytes 5308424 | tf_op jit(solution)/shard_map/ppermute | solution.py:169
  106.8 33.9 %collective-permute-start.29 = (f32[48,768]{1,0:T(8,128)}, f32[48,768]{1,0:T(8,128)}, u32[]{:S(2)}, u32[]{:S(2)}) collective-permute-start(f32[48,768]{1,0:T(8,128)} %get-tuple-element.173), channel_id=1, source_target_pairs={{0,8},{4,12},{8,0},{12,4},{16,24},{20,28},{24,16},{28,20},{1,9},{5... | collective-permute-start | bytes 442376 | tf_op jit(solution)/shard_map/ppermute | solution.py:199
  108.1 32.7 %collective-permute-start.31 = (f32[48,768]{1,0:T(8,128)}, f32[48,768]{1,0:T(8,128)}, u32[]{:S(2)}, u32[]{:S(2)}) collective-permute-start(f32[48,768]{1,0:T(8,128)} %get-tuple-element.174), channel_id=1, source_target_pairs={{0,24},{4,28},{8,16},{12,20},{16,8},{20,12},{24,0},{28,4},{1,25},{... | collective-permute-start | bytes 442376 | tf_op jit(solution)/shard_map/ppermute | solution.py:199
  109.8 30.9 %collective-permute-start.30 = (f32[48,768]{1,0:T(8,128)}, f32[48,768]{1,0:T(8,128)}, u32[]{:S(2)}, u32[]{:S(2)}) collective-permute-start(f32[48,768]{1,0:T(8,128)} %get-tuple-element.175), channel_id=1, source_target_pairs={{0,16},{4,20},{8,24},{12,28},{16,0},{20,4},{24,8},{28,12},{1,17},{... | collective-permute-start | bytes 442376 | tf_op jit(solution)/shard_map/ppermute | solution.py:199
  138.5 43.6 %collective-permute-start.10 = (bf16[384,2304]{1,0:T(8,128)(2,1)}, bf16[384,2304]{1,0:T(8,128)(2,1)S(1)}, u32[]{:S(2)}, u32[]{:S(2)}) collective-permute-start(bf16[384,2304]{1,0:T(8,128)(2,1)} %copy-done.17), channel_id=1, source_target_pairs={{1,0},{2,3},{5,4},{6,7},{9,8},{10,11},{13,12},{14,15},{17,16},{18,... | collective-permute-start | bytes 5308424 | tf_op jit(solution)/shard_map/ppermute | solution.py:169
  139.8 42.3 %collective-permute-start.11 = (bf16[384,2304]{1,0:T(8,128)(2,1)}, bf16[384,2304]{1,0:T(8,128)(2,1)S(1)}, u32[]{:S(2)}, u32[]{:S(2)}) collective-permute-start(bf16[384,2304]{1,0:T(8,128)(2,1)} %copy-done.19), channel_id=1, source_target_pairs={{1,2},{2,1},{5,6},{6,5},{9,10},{10,9},{13,14},{14,13},{17,18},{18,... | collective-permute-start | bytes 5308424 | tf_op jit(solution)/shard_map/ppermute | solution.py:169
  151.5 37.2 %collective-permute-start.36 = (f32[192,768]{1,0:T(8,128)S(1)}, f32[192,768]{1,0:T(8,128)S(1)}, u32[]{:S(2)}, u32[]{:S(2)}) collective-permute-start(f32[192,768]{1,0:T(8,128)S(1)} %constant_dynamic-slice_fusion.16), channel_id=1, source_target_pairs={{0,4},{4,0},{8,12},{12,8},{16,20},{20,16},{24,28},{28,24},{1,5},{5... | collective-permute-start | bytes 1769480 | tf_op jit(solution)/shard_map/ppermute | solution.py:199
  152.1 67.8 %collective-permute-start.4 = (bf16[384,2304]{1,0:T(8,128)(2,1)}, bf16[384,2304]{1,0:T(8,128)(2,1)S(1)}, u32[]{:S(2)}, u32[]{:S(2)}) collective-permute-start(bf16[384,2304]{1,0:T(8,128)(2,1)} %collective-permute-done.3), channel_id=1, source_target_pairs={{1,0},{2,3},{5,4},{6,7},{9,8},{10,11},{13,12},{14,15},{17,16},{18,... | collective-permute-start | bytes 5308424 | tf_op jit(solution)/shard_map/ppermute | solution.py:169
  218.6 42.0 %collective-permute-start.59 = (bf16[384,2304]{1,0:T(8,128)(2,1)S(1)}, bf16[384,2304]{1,0:T(8,128)(2,1)S(1)}, u32[]{:S(2)}, u32[]{:S(2)}) collective-permute-start(bf16[384,2304]{1,0:T(8,128)(2,1)S(1)} %collective-permute-done.11), channel_id=1, source_target_pairs={{1,0},{2,3},{5,4},{6,7},{9,8},{10,11},{13,12},{14,15},{17,16},{18,... | collective-permute-start | bytes 5308424 | tf_op jit(solution)/shard_map/ppermute | solution.py:169
  267.9 17.8 %collective-permute-start.64 = (f32[48,768]{1,0:T(8,128)S(1)}, f32[48,768]{1,0:T(8,128)S(1)}, u32[]{:S(2)}, u32[]{:S(2)}) collective-permute-start(f32[48,768]{1,0:T(8,128)S(1)} %get-tuple-element.161), channel_id=1, source_target_pairs={{0,24},{4,28},{8,16},{12,20},{16,8},{20,12},{24,0},{28,4},{1,25},{... | collective-permute-start | bytes 442376 | tf_op jit(solution)/shard_map/ppermute | solution.py:199
  269.3 16.4 %collective-permute-start.63 = (f32[48,768]{1,0:T(8,128)S(1)}, f32[48,768]{1,0:T(8,128)S(1)}, u32[]{:S(2)}, u32[]{:S(2)}) collective-permute-start(f32[48,768]{1,0:T(8,128)S(1)} %get-tuple-element.162), channel_id=1, source_target_pairs={{0,16},{4,20},{8,24},{12,28},{16,0},{20,4},{24,8},{28,12},{1,17},{... | collective-permute-start | bytes 442376 | tf_op jit(solution)/shard_map/ppermute | solution.py:199
  285.8 17.9 %collective-permute-start.67 = (bf16[48,768]{1,0:T(8,128)(2,1)S(1)}, bf16[48,768]{1,0:T(8,128)(2,1)S(1)}, u32[]{:S(2)}, u32[]{:S(2)}) collective-permute-start(bf16[48,768]{1,0:T(8,128)(2,1)S(1)} %multiply_convert_fusion.4), channel_id=1, source_target_pairs={{0,24},{4,28},{8,16},{12,20},{16,8},{20,12},{24,0},{28,4},{1,25},{... | collective-permute-start | bytes 221192 | tf_op jit(solution)/shard_map/ppermute | solution.py:199
  287.3 16.4 %collective-permute-start.66 = (bf16[48,768]{1,0:T(8,128)(2,1)S(1)}, bf16[48,768]{1,0:T(8,128)(2,1)S(1)}, u32[]{:S(2)}, u32[]{:S(2)}) collective-permute-start(bf16[48,768]{1,0:T(8,128)(2,1)S(1)} %multiply_convert_fusion.4), channel_id=1, source_target_pairs={{0,16},{4,20},{8,24},{12,28},{16,0},{20,4},{24,8},{28,12},{1,17},{... | collective-permute-start | bytes 221192 | tf_op jit(solution)/shard_map/ppermute | solution.py:199
  (67 other events, 458.3 us)

commit v7 on v5

--- a/solution.py
+++ b/solution.py
@@ -53,33 +53,67 @@
     return block
 
 
-def grad_kernel(parts, *refs):
-    lefts, rights, out = refs[:parts], refs[parts : 2 * parts], refs[2 * parts]
-    total = over_rows(lefts[0][...], rights[0][...])
-    for left, right in zip(lefts[1:], rights[1:]):
+def fetch_kernel(parts, *refs):
+    count = (len(refs) - 1) // (parts + 1)
+    sources, targets, sems = refs[:count], refs[count:-1], refs[-1]
+    copies = []
+    for i, target in enumerate(targets):
+        part, source = divmod(i, len(sources))
+        width = target.shape[1]
+        columns = sources[source].at[:, pl.ds(part * width, width)]
+        copies.append(pltpu.make_async_copy(columns, target, sems.at[i]))
+    for copy in copies:
+        copy.start()
+    for copy in copies:
+        copy.wait()
+
+
+def fetch(arrays, parts):
+    shapes = [pltpu.VMEM((x.shape[0], x.shape[1] // parts), x.dtype) for x in arrays] * parts
+    fetched = pl.pallas_call(
+        functools.partial(fetch_kernel, parts),
+        in_specs=[pl.BlockSpec(memory_space=pl.ANY)] * len(arrays),
+        out_specs=[pl.BlockSpec(memory_space=pltpu.VMEM)] * len(shapes),
+        out_shape=shapes,
+        scratch_shapes=[pltpu.SemaphoreType.DMA((len(shapes),))],
+        compiler_params=pltpu.CompilerParams(vmem_limit_bytes=26 * 2**20),
+        cost_estimate=pl.CostEstimate(
+            flops=0, bytes_accessed=4 * sum(x.size for x in arrays), transcendentals=0
+        ),
+    )(*arrays)
+    return [fetched[i : i + len(arrays)] for i in range(0, len(shapes), len(arrays))]
+
+
+def grad_kernel(pieces, *refs):
+    lefts, rights, out = refs[:pieces], refs[pieces : 2 * pieces], refs[-1]
+    total = refs[2 * pieces][...] if len(refs) > 2 * pieces + 1 else 0.0
+    for left, right in zip(lefts, rights):
         total += over_rows(left[...], right[...])
     out[...] = total
 
 
-def grad_sum(lefts, rights, most):
+def grad_sum(lefts, rights, most, so_far=()):
     rows, height = lefts[0].shape
     width = rights[0].shape[1]
-    parts = len(lefts)
+    pieces = len(lefts)
     block = block_of(height, most)
+    panel = pl.BlockSpec((block, width), lambda i: (i, 0))
     return pl.pallas_call(
-        functools.partial(grad_kernel, parts),
+        functools.partial(grad_kernel, pieces),
         grid=(height // block,),
-        in_specs=[pl.BlockSpec((rows, block), lambda i: (0, i))] * parts
-        + [pl.BlockSpec((rows, width), lambda i: (0, 0))] * parts,
-        out_specs=pl.BlockSpec((block, width), lambda i: (i, 0)),
-        out_shape=jax.ShapeDtypeStruct((height, width), jnp.float32),
-        compiler_params=pltpu.CompilerParams(vmem_limit_bytes=44 * 2**20),
+        in_specs=[pl.BlockSpec((rows, block), lambda i: (0, i))] * pieces
+        + [pl.BlockSpec((rows, width), lambda i: (0, 0))] * pieces
+        + [panel] * len(so_far),
+        out_specs=panel,
+        out_shape=pltpu.VMEM((height, width), jnp.float32),
+        input_output_aliases={2 * pieces + i: i for i in range(len(so_far))},
+        compiler_params=pltpu.CompilerParams(vmem_limit_bytes=20 * 2**20),
         cost_estimate=pl.CostEstimate(
-            flops=2 * parts * rows * height * width,
-            bytes_accessed=4 * height * width + 2 * parts * rows * (height + width),
+            flops=2 * pieces * rows * height * width,
+            bytes_accessed=4 * height * width + 2 * pieces * rows * (height + width),
             transcendentals=0,
         ),
-    )(*lefts, *rights)
+    )(*lefts, *rights, *so_far)
 
 
 def update_kernel(left, right, grad, w, m, v, *refs):
@@ -88,25 +122,27 @@
     new_w[...], new_m[...], new_v[...] = adamw(w[...], m[...], v[...], total)
 
 
-def update(left, right, grad, w, m, v, most, part=0, parts=1, so_far=()):
+def update(left, right, grad, w, m, v, most, limit, part=0, parts=1, so_far=()):
     rows, height = left.shape
     width = right.shape[1] // parts
     block = block_of(height, most)
     panel = pl.BlockSpec((block, width), lambda i: (i, part))
-    shape = jax.ShapeDtypeStruct(w.shape, jnp.float32)
+    own = pl.BlockSpec((block, width), lambda i: (i, 0))
+    shape = jax.ShapeDtypeStruct((height, right.shape[1]), jnp.float32)
     return pl.pallas_call(
         update_kernel,
         grid=(height // block,),
         in_specs=[
             pl.BlockSpec((rows, block), lambda i: (0, i)),
             pl.BlockSpec((rows, width), lambda i: (0, part)),
+            panel,
         ]
-        + [panel] * 4
+        + [own] * 3
         + [pl.BlockSpec(memory_space=pl.ANY)] * len(so_far),
         out_specs=[panel] * 3,
         out_shape=[shape] * 3,
         input_output_aliases={6 + i: i for i in range(len(so_far))},
-        compiler_params=pltpu.CompilerParams(vmem_limit_bytes=56 * 2**20),
+        compiler_params=pltpu.CompilerParams(vmem_limit_bytes=limit * 2**20),
         cost_estimate=pl.CostEstimate(
             flops=2 * rows * height * width,
             bytes_accessed=7 * 4 * height * width + 2 * rows * (height + width),
@@ -290,7 +326,7 @@
         def run():
             nonlocal outs_out
             outs_out = update(
-                acts[-1], dys[-1], grad_out, w_out, m_out, v_out, 128, part, parts, outs_out
+                acts[-1], dys[-1], grad_out, *state_out[part], 128, 20, part, parts, outs_out
             )
             return outs_out
 
@@ -309,9 +345,14 @@
         if slot > 1:
             last = (last, tokens_came[slot])
             beside, latest = None, None
+            if slot == n - 2:
+                grad_in = grad_sum(token_slots[:slot], dpres, 256)
+                grad_out = grad_sum(acts, dys, 128)
+                state_out = fetch((w_out, m_out, v_out), parts)
+                beside = [None, (grad_in, grad_out, state_out)]
             if slot == n - 1:
-                grad_in = grad_sum(token_slots[:-1], dpres, 256)
-                grad_out = grad_sum(acts, dys, 128)
+                grad_in = grad_sum(token_slots[slot - 1 : slot], dpres[-1:], 256, (grad_in,))
+                grad_out = grad_sum(acts[-1:], dys[-1:], 128, (grad_out,))
                 beside, latest = [None, (grad_in, grad_out)], [out_grads_came[slot]]
             pre = row_sum(after(pre_of(token_slots[slot]), last), "row", beside)
             last = row_gather(square(pre), "row", latest)
@@ -328,7 +369,7 @@
     dpres.append(row_gather(chain(pre, back), "row", work))
     while work:
         work.pop(0)()
-    outs_in = update(token_slots[-1], dpres[-1], grad_in, w_in, m_in, v_in, 256)
+    outs_in = update(token_slots[-1], dpres[-1], grad_in, w_in, m_in, v_in, 256, 42)
     return (*outs_in, *outs_out)
 
 

time: 330 us -> 308 us (0.933)
  waiting for transfers between devices: 141 us -> 120 us
  local copies, waits for them, and re-layouts: 9.76 us -> 16.6 us
  Pallas kernels: 65.4 us -> 59.3 us
    ppermute x10, waiting for transfers between devices: 91.7 us -> 67.5 us  [line_gather(): arrived[links, step] = lax.ppermute(came[1 - links, step - 1], axis, pairs)]
    pallas_call x3, Pallas kernels: 46.5 us -> 33.2 us  [update(): pl.pallas_call(update_kernel, grid=(height // block,), in_specs=[pl.Block...]
    pallas_call x2 -> x5, Pallas kernels: 18.9 us -> 26.1 us  [the longest x4 20.7 us: grad_sum(): pl.pallas_call(functools.partial(grad_kernel, pieces), grid=(height // bl...]
    unnamed x65 -> x95, local copies, waits for them, and re-layouts: 5.07 us -> 11.1 us
  transfers between devices with their start and end apart: 69 -> 69, of which waited for: 31 -> 31; matrix products, arithmetic and copies ran while one was open for 9% -> 10% of each run, Pallas kernels for 13% -> 13%
where the time goes in v7:
time: 308 us
  waiting for transfers between devices  120 us (39%)
  starting transfers between devices  74.8 us (24%)
  Pallas kernels  59.3 us (19%)
  other arithmetic  19.3 us (6%)
  local copies, waits for them, and re-layouts  16.6 us (5%)
  matrix products  13.9 us (5%)
  between operations  4.18 us (1%)
    ppermute x10, waiting for transfers between devices, line_gather(): arrived[links, step] = lax.ppermute(came[1 - links, step - 1], axis, pairs)  67.5 us
    ppermute x56, starting transfers between devices, exchange(): lax.ppermute(part, axis, [(i, i ^ mask) for i in range(lax.axis_size(axis...  52.7 us
    ppermute x56, waiting for transfers between devices, exchange(): lax.ppermute(part, axis, [(i, i ^ mask) for i in range(lax.axis_size(axis...  52.1 us
    pallas_call x3, Pallas kernels, update(): pl.pallas_call(update_kernel, grid=(height // block,), in_specs=[pl.Block...  33.2 us
    pallas_call x4, Pallas kernels, grad_sum(): pl.pallas_call(functools.partial(grad_kernel, pieces), grid=(height // bl...  20.7 us
    ppermute x10, starting transfers between devices, line_gather(): arrived[links, step] = lax.ppermute(came[1 - links, step - 1], axis, pairs)  14.2 us
    unnamed x95, local copies, waits for them, and re-layouts  11.1 us
    ppermute x3, starting transfers between devices, on_device(): lax.ppermute(codes, 'col', [(i, (i + shift) % n) for i in range(n)])  7.93 us
  transfers between devices with their start and end apart: 69, of which 31 were waited for; matrix products, arithmetic and copies ran while one was open for 10% of the time, Pallas kernels for 13%

profile of v7, /device:TPU:0, one launch (start us, length us, event | category | flops | bytes accessed | tf_op | source)
XLA Modules:
  0.0 307.7 jit_solution(53458448163036587)
XLA Ops:
  1.4 4.1 %collective-permute-start.6 = (f32[2,384]{1,0:T(2,128)S(1)}, f32[2,384]{1,0:T(2,128)S(1)}, u32[]{:S(2)}, u32[]{:S(2)}) collective-permute-start(f32[2,384]{1,0:T(2,128)S(1)} %get-tuple-element.214), channel_id=1, source_target_pairs={{0,2},{1,3},{2,0},{3,1},{4,6},{5,7},{6,4},{7,5},{8,10},{9,11},{10,... | collective-permute-start | bytes 9224 | tf_op jit(solution)/shard_map/ppermute | solution.py:295
  7.1 2.2 collective-permute-start.7
  13.1 3.5 %convert_element_type.80 = bf16[2304,768]{1,0:T(8,128)(2,1)S(1)} convert(f32[2304,768]{1,0:T(8,128)} %w.1) | non-fusion elementwise | flops 1769472 | bytes 10616832 | tf_op jit(solution)/shard_map/convert_element_type | solution.py:302
  18.2 2.1 convert_element_type.81
  32.4 3.2 %collective-permute-done.13 = f32[48,768]{1,0:T(8,128)S(1)} collective-permute-done((f32[48,768]{1,0:T(8,128)S(1)}, f32[48,768]{1,0:T(8,128)S(1)}, u32[]{:S(2)}, u32[]{:S(2)}) %collective-permute-start.13) | collective-permute-done | bytes 147488 | tf_op jit(solution)/shard_map/ppermute | solution.py:212
  35.5 3.4 %collective-permute-done.15 = f32[48,768]{1,0:T(8,128)S(1)} collective-permute-done((f32[48,768]{1,0:T(8,128)S(1)}, f32[48,768]{1,0:T(8,128)S(1)}, u32[]{:S(2)}, u32[]{:S(2)}) %collective-permute-start.15) | collective-permute-done | bytes 147488 | tf_op jit(solution)/shard_map/ppermute | solution.py:212
  51.0 3.0 convolution_bitcast_fusion
  55.2 3.2 %collective-permute-start.8 = (bf16[384,2304]{1,0:T(8,128)(2,1)S(1)}, bf16[384,2304]{1,0:T(8,128)(2,1)S(1)}, u32[]{:S(2)}, u32[]{:S(2)}) collective-permute-start(bf16[384,2304]{1,0:T(8,128)(2,1)S(1)} %copy-done.25), channel_id=1, source_target_pairs={{0,1},{1,0},{2,3},{3,2},{4,5},{5,4},{6,7},{7,6},{8,9},{9,8},{10,11... | collective-permute-start | bytes 5308424 | tf_op jit(solution)/shard_map/ppermute | solution.py:182
  62.2 6.4 %collective-permute-done.21 = f32[2,48,768]{2,1,0:T(8,128)S(1)} collective-permute-done((f32[2,48,768]{2,1,0:T(8,128)S(1)}, f32[2,48,768]{2,1,0:T(8,128)S(1)}, u32[]{:S(2)}, u32[]{:S(2)}) %collective-permute-start.21) | collective-permute-done | bytes 294944 | tf_op jit(solution)/shard_map/ppermute | solution.py:212
  68.6 6.1 %collective-permute-done.23 = f32[2,48,768]{2,1,0:T(8,128)S(1)} collective-permute-done((f32[2,48,768]{2,1,0:T(8,128)S(1)}, f32[2,48,768]{2,1,0:T(8,128)S(1)}, u32[]{:S(2)}, u32[]{:S(2)}) %collective-permute-start.23) | collective-permute-done | bytes 294944 | tf_op jit(solution)/shard_map/ppermute | solution.py:212
  81.8 15.4 %collective-permute-done.8 = bf16[384,2304]{1,0:T(8,128)(2,1)S(1)} collective-permute-done((bf16[384,2304]{1,0:T(8,128)(2,1)S(1)}, bf16[384,2304]{1,0:T(8,128)(2,1)S(1)}, u32[]{:S(2)}, u32[]{:S(2)}) %collective-permute-start.8) | collective-permute-done | bytes 1769504 | tf_op jit(solution)/shard_map/ppermute | solution.py:182
  110.3 28.1 %collective-permute-done.2 = bf16[384,2304]{1,0:T(8,128)(2,1)} collective-permute-done((bf16[384,2304]{1,0:T(8,128)(2,1)}, bf16[384,2304]{1,0:T(8,128)(2,1)}, u32[]{:S(2)}, u32[]{:S(2)}) %collective-permute-start.2) | collective-permute-done | bytes 1769504 | tf_op jit(solution)/shard_map/ppermute | solution.py:182
  153.3 5.4 %shard_map.192 = (f32[768,1152]{1,0:T(8,128)S(1)}, f32[768,1152]{1,0:T(8,128)S(1)}, f32[768,1152]{1,0:T(8,128)S(1)}, f32[768,1152]{1,0:T(8,128)S(1)}, f32[768,1152]{1,0:T(8,128)S(1)}, /*index=5*/f32[768,1152]{1,0:T(8,128)S(1)}) custom-call(f32[768,2304]{1,0:T(8,128)S(1)} %bitcast.54, f32[768,2304]{1,0:T(8,128)} %refs_1_.1, f32[768,2304]{1,0:T(8,128)} %refs_2_.1), custom_call_target="tpu_custom_call" | custom-call | bytes 21233664 | tf_op jit(solution)/shard_map/pallas_call | solution.py:73
  165.6 16.5 %collective-permute-done.10 = bf16[384,2304]{1,0:T(8,128)(2,1)S(1)} collective-permute-done((bf16[384,2304]{1,0:T(8,128)(2,1)}, bf16[384,2304]{1,0:T(8,128)(2,1)S(1)}, u32[]{:S(2)}, u32[]{:S(2)}) %collective-permute-start.10) | collective-permute-done | bytes 1769504 | tf_op jit(solution)/shard_map/ppermute | solution.py:182
  183.3 5.2 %shard_map.191.refs_2_ = f32[768,2304]{1,0:T(8,128)S(1)} custom-call(bf16[384,768]{1,0:T(8,128)(2,1)S(1)} %copy-done.13, bf16[384,768]{1,0:T(8,128)(2,1)S(1)} %get-tuple-element.174.refs_1_, bf16[384,2304]{1,0:T(8,128)(2,1)S(1)} %multiply_convert_fusion.1.refs_2_, bf16[384,2304]{1,0:T(8,128)(2,1)S(1)} %multiply_convert_fusion.2.refs_3_), custom_call_target="tpu_custom_call" | custom-call | flops 2717908992 | bytes 11796480 | tf_op jit(solution)/shard_map/pallas_call | solution.py:101
  193.4 7.9 %shard_map.190.refs_2_ = f32[2304,768]{1,0:T(8,128)S(1)} custom-call(bf16[384,2304]{1,0:T(8,128)(2,1)S(1)} %copy-done.15, bf16[384,2304]{1,0:T(8,128)(2,1)} %collective-permute-done.refs_1_, bf16[384,768]{1,0:T(8,128)(2,1)S(1)} %get-tuple-element.175.refs_2_, bf16[384,768]{1,0:T(8,128)(2,1)S(1)} %broadcast_select_fusion.7.refs_3_), custom_call_target="tpu_custom_call" | custom-call | flops 2717908992 | bytes 11796480 | tf_op jit(solution)/shard_map/pallas_call | solution.py:101
  206.4 2.4 collective-permute-done.40
  220.0 2.7 collective-permute-done.47
  240.4 3.6 %shard_map.194.grad = f32[768,2304]{1,0:T(8,128)S(1)} custom-call(bf16[384,768]{1,0:T(8,128)(2,1)S(1)} %broadcast_select_fusion.6.refs_0_, bf16[384,2304]{1,0:T(8,128)(2,1)S(1)} %multiply_convert_fusion.3.refs_1_, f32[768,2304]{1,0:T(8,128)S(1)} %shard_map.191.refs_2_), custom_call_target="tpu_custom_call", output_to_operand_aliasing={{}: (2, {})} | custom-call | flops 1358954496 | bytes 9437184 | tf_op jit(solution)/shard_map/pallas_call | solution.py:101
  244.0 4.0 %shard_map.193.grad = f32[2304,768]{1,0:T(8,128)S(1)} custom-call(bf16[384,2304]{1,0:T(8,128)(2,1)S(1)} %broadcast_select_fusion.refs_0_, bf16[384,768]{1,0:T(8,128)(2,1)S(1)} %broadcast_select_fusion.5.refs_1_, f32[2304,768]{1,0:T(8,128)S(1)} %shard_map.190.refs_2_), custom_call_target="tpu_custom_call", output_to_operand_aliasing={{}: (2, {})} | custom-call | flops 1358954496 | bytes 9437184 | tf_op jit(solution)/shard_map/pallas_call | solution.py:101
  251.6 7.1 %collective-permute-done.59 = bf16[384,2304]{1,0:T(8,128)(2,1)S(1)} collective-permute-done((bf16[384,2304]{1,0:T(8,128)(2,1)S(1)}, bf16[384,2304]{1,0:T(8,128)(2,1)S(1)}, u32[]{:S(2)}, u32[]{:S(2)}) %collective-permute-start.59) | collective-permute-done | bytes 1769504 | tf_op jit(solution)/shard_map/ppermute | solution.py:182
  268.8 6.5 %shard_map.195 = (f32[768,2304]{1,0:T(8,128)}, f32[768,2304]{1,0:T(8,128)}, f32[768,2304]{1,0:T(8,128)}) custom-call(bf16[384,768]{1,0:T(8,128)(2,1)S(1)} %broadcast_select_fusion.4.left, bf16[384,2304]{1,0:T(8,128)(2,1)S(1)} %multiply_convert_fusion.right, f32[768,2304]{1,0:T(8,128)S(1)} %shard_map.194.grad, f32[768,1152]{1,0:T(8,128)S(1)} %copy-done.8, ...), custom_call_target="tpu_custom_call" | custom-call | flops 679477248 | bytes 26247168 | tf_op jit(solution)/shard_map/pallas_call | solution.py:132
  279.0 6.5 %shard_map.196 = (f32[768,2304]{1,0:T(8,128)}, f32[768,2304]{1,0:T(8,128)}, f32[768,2304]{1,0:T(8,128)}) custom-call(bf16[384,768]{1,0:T(8,128)(2,1)S(1)} %broadcast_select_fusion.4.left, bf16[384,2304]{1,0:T(8,128)(2,1)S(1)} %multiply_convert_fusion.right, ...), custom_call_target="tpu_custom_call", output_to_operand_aliasing={{0}: (6, {}), {1}: (7, {}), {2}: (8, {})} | custom-call | flops 679477248 | bytes 26247168 | tf_op jit(solution)/shard_map/pallas_call | solution.py:132
  287.6 20.1 %shard_map.197 = (f32[2304,768]{1,0:T(8,128)}, f32[2304,768]{1,0:T(8,128)}, f32[2304,768]{1,0:T(8,128)}) custom-call(bf16[384,2304]{1,0:T(8,128)(2,1)S(1)} %broadcast_select_fusion.1.left, bf16[384,768]{1,0:T(8,128)(2,1)S(1)} %broadcast_select_fusion.3.right, f32[2304,768]{1,0:T(8,128)S(1)} %shard_map.193.grad, f32[2304,768]{1,0:T(8,128)} %w.1, ...), custom_call_target="tpu_custom_call" | custom-call | flops 1358954496 | bytes 51904512 | tf_op jit(solution)/shard_map/pallas_call | solution.py:132
  (348 shorter events, 134.7 us)
Async XLA Ops:
  1.4 24.0 %collective-permute-start.6 = (f32[2,384]{1,0:T(2,128)S(1)}, f32[2,384]{1,0:T(2,128)S(1)}, u32[]{:S(2)}, u32[]{:S(2)}) collective-permute-start(f32[2,384]{1,0:T(2,128)S(1)} %get-tuple-element.214), channel_id=1, source_target_pairs={{0,2},{1,3},{2,0},{3,1},{4,6},{5,7},{6,4},{7,5},{8,10},{9,11},{10,... | collective-permute-start | bytes 9224 | tf_op jit(solution)/shard_map/ppermute | solution.py:295
  5.5 20.0 %collective-permute-start.5 = (f32[2,384]{1,0:T(2,128)S(1)}, f32[2,384]{1,0:T(2,128)S(1)}, u32[]{:S(2)}, u32[]{:S(2)}) collective-permute-start(f32[2,384]{1,0:T(2,128)S(1)} %get-tuple-element.214), channel_id=1, source_target_pairs={{0,1},{1,2},{2,3},{3,0},{4,5},{5,6},{6,7},{7,4},{8,9},{9,10},{10,1... | collective-permute-start | bytes 9224 | tf_op jit(solution)/shard_map/ppermute | solution.py:295
  7.1 18.4 %collective-permute-start.7 = (f32[2,384]{1,0:T(2,128)S(1)}, f32[2,384]{1,0:T(2,128)S(1)}, u32[]{:S(2)}, u32[]{:S(2)}) collective-permute-start(f32[2,384]{1,0:T(2,128)S(1)} %get-tuple-element.214), channel_id=1, source_target_pairs={{0,3},{1,0},{2,1},{3,2},{4,7},{5,4},{6,5},{7,6},{8,11},{9,8},{10,9... | collective-permute-start | bytes 9224 | tf_op jit(solution)/shard_map/ppermute | solution.py:295
  9.4 41.2 %collective-permute-start.1 = (bf16[384,2304]{1,0:T(8,128)(2,1)}, bf16[384,2304]{1,0:T(8,128)(2,1)}, u32[]{:S(2)}, u32[]{:S(2)}) collective-permute-start(bf16[384,2304]{1,0:T(8,128)(2,1)} %refs_0_.2), channel_id=1, source_target_pairs={{1,2},{2,1},{5,6},{6,5},{9,10},{10,9},{13,14},{14,13},{17,18},{18,... | collective-permute-start | bytes 5308424 | tf_op jit(solution)/shard_map/ppermute | solution.py:182
  11.2 39.8 %collective-permute-start = (bf16[384,2304]{1,0:T(8,128)(2,1)}, bf16[384,2304]{1,0:T(8,128)(2,1)}, u32[]{:S(2)}, u32[]{:S(2)}) collective-permute-start(bf16[384,2304]{1,0:T(8,128)(2,1)} %refs_0_.2), channel_id=1, source_target_pairs={{0,1},{1,0},{2,3},{3,2},{4,5},{5,4},{6,7},{7,6},{8,9},{9,8},{10,11... | collective-permute-start | bytes 5308424 | tf_op jit(solution)/shard_map/ppermute | solution.py:182
  54.4 26.1 %collective-permute-start.9 = (bf16[384,2304]{1,0:T(8,128)(2,1)S(1)}, bf16[384,2304]{1,0:T(8,128)(2,1)S(1)}, u32[]{:S(2)}, u32[]{:S(2)}) collective-permute-start(bf16[384,2304]{1,0:T(8,128)(2,1)S(1)} %copy-done.25), channel_id=1, source_target_pairs={{1,2},{2,1},{5,6},{6,5},{9,10},{10,9},{13,14},{14,13},{17,18},{18,... | collective-permute-start | bytes 5308424 | tf_op jit(solution)/shard_map/ppermute | solution.py:182
  55.2 42.0 %collective-permute-start.8 = (bf16[384,2304]{1,0:T(8,128)(2,1)S(1)}, bf16[384,2304]{1,0:T(8,128)(2,1)S(1)}, u32[]{:S(2)}, u32[]{:S(2)}) collective-permute-start(bf16[384,2304]{1,0:T(8,128)(2,1)S(1)} %copy-done.25), channel_id=1, source_target_pairs={{0,1},{1,0},{2,3},{3,2},{4,5},{5,4},{6,7},{7,6},{8,9},{9,8},{10,11... | collective-permute-start | bytes 5308424 | tf_op jit(solution)/shard_map/ppermute | solution.py:182
  59.8 15.0 %collective-permute-start.23 = (f32[2,48,768]{2,1,0:T(8,128)S(1)}, f32[2,48,768]{2,1,0:T(8,128)S(1)}, u32[]{:S(2)}, u32[]{:S(2)}) collective-permute-start(f32[2,48,768]{2,1,0:T(8,128)S(1)} %get-tuple-element.177), channel_id=1, source_target_pairs={{0,24},{4,28},{8,16},{12,20},{16,8},{20,12},{24,0},{28,4},{1,25},{... | collective-permute-start | bytes 884744 | tf_op jit(solution)/shard_map/ppermute | solution.py:212
  61.7 14.4 %collective-permute-start.22 = (f32[2,48,768]{2,1,0:T(8,128)S(1)}, f32[2,48,768]{2,1,0:T(8,128)S(1)}, u32[]{:S(2)}, u32[]{:S(2)}) collective-permute-start(f32[2,48,768]{2,1,0:T(8,128)S(1)} %get-tuple-element.178), channel_id=1, source_target_pairs={{0,16},{4,20},{8,24},{12,28},{16,0},{20,4},{24,8},{28,12},{1,17},{... | collective-permute-start | bytes 884744 | tf_op jit(solution)/shard_map/ppermute | solution.py:212
  77.0 22.2 %collective-permute-start.26 = (bf16[2,48,768]{2,1,0:T(8,128)(2,1)S(1)}, bf16[2,48,768]{2,1,0:T(8,128)(2,1)S(1)}, u32[]{:S(2)}, u32[]{:S(2)}) collective-permute-start(bf16[2,48,768]{2,1,0:T(8,128)(2,1)S(1)} %pad_maximum_fusion.8), channel_id=1, source_target_pairs={{0,8},{4,12},{8,0},{12,4},{16,24},{20,28},{24,16},{28,20},{1,9},{5... | collective-permute-start | bytes 442376 | tf_op jit(solution)/shard_map/ppermute | solution.py:212
  78.3 20.9 %collective-permute-start.25 = (bf16[2,48,768]{2,1,0:T(8,128)(2,1)S(1)}, bf16[2,48,768]{2,1,0:T(8,128)(2,1)S(1)}, u32[]{:S(2)}, u32[]{:S(2)}) collective-permute-start(bf16[2,48,768]{2,1,0:T(8,128)(2,1)S(1)} %pad_maximum_fusion.8), channel_id=1, source_target_pairs={{0,16},{4,20},{8,24},{12,28},{16,0},{20,4},{24,8},{28,12},{1,17},{... | collective-permute-start | bytes 442376 | tf_op jit(solution)/shard_map/ppermute | solution.py:212
  78.8 20.4 %collective-permute-start.24 = (bf16[2,48,768]{2,1,0:T(8,128)(2,1)S(1)}, bf16[2,48,768]{2,1,0:T(8,128)(2,1)S(1)}, u32[]{:S(2)}, u32[]{:S(2)}) collective-permute-start(bf16[2,48,768]{2,1,0:T(8,128)(2,1)S(1)} %pad_maximum_fusion.8), channel_id=1, source_target_pairs={{0,24},{4,28},{8,16},{12,20},{16,8},{20,12},{24,0},{28,4},{1,25},{... | collective-permute-start | bytes 442376 | tf_op jit(solution)/shard_map/ppermute | solution.py:212
  80.5 57.9 %collective-permute-start.2 = (bf16[384,2304]{1,0:T(8,128)(2,1)}, bf16[384,2304]{1,0:T(8,128)(2,1)}, u32[]{:S(2)}, u32[]{:S(2)}) collective-permute-start(bf16[384,2304]{1,0:T(8,128)(2,1)} %collective-permute-done.1), channel_id=1, source_target_pairs={{1,0},{2,3},{5,4},{6,7},{9,8},{10,11},{13,12},{14,15},{17,16},{18,... | collective-permute-start | bytes 5308424 | tf_op jit(solution)/shard_map/ppermute | solution.py:182
  97.2 42.5 %collective-permute-start.3 = (bf16[384,2304]{1,0:T(8,128)(2,1)}, bf16[384,2304]{1,0:T(8,128)(2,1)}, u32[]{:S(2)}, u32[]{:S(2)}) collective-permute-start(bf16[384,2304]{1,0:T(8,128)(2,1)} %collective-permute-done.refs_1_), channel_id=1, source_target_pairs={{1,2},{2,1},{5,6},{6,5},{9,10},{10,9},{13,14},{14,13},{17,18},{18,... | collective-permute-start | bytes 5308424 | tf_op jit(solution)/shard_map/ppermute | solution.py:182
  106.8 33.9 %collective-permute-start.29 = (f32[48,768]{1,0:T(8,128)}, f32[48,768]{1,0:T(8,128)}, u32[]{:S(2)}, u32[]{:S(2)}) collective-permute-start(f32[48,768]{1,0:T(8,128)} %get-tuple-element.191), channel_id=1, source_target_pairs={{0,8},{4,12},{8,0},{12,4},{16,24},{20,28},{24,16},{28,20},{1,9},{5... | collective-permute-start | bytes 442376 | tf_op jit(solution)/shard_map/ppermute | solution.py:212
  108.1 32.6 %collective-permute-start.31 = (f32[48,768]{1,0:T(8,128)}, f32[48,768]{1,0:T(8,128)}, u32[]{:S(2)}, u32[]{:S(2)}) collective-permute-start(f32[48,768]{1,0:T(8,128)} %get-tuple-element.192), channel_id=1, source_target_pairs={{0,24},{4,28},{8,16},{12,20},{16,8},{20,12},{24,0},{28,4},{1,25},{... | collective-permute-start | bytes 442376 | tf_op jit(solution)/shard_map/ppermute | solution.py:212
  109.8 30.9 %collective-permute-start.30 = (f32[48,768]{1,0:T(8,128)}, f32[48,768]{1,0:T(8,128)}, u32[]{:S(2)}, u32[]{:S(2)}) collective-permute-start(f32[48,768]{1,0:T(8,128)} %get-tuple-element.193), channel_id=1, source_target_pairs={{0,16},{4,20},{8,24},{12,28},{16,0},{20,4},{24,8},{28,12},{1,17},{... | collective-permute-start | bytes 442376 | tf_op jit(solution)/shard_map/ppermute | solution.py:212
  138.4 43.6 %collective-permute-start.10 = (bf16[384,2304]{1,0:T(8,128)(2,1)}, bf16[384,2304]{1,0:T(8,128)(2,1)S(1)}, u32[]{:S(2)}, u32[]{:S(2)}) collective-permute-start(bf16[384,2304]{1,0:T(8,128)(2,1)} %copy-done.26), channel_id=1, source_target_pairs={{1,0},{2,3},{5,4},{6,7},{9,8},{10,11},{13,12},{14,15},{17,16},{18,... | collective-permute-start | bytes 5308424 | tf_op jit(solution)/shard_map/ppermute | solution.py:182
  139.7 42.3 %collective-permute-start.11 = (bf16[384,2304]{1,0:T(8,128)(2,1)}, bf16[384,2304]{1,0:T(8,128)(2,1)S(1)}, u32[]{:S(2)}, u32[]{:S(2)}) collective-permute-start(bf16[384,2304]{1,0:T(8,128)(2,1)} %copy-done.28), channel_id=1, source_target_pairs={{1,2},{2,1},{5,6},{6,5},{9,10},{10,9},{13,14},{14,13},{17,18},{18,... | collective-permute-start | bytes 5308424 | tf_op jit(solution)/shard_map/ppermute | solution.py:182
  152.5 36.0 %collective-permute-start.36 = (f32[192,768]{1,0:T(8,128)}, f32[192,768]{1,0:T(8,128)}, u32[]{:S(2)}, u32[]{:S(2)}) collective-permute-start(f32[192,768]{1,0:T(8,128)} %constant_dynamic-slice_fusion.15), channel_id=1, source_target_pairs={{0,4},{4,0},{8,12},{12,8},{16,20},{20,16},{24,28},{28,24},{1,5},{5... | collective-permute-start | bytes 1769480 | tf_op jit(solution)/shard_map/ppermute | solution.py:212
  164.2 54.2 %collective-permute-start.4 = (bf16[384,2304]{1,0:T(8,128)(2,1)}, bf16[384,2304]{1,0:T(8,128)(2,1)S(1)}, u32[]{:S(2)}, u32[]{:S(2)}) collective-permute-start(bf16[384,2304]{1,0:T(8,128)(2,1)} %collective-permute-done.3), channel_id=1, source_target_pairs={{1,0},{2,3},{5,4},{6,7},{9,8},{10,11},{13,12},{14,15},{17,16},{18,... | collective-permute-start | bytes 5308424 | tf_op jit(solution)/shard_map/ppermute | solution.py:182
  189.8 11.5 %collective-permute-start.39 = (f32[48,768]{1,0:T(8,128)S(1)}, f32[48,768]{1,0:T(8,128)S(1)}, u32[]{:S(2)}, u32[]{:S(2)}) collective-permute-start(f32[48,768]{1,0:T(8,128)S(1)} %get-tuple-element.188), channel_id=1, source_target_pairs={{0,24},{4,28},{8,16},{12,20},{16,8},{20,12},{24,0},{28,4},{1,25},{... | collective-permute-start | bytes 442376 | tf_op jit(solution)/shard_map/ppermute | solution.py:212
  216.8 41.9 %collective-permute-start.59 = (bf16[384,2304]{1,0:T(8,128)(2,1)S(1)}, bf16[384,2304]{1,0:T(8,128)(2,1)S(1)}, u32[]{:S(2)}, u32[]{:S(2)}) collective-permute-start(bf16[384,2304]{1,0:T(8,128)(2,1)S(1)} %collective-permute-done.11), channel_id=1, source_target_pairs={{1,0},{2,3},{5,4},{6,7},{9,8},{10,11},{13,12},{14,15},{17,16},{18,... | collective-permute-start | bytes 5308424 | tf_op jit(solution)/shard_map/ppermute | solution.py:182
  236.8 11.2 %collective-permute-start.55 = (f32[48,768]{1,0:T(8,128)S(1)}, f32[48,768]{1,0:T(8,128)S(1)}, u32[]{:S(2)}, u32[]{:S(2)}) collective-permute-start(f32[48,768]{1,0:T(8,128)S(1)} %get-tuple-element.182), channel_id=1, source_target_pairs={{0,24},{4,28},{8,16},{12,20},{16,8},{20,12},{24,0},{28,4},{1,25},{... | collective-permute-start | bytes 442376 | tf_op jit(solution)/shard_map/ppermute | solution.py:212
  (82 other events, 561.3 us)

commit v8 on v7

--- a/solution.py
+++ b/solution.py
@@ -53,35 +53,35 @@
     return block
 
 
-def fetch_kernel(parts, *refs):
-    count = (len(refs) - 1) // (parts + 1)
-    sources, targets, sems = refs[:count], refs[count:-1], refs[-1]
+def fetch_kernel(count, axis, part, *refs):
+    sources, targets, sems = refs[:count], refs[-1 - count : -1], refs[-1]
     copies = []
-    for i, target in enumerate(targets):
-        part, source = divmod(i, len(sources))
-        width = target.shape[1]
-        columns = sources[source].at[:, pl.ds(part * width, width)]
-        copies.append(pltpu.make_async_copy(columns, target, sems.at[i]))
+    for i, (source, target) in enumerate(zip(sources, targets)):
+        size = target.shape[axis]
+        span = pl.ds(part * size, size)
+        source = source.at[span, :] if axis == 0 else source.at[:, span]
+        copies.append(pltpu.make_async_copy(source, target, sems.at[i]))
     for copy in copies:
         copy.start()
     for copy in copies:
         copy.wait()
 
 
-def fetch(arrays, parts):
-    shapes = [pltpu.VMEM((x.shape[0], x.shape[1] // parts), x.dtype) for x in arrays] * parts
-    fetched = pl.pallas_call(
-        functools.partial(fetch_kernel, parts),
-        in_specs=[pl.BlockSpec(memory_space=pl.ANY)] * len(arrays),
-        out_specs=[pl.BlockSpec(memory_space=pltpu.VMEM)] * len(shapes),
-        out_shape=shapes,
-        scratch_shapes=[pltpu.SemaphoreType.DMA((len(shapes),))],
-        compiler_params=pltpu.CompilerParams(vmem_limit_bytes=26 * 2**20),
+def fetch(arrays, axis, part, parts, earlier=()):
+    shape = list(arrays[0].shape)
+    shape[axis] //= parts
+    count = len(arrays)
+    return pl.pallas_call(
+        functools.partial(fetch_kernel, count, axis, part),
+        in_specs=[pl.BlockSpec(memory_space=pltpu.HBM)] * (count + len(earlier)),
+        out_specs=[pl.BlockSpec(memory_space=pltpu.VMEM)] * count,
+        out_shape=[pltpu.VMEM(tuple(shape), jnp.float32)] * count,
+        scratch_shapes=[pltpu.SemaphoreType.DMA((count,))],
+        compiler_params=pltpu.CompilerParams(vmem_limit_bytes=4 * 2**20),
         cost_estimate=pl.CostEstimate(
-            flops=0, bytes_accessed=4 * sum(x.size for x in arrays), transcendentals=0
+            flops=0, bytes_accessed=4 * count * math.prod(shape), transcendentals=0
         ),
-    )(*arrays)
-    return [fetched[i : i + len(arrays)] for i in range(0, len(shapes), len(arrays))]
+    )(*[pltpu.with_memory_space_constraint(x, pltpu.HBM) for x in (*arrays, *earlier)])
 
 
 def grad_kernel(pieces, *refs):
@@ -107,7 +107,7 @@
         out_specs=panel,
         out_shape=pltpu.VMEM((height, width), jnp.float32),
         input_output_aliases={2 * pieces + i: i for i in range(len(so_far))},
-        compiler_params=pltpu.CompilerParams(vmem_limit_bytes=20 * 2**20),
+        compiler_params=pltpu.CompilerParams(vmem_limit_bytes=16 * 2**20),
         cost_estimate=pl.CostEstimate(
             flops=2 * pieces * rows * height * width,
             bytes_accessed=4 * height * width + 2 * pieces * rows * (height + width),
@@ -122,19 +122,21 @@
     new_w[...], new_m[...], new_v[...] = adamw(w[...], m[...], v[...], total)
 
 
-def update(left, right, grad, w, m, v, most, limit, part=0, parts=1, so_far=()):
-    rows, height = left.shape
-    width = right.shape[1] // parts
+def update(left, right, grad, state, most, axis, part, parts, so_far=()):
+    rows = left.shape[0]
+    height, width = state[0].shape
     block = block_of(height, most)
-    panel = pl.BlockSpec((block, width), lambda i: (i, part))
+    steps = height // block
+    row0, column = (part * steps, 0) if axis == 0 else (0, part)
+    panel = pl.BlockSpec((block, width), lambda i: (row0 + i, column))
     own = pl.BlockSpec((block, width), lambda i: (i, 0))
-    shape = jax.ShapeDtypeStruct((height, right.shape[1]), jnp.float32)
+    shape = jax.ShapeDtypeStruct((left.shape[1], right.shape[1]), jnp.float32)
     return pl.pallas_call(
         update_kernel,
-        grid=(height // block,),
+        grid=(steps,),
         in_specs=[
-            pl.BlockSpec((rows, block), lambda i: (0, i)),
-            pl.BlockSpec((rows, width), lambda i: (0, part)),
+            pl.BlockSpec((rows, block), lambda i: (0, row0 + i)),
+            pl.BlockSpec((rows, width), lambda i: (0, column)),
             panel,
         ]
         + [own] * 3
@@ -142,13 +144,13 @@
         out_specs=[panel] * 3,
         out_shape=[shape] * 3,
         input_output_aliases={6 + i: i for i in range(len(so_far))},
-        compiler_params=pltpu.CompilerParams(vmem_limit_bytes=limit * 2**20),
+        compiler_params=pltpu.CompilerParams(vmem_limit_bytes=16 * 2**20),
         cost_estimate=pl.CostEstimate(
             flops=2 * rows * height * width,
             bytes_accessed=7 * 4 * height * width + 2 * rows * (height + width),
             transcendentals=2 * height * width,
         ),
-    )(left, right, grad, w, m, v, *so_far)
+    )(left, right, grad, *state, *so_far)
 
 
 def link_pairs(n, first, step):
@@ -319,19 +321,8 @@
 
     token_slots, owners, tokens_came = line_gather(tokens, "col")
     out_grad_slots, _, out_grads_came = line_gather(out_grad, "col")
-    parts = next(p for p in (2, 3, 1) if w_out.shape[1] % (128 * p) == 0)
-    outs_out = ()
-
-    def update_part(part):
-        def run():
-            nonlocal outs_out
-            outs_out = update(
-                acts[-1], dys[-1], grad_out, *state_out[part], 128, 20, part, parts, outs_out
-            )
-            return outs_out
-
-        return run
-
+    parts = 2 if w_out.shape[1] % 256 == 0 else 1
+    parts_in = 2 if w_in.shape[0] % 256 == 0 else 1
     dys = [scaled(out_grad, here)]
     pre = row_sum(pre_of(tokens), "row")
     acts, dpres = [row_gather(square(pre), "row")], []
@@ -348,8 +339,8 @@
             if slot == n - 2:
                 grad_in = grad_sum(token_slots[:slot], dpres, 256)
                 grad_out = grad_sum(acts, dys, 128)
-                state_out = fetch((w_out, m_out, v_out), parts)
-                beside = [None, (grad_in, grad_out, state_out)]
+                states_out = [fetch((w_out, m_out, v_out), 1, p, parts) for p in range(parts)]
+                beside = [None, (grad_in, grad_out, states_out)]
             if slot == n - 1:
                 grad_in = grad_sum(token_slots[slot - 1 : slot], dpres[-1:], 256, (grad_in,))
                 grad_out = grad_sum(acts[-1:], dys[-1:], 128, (grad_out,))
@@ -364,12 +355,30 @@
             dpres.append(last)
 
     dys.append(scaled(out_grad_slots[n - 1], owners[n - 1], acts[-1]))
-    work = [None] + [update_part(part) for part in range(parts)]
+    outs_out, states_in = (), []
+
+    def update_out(part):
+        nonlocal outs_out
+        outs_out = update(
+            acts[-1], dys[-1], grad_out, states_out[part], 128, 1, part, parts, outs_out
+        )
+        return outs_out
+
+    def state_in(part):
+        states_in.append(fetch((w_in, m_in, v_in), 0, part, parts_in, outs_out))
+        return states_in[part]
+
+    runs = [lambda p=p: update_out(p) for p in range(parts)]
+    for p in range(parts_in):
+        runs.insert(1 + 2 * p, lambda p=p: state_in(p))
+    work = [None, runs[0], lambda: [run() for run in runs[1:-1]], runs[-1]]
     back = row_sum(against(dys[n - 1], w_out16), "row", work)
     dpres.append(row_gather(chain(pre, back), "row", work))
-    while work:
-        work.pop(0)()
-    outs_in = update(token_slots[-1], dpres[-1], grad_in, w_in, m_in, v_in, 256, 42)
+    outs_in = ()
+    for p in range(parts_in):
+        outs_in = update(
+            token_slots[-1], dpres[-1], grad_in, states_in[p], 256, 0, p, parts_in, outs_in
+        )
     return (*outs_in, *outs_out)
 
 

time: 308 us -> 309 us (level)
  waiting for transfers between devices: 120 us -> 114 us
  Pallas kernels: 59.3 us -> 65.2 us
    pallas_call x4 -> x8, Pallas kernels: 38.6 us -> 44.6 us  [the longest x4 27.9 us: update(): pl.pallas_call(update_kernel, grid=(steps,), in_specs=[pl.BlockSpec((rows...]
    ppermute x56, waiting for transfers between devices: 52.1 us -> 47.2 us  [exchange(): lax.ppermute(part, axis, [(i, i ^ mask) for i in range(lax.axis_size(axis...]
    unnamed x95 -> x73, local copies, waits for them, and re-layouts: 11.1 us -> 10.3 us
  transfers between devices with their start and end apart: 69 -> 69, of which waited for: 31 -> 30; matrix products, arithmetic and copies ran while one was open for 10% -> 10% of each run, Pallas kernels for 13% -> 16%
where the time goes in v8:
time: 309 us; the launch traced here: 308 us
  waiting for transfers between devices  114 us (37%)
  starting transfers between devices  76 us (25%)
  Pallas kernels  65.2 us (21%)
  other arithmetic  19.9 us (6%)
  local copies, waits for them, and re-layouts  14.9 us (5%)
  matrix products  13.9 us (4%)
  between operations  4.07 us (1%)
    ppermute x10, waiting for transfers between devices, line_gather(): arrived[links, step] = lax.ppermute(came[1 - links, step - 1], axis, pairs)  66.9 us
    ppermute x56, starting transfers between devices, exchange(): lax.ppermute(part, axis, [(i, i ^ mask) for i in range(lax.axis_size(axis...  52.8 us
    ppermute x56, waiting for transfers between devices, exchange(): lax.ppermute(part, axis, [(i, i ^ mask) for i in range(lax.axis_size(axis...  47.2 us
    pallas_call x4, Pallas kernels, update(): pl.pallas_call(update_kernel, grid=(steps,), in_specs=[pl.BlockSpec((rows...  27.9 us
    pallas_call x4, Pallas kernels, grad_sum(): pl.pallas_call(functools.partial(grad_kernel, pieces), grid=(height // bl...  20.6 us
    pallas_call x4, Pallas kernels, fetch(): pl.pallas_call(functools.partial(fetch_kernel, count, axis, part), in_spe...  16.7 us
    ppermute x10, starting transfers between devices, line_gather(): arrived[links, step] = lax.ppermute(came[1 - links, step - 1], axis, pairs)  15.2 us
    unnamed x73, local copies, waits for them, and re-layouts  10.3 us
  transfers between devices with their start and end apart: 69, of which 30 were waited for; matrix products, arithmetic and copies ran while one was open for 10% of the time, Pallas kernels for 16%

profile of v8, /device:TPU:0, one launch (start us, length us, event | category | flops | bytes accessed | tf_op | source)
XLA Modules:
  0.0 308.1 jit_solution(3327478065403739715)
XLA Ops:
  1.4 4.1 %collective-permute-start.6 = (f32[2,384]{1,0:T(2,128)S(1)}, f32[2,384]{1,0:T(2,128)S(1)}, u32[]{:S(2)}, u32[]{:S(2)}) collective-permute-start(f32[2,384]{1,0:T(2,128)S(1)} %get-tuple-element.234), channel_id=1, source_target_pairs={{0,2},{1,3},{2,0},{3,1},{4,6},{5,7},{6,4},{7,5},{8,10},{9,11},{10,... | collective-permute-start | bytes 9224 | tf_op jit(solution)/shard_map/ppermute | solution.py:297
  13.2 3.5 %convert_element_type.80 = bf16[2304,768]{1,0:T(8,128)(2,1)S(1)} convert(f32[2304,768]{1,0:T(8,128)} %refs_0_.9) | non-fusion elementwise | flops 1769472 | bytes 10616832 | tf_op jit(solution)/shard_map/convert_element_type | solution.py:304
  32.4 3.2 %collective-permute-done.13 = f32[48,768]{1,0:T(8,128)S(1)} collective-permute-done((f32[48,768]{1,0:T(8,128)S(1)}, f32[48,768]{1,0:T(8,128)S(1)}, u32[]{:S(2)}, u32[]{:S(2)}) %collective-permute-start.13) | collective-permute-done | bytes 147488 | tf_op jit(solution)/shard_map/ppermute | solution.py:214
  35.6 3.4 %collective-permute-done.15 = f32[48,768]{1,0:T(8,128)S(1)} collective-permute-done((f32[48,768]{1,0:T(8,128)S(1)}, f32[48,768]{1,0:T(8,128)S(1)}, u32[]{:S(2)}, u32[]{:S(2)}) %collective-permute-start.15) | collective-permute-done | bytes 147488 | tf_op jit(solution)/shard_map/ppermute | solution.py:214
  51.1 3.0 convolution_bitcast_fusion
  55.3 3.2 %collective-permute-start.8 = (bf16[384,2304]{1,0:T(8,128)(2,1)S(1)}, bf16[384,2304]{1,0:T(8,128)(2,1)S(1)}, u32[]{:S(2)}, u32[]{:S(2)}) collective-permute-start(bf16[384,2304]{1,0:T(8,128)(2,1)S(1)} %copy-done.19), channel_id=1, source_target_pairs={{0,1},{1,0},{2,3},{3,2},{4,5},{5,4},{6,7},{7,6},{8,9},{9,8},{10,11... | collective-permute-start | bytes 5308424 | tf_op jit(solution)/shard_map/ppermute | solution.py:184
  62.3 6.4 %collective-permute-done.21 = f32[2,48,768]{2,1,0:T(8,128)S(1)} collective-permute-done((f32[2,48,768]{2,1,0:T(8,128)S(1)}, f32[2,48,768]{2,1,0:T(8,128)S(1)}, u32[]{:S(2)}, u32[]{:S(2)}) %collective-permute-start.21) | collective-permute-done | bytes 294944 | tf_op jit(solution)/shard_map/ppermute | solution.py:214
  68.7 6.1 %collective-permute-done.23 = f32[2,48,768]{2,1,0:T(8,128)S(1)} collective-permute-done((f32[2,48,768]{2,1,0:T(8,128)S(1)}, f32[2,48,768]{2,1,0:T(8,128)S(1)}, u32[]{:S(2)}, u32[]{:S(2)}) %collective-permute-start.23) | collective-permute-done | bytes 294944 | tf_op jit(solution)/shard_map/ppermute | solution.py:214
  81.9 15.4 %collective-permute-done.8 = bf16[384,2304]{1,0:T(8,128)(2,1)S(1)} collective-permute-done((bf16[384,2304]{1,0:T(8,128)(2,1)S(1)}, bf16[384,2304]{1,0:T(8,128)(2,1)S(1)}, u32[]{:S(2)}, u32[]{:S(2)}) %collective-permute-start.8) | collective-permute-done | bytes 1769504 | tf_op jit(solution)/shard_map/ppermute | solution.py:184
  110.5 28.0 %collective-permute-done.2 = bf16[384,2304]{1,0:T(8,128)(2,1)} collective-permute-done((bf16[384,2304]{1,0:T(8,128)(2,1)}, bf16[384,2304]{1,0:T(8,128)(2,1)}, u32[]{:S(2)}, u32[]{:S(2)}) %collective-permute-start.2) | collective-permute-done | bytes 1769504 | tf_op jit(solution)/shard_map/ppermute | solution.py:184
  153.0 4.1 %shard_map.193 = (f32[768,1152]{1,0:T(8,128)S(1)}, f32[768,1152]{1,0:T(8,128)S(1)}, f32[768,1152]{1,0:T(8,128)S(1)}) custom-call(f32[768,2304]{1,0:T(8,128)} %refs_0_.7, f32[768,2304]{1,0:T(8,128)} %refs_1_.5, f32[768,2304]{1,0:T(8,128)} %refs_2_.5), custom_call_target="tpu_custom_call" | custom-call | bytes 10616832 | tf_op jit(solution)/shard_map/pallas_call | solution.py:74
  158.9 4.2 %shard_map.192 = (f32[768,1152]{1,0:T(8,128)S(1)}, f32[768,1152]{1,0:T(8,128)S(1)}, f32[768,1152]{1,0:T(8,128)S(1)}) custom-call(f32[768,2304]{1,0:T(8,128)} %refs_0_.7, f32[768,2304]{1,0:T(8,128)} %refs_1_.5, f32[768,2304]{1,0:T(8,128)} %refs_2_.5), custom_call_target="tpu_custom_call" | custom-call | bytes 10616832 | tf_op jit(solution)/shard_map/pallas_call | solution.py:74
  168.1 14.0 %collective-permute-done.10 = bf16[384,2304]{1,0:T(8,128)(2,1)S(1)} collective-permute-done((bf16[384,2304]{1,0:T(8,128)(2,1)}, bf16[384,2304]{1,0:T(8,128)(2,1)S(1)}, u32[]{:S(2)}, u32[]{:S(2)}) %collective-permute-start.10) | collective-permute-done | bytes 1769504 | tf_op jit(solution)/shard_map/ppermute | solution.py:184
  182.2 5.2 %shard_map.191.refs_2_ = f32[768,2304]{1,0:T(8,128)S(1)} custom-call(bf16[384,768]{1,0:T(8,128)(2,1)S(1)} %copy-done.6, bf16[384,768]{1,0:T(8,128)(2,1)S(1)} %get-tuple-element.194.refs_1_, bf16[384,2304]{1,0:T(8,128)(2,1)S(1)} %multiply_convert_fusion.1.refs_2_, bf16[384,2304]{1,0:T(8,128)(2,1)S(1)} %multiply_convert_fusion.2.refs_3_), custom_call_target="tpu_custom_call" | custom-call | flops 2717908992 | bytes 11796480 | tf_op jit(solution)/shard_map/pallas_call | solution.py:101
  191.1 7.9 %shard_map.190.refs_2_ = f32[2304,768]{1,0:T(8,128)S(1)} custom-call(bf16[384,2304]{1,0:T(8,128)(2,1)S(1)} %copy-done.8, bf16[384,2304]{1,0:T(8,128)(2,1)} %collective-permute-done.refs_1_, bf16[384,768]{1,0:T(8,128)(2,1)S(1)} %get-tuple-element.195.refs_2_, bf16[384,768]{1,0:T(8,128)(2,1)S(1)} %broadcast_select_fusion.7.refs_3_), custom_call_target="tpu_custom_call" | custom-call | flops 2717908992 | bytes 11796480 | tf_op jit(solution)/shard_map/pallas_call | solution.py:101
  238.1 3.6 %shard_map.195.grad = f32[768,2304]{1,0:T(8,128)S(1)} custom-call(bf16[384,768]{1,0:T(8,128)(2,1)S(1)} %broadcast_select_fusion.6.refs_0_, bf16[384,2304]{1,0:T(8,128)(2,1)S(1)} %multiply_convert_fusion.3.refs_1_, f32[768,2304]{1,0:T(8,128)S(1)} %shard_map.191.refs_2_), custom_call_target="tpu_custom_call", output_to_operand_aliasing={{}: (2, {})} | custom-call | flops 1358954496 | bytes 9437184 | tf_op jit(solution)/shard_map/pallas_call | solution.py:101
  241.7 3.9 %shard_map.194.grad = f32[2304,768]{1,0:T(8,128)S(1)} custom-call(bf16[384,2304]{1,0:T(8,128)(2,1)S(1)} %broadcast_select_fusion.refs_0_, bf16[384,768]{1,0:T(8,128)(2,1)S(1)} %broadcast_select_fusion.5.refs_1_, f32[2304,768]{1,0:T(8,128)S(1)} %shard_map.190.refs_2_), custom_call_target="tpu_custom_call", output_to_operand_aliasing={{}: (2, {})} | custom-call | flops 1358954496 | bytes 9437184 | tf_op jit(solution)/shard_map/pallas_call | solution.py:101
  249.3 7.5 %collective-permute-done.59 = bf16[384,2304]{1,0:T(8,128)(2,1)S(1)} collective-permute-done((bf16[384,2304]{1,0:T(8,128)(2,1)}, bf16[384,2304]{1,0:T(8,128)(2,1)S(1)}, u32[]{:S(2)}, u32[]{:S(2)}) %collective-permute-start.59) | collective-permute-done | bytes 1769504 | tf_op jit(solution)/shard_map/ppermute | solution.py:184
  266.9 6.5 %shard_map.196 = (f32[768,2304]{1,0:T(8,128)}, f32[768,2304]{1,0:T(8,128)}, f32[768,2304]{1,0:T(8,128)}) custom-call(bf16[384,768]{1,0:T(8,128)(2,1)S(1)} %broadcast_select_fusion.4.left, bf16[384,2304]{1,0:T(8,128)(2,1)S(1)} %multiply_convert_fusion.right, f32[768,2304]{1,0:T(8,128)S(1)} %shard_map.195.grad, f32[768,1152]{1,0:T(8,128)S(1)} %copy-done.3, ...), custom_call_target="tpu_custom_call" | custom-call | flops 679477248 | bytes 26247168 | tf_op jit(solution)/shard_map/pallas_call | solution.py:134
  277.0 4.2 %shard_map.197 = (f32[1152,768]{1,0:T(8,128)S(1)}, f32[1152,768]{1,0:T(8,128)S(1)}, f32[1152,768]{1,0:T(8,128)S(1)}) custom-call(f32[2304,768]{1,0:T(8,128)} %refs_0_.9, f32[2304,768]{1,0:T(8,128)} %refs_1_.7, f32[2304,768]{1,0:T(8,128)} %refs_2_.7, f32[768,2304]{1,0:T(8,128)} %get-tuple-element.100.refs_3_.refs_0_, ...), custom_call_target="tpu_custom_call" | custom-call | bytes 10616832 | tf_op jit(solution)/shard_map/pallas_call | solution.py:74
  282.1 6.5 %shard_map.198 = (f32[768,2304]{1,0:T(8,128)}, f32[768,2304]{1,0:T(8,128)}, f32[768,2304]{1,0:T(8,128)}) custom-call(bf16[384,768]{1,0:T(8,128)(2,1)S(1)} %broadcast_select_fusion.4.left, bf16[384,2304]{1,0:T(8,128)(2,1)S(1)} %multiply_convert_fusion.right, ...), custom_call_target="tpu_custom_call", output_to_operand_aliasing={{0}: (6, {}), {1}: (7, {}), {2}: (8, {})} | custom-call | flops 679477248 | bytes 26247168 | tf_op jit(solution)/shard_map/pallas_call | solution.py:134
  288.9 4.1 %shard_map.199 = (f32[1152,768]{1,0:T(8,128)S(1)}, f32[1152,768]{1,0:T(8,128)S(1)}, f32[1152,768]{1,0:T(8,128)S(1)}) custom-call(f32[2304,768]{1,0:T(8,128)} %refs_0_.9, f32[2304,768]{1,0:T(8,128)} %refs_1_.7, f32[2304,768]{1,0:T(8,128)} %refs_2_.7, f32[768,2304]{1,0:T(8,128)} %get-tuple-element.63.refs_3_, f32[768,2304]{1,0:T(8,128)} %get-tuple-element.64.refs_4_, ...), custom_call_target="tpu_custom_call" | custom-call | bytes 10616832 | tf_op jit(solution)/shard_map/pallas_call | solution.py:74
  293.3 7.5 %shard_map.200 = (f32[2304,768]{1,0:T(8,128)}, f32[2304,768]{1,0:T(8,128)}, f32[2304,768]{1,0:T(8,128)}) custom-call(bf16[384,2304]{1,0:T(8,128)(2,1)S(1)} %broadcast_select_fusion.1.left, bf16[384,768]{1,0:T(8,128)(2,1)S(1)} %broadcast_select_fusion.3.right, f32[2304,768]{1,0:T(8,128)S(1)} %shard_map.194.grad, f32[1152,768]{1,0:T(8,128)S(1)} %get-tuple-element.106.w, ...), custom_call_target="tpu_custom_call" | custom-call | flops 679477248 | bytes 26247168 | tf_op jit(solution)/shard_map/pallas_call | solution.py:134
  300.7 7.4 %shard_map.201 = (f32[2304,768]{1,0:T(8,128)}, f32[2304,768]{1,0:T(8,128)}, f32[2304,768]{1,0:T(8,128)}) custom-call(bf16[384,2304]{1,0:T(8,128)(2,1)S(1)} %broadcast_select_fusion.1.left, bf16[384,768]{1,0:T(8,128)(2,1)S(1)} %broadcast_select_fusion.3.right, ...), custom_call_target="tpu_custom_call", output_to_operand_aliasing={{0}: (6, {}), {1}: (7, {}), {2}: (8, {})} | custom-call | flops 679477248 | bytes 26247168 | tf_op jit(solution)/shard_map/pallas_call | solution.py:134
  (329 shorter events, 140.9 us)
Async XLA Ops:
  1.4 24.0 %collective-permute-start.6 = (f32[2,384]{1,0:T(2,128)S(1)}, f32[2,384]{1,0:T(2,128)S(1)}, u32[]{:S(2)}, u32[]{:S(2)}) collective-permute-start(f32[2,384]{1,0:T(2,128)S(1)} %get-tuple-element.234), channel_id=1, source_target_pairs={{0,2},{1,3},{2,0},{3,1},{4,6},{5,7},{6,4},{7,5},{8,10},{9,11},{10,... | collective-permute-start | bytes 9224 | tf_op jit(solution)/shard_map/ppermute | solution.py:297
  5.5 20.0 %collective-permute-start.5 = (f32[2,384]{1,0:T(2,128)S(1)}, f32[2,384]{1,0:T(2,128)S(1)}, u32[]{:S(2)}, u32[]{:S(2)}) collective-permute-start(f32[2,384]{1,0:T(2,128)S(1)} %get-tuple-element.234), channel_id=1, source_target_pairs={{0,1},{1,2},{2,3},{3,0},{4,5},{5,6},{6,7},{7,4},{8,9},{9,10},{10,1... | collective-permute-start | bytes 9224 | tf_op jit(solution)/shard_map/ppermute | solution.py:297
  7.1 18.5 %collective-permute-start.7 = (f32[2,384]{1,0:T(2,128)S(1)}, f32[2,384]{1,0:T(2,128)S(1)}, u32[]{:S(2)}, u32[]{:S(2)}) collective-permute-start(f32[2,384]{1,0:T(2,128)S(1)} %get-tuple-element.234), channel_id=1, source_target_pairs={{0,3},{1,0},{2,1},{3,2},{4,7},{5,4},{6,5},{7,6},{8,11},{9,8},{10,9... | collective-permute-start | bytes 9224 | tf_op jit(solution)/shard_map/ppermute | solution.py:297
  9.4 41.3 %collective-permute-start.1 = (bf16[384,2304]{1,0:T(8,128)(2,1)}, bf16[384,2304]{1,0:T(8,128)(2,1)}, u32[]{:S(2)}, u32[]{:S(2)}) collective-permute-start(bf16[384,2304]{1,0:T(8,128)(2,1)} %refs_0_.5), channel_id=1, source_target_pairs={{1,2},{2,1},{5,6},{6,5},{9,10},{10,9},{13,14},{14,13},{17,18},{18,... | collective-permute-start | bytes 5308424 | tf_op jit(solution)/shard_map/ppermute | solution.py:184
  11.3 39.8 %collective-permute-start = (bf16[384,2304]{1,0:T(8,128)(2,1)}, bf16[384,2304]{1,0:T(8,128)(2,1)}, u32[]{:S(2)}, u32[]{:S(2)}) collective-permute-start(bf16[384,2304]{1,0:T(8,128)(2,1)} %refs_0_.5), channel_id=1, source_target_pairs={{0,1},{1,0},{2,3},{3,2},{4,5},{5,4},{6,7},{7,6},{8,9},{9,8},{10,11... | collective-permute-start | bytes 5308424 | tf_op jit(solution)/shard_map/ppermute | solution.py:184
  54.5 26.1 %collective-permute-start.9 = (bf16[384,2304]{1,0:T(8,128)(2,1)S(1)}, bf16[384,2304]{1,0:T(8,128)(2,1)S(1)}, u32[]{:S(2)}, u32[]{:S(2)}) collective-permute-start(bf16[384,2304]{1,0:T(8,128)(2,1)S(1)} %copy-done.19), channel_id=1, source_target_pairs={{1,2},{2,1},{5,6},{6,5},{9,10},{10,9},{13,14},{14,13},{17,18},{18,... | collective-permute-start | bytes 5308424 | tf_op jit(solution)/shard_map/ppermute | solution.py:184
  55.3 42.0 %collective-permute-start.8 = (bf16[384,2304]{1,0:T(8,128)(2,1)S(1)}, bf16[384,2304]{1,0:T(8,128)(2,1)S(1)}, u32[]{:S(2)}, u32[]{:S(2)}) collective-permute-start(bf16[384,2304]{1,0:T(8,128)(2,1)S(1)} %copy-done.19), channel_id=1, source_target_pairs={{0,1},{1,0},{2,3},{3,2},{4,5},{5,4},{6,7},{7,6},{8,9},{9,8},{10,11... | collective-permute-start | bytes 5308424 | tf_op jit(solution)/shard_map/ppermute | solution.py:184
  59.8 15.0 %collective-permute-start.23 = (f32[2,48,768]{2,1,0:T(8,128)S(1)}, f32[2,48,768]{2,1,0:T(8,128)S(1)}, u32[]{:S(2)}, u32[]{:S(2)}) collective-permute-start(f32[2,48,768]{2,1,0:T(8,128)S(1)} %get-tuple-element.197), channel_id=1, source_target_pairs={{0,24},{4,28},{8,16},{12,20},{16,8},{20,12},{24,0},{28,4},{1,25},{... | collective-permute-start | bytes 884744 | tf_op jit(solution)/shard_map/ppermute | solution.py:214
  61.8 14.4 %collective-permute-start.22 = (f32[2,48,768]{2,1,0:T(8,128)S(1)}, f32[2,48,768]{2,1,0:T(8,128)S(1)}, u32[]{:S(2)}, u32[]{:S(2)}) collective-permute-start(f32[2,48,768]{2,1,0:T(8,128)S(1)} %get-tuple-element.198), channel_id=1, source_target_pairs={{0,16},{4,20},{8,24},{12,28},{16,0},{20,4},{24,8},{28,12},{1,17},{... | collective-permute-start | bytes 884744 | tf_op jit(solution)/shard_map/ppermute | solution.py:214
  77.0 22.2 %collective-permute-start.26 = (bf16[2,48,768]{2,1,0:T(8,128)(2,1)S(1)}, bf16[2,48,768]{2,1,0:T(8,128)(2,1)S(1)}, u32[]{:S(2)}, u32[]{:S(2)}) collective-permute-start(bf16[2,48,768]{2,1,0:T(8,128)(2,1)S(1)} %pad_maximum_fusion.8), channel_id=1, source_target_pairs={{0,8},{4,12},{8,0},{12,4},{16,24},{20,28},{24,16},{28,20},{1,9},{5... | collective-permute-start | bytes 442376 | tf_op jit(solution)/shard_map/ppermute | solution.py:214
  78.3 21.0 %collective-permute-start.25 = (bf16[2,48,768]{2,1,0:T(8,128)(2,1)S(1)}, bf16[2,48,768]{2,1,0:T(8,128)(2,1)S(1)}, u32[]{:S(2)}, u32[]{:S(2)}) collective-permute-start(bf16[2,48,768]{2,1,0:T(8,128)(2,1)S(1)} %pad_maximum_fusion.8), channel_id=1, source_target_pairs={{0,16},{4,20},{8,24},{12,28},{16,0},{20,4},{24,8},{28,12},{1,17},{... | collective-permute-start | bytes 442376 | tf_op jit(solution)/shard_map/ppermute | solution.py:214
  78.8 20.5 %collective-permute-start.24 = (bf16[2,48,768]{2,1,0:T(8,128)(2,1)S(1)}, bf16[2,48,768]{2,1,0:T(8,128)(2,1)S(1)}, u32[]{:S(2)}, u32[]{:S(2)}) collective-permute-start(bf16[2,48,768]{2,1,0:T(8,128)(2,1)S(1)} %pad_maximum_fusion.8), channel_id=1, source_target_pairs={{0,24},{4,28},{8,16},{12,20},{16,8},{20,12},{24,0},{28,4},{1,25},{... | collective-permute-start | bytes 442376 | tf_op jit(solution)/shard_map/ppermute | solution.py:214
  80.6 57.9 %collective-permute-start.2 = (bf16[384,2304]{1,0:T(8,128)(2,1)}, bf16[384,2304]{1,0:T(8,128)(2,1)}, u32[]{:S(2)}, u32[]{:S(2)}) collective-permute-start(bf16[384,2304]{1,0:T(8,128)(2,1)} %collective-permute-done.1), channel_id=1, source_target_pairs={{1,0},{2,3},{5,4},{6,7},{9,8},{10,11},{13,12},{14,15},{17,16},{18,... | collective-permute-start | bytes 5308424 | tf_op jit(solution)/shard_map/ppermute | solution.py:184
  97.3 42.5 %collective-permute-start.3 = (bf16[384,2304]{1,0:T(8,128)(2,1)}, bf16[384,2304]{1,0:T(8,128)(2,1)}, u32[]{:S(2)}, u32[]{:S(2)}) collective-permute-start(bf16[384,2304]{1,0:T(8,128)(2,1)} %collective-permute-done.refs_1_), channel_id=1, source_target_pairs={{1,2},{2,1},{5,6},{6,5},{9,10},{10,9},{13,14},{14,13},{17,18},{18,... | collective-permute-start | bytes 5308424 | tf_op jit(solution)/shard_map/ppermute | solution.py:184
  107.0 34.7 %collective-permute-start.29 = (f32[48,768]{1,0:T(8,128)}, f32[48,768]{1,0:T(8,128)}, u32[]{:S(2)}, u32[]{:S(2)}) collective-permute-start(f32[48,768]{1,0:T(8,128)} %get-tuple-element.211), channel_id=1, source_target_pairs={{0,8},{4,12},{8,0},{12,4},{16,24},{20,28},{24,16},{28,20},{1,9},{5... | collective-permute-start | bytes 442376 | tf_op jit(solution)/shard_map/ppermute | solution.py:214
  108.2 33.5 %collective-permute-start.31 = (f32[48,768]{1,0:T(8,128)}, f32[48,768]{1,0:T(8,128)}, u32[]{:S(2)}, u32[]{:S(2)}) collective-permute-start(f32[48,768]{1,0:T(8,128)} %get-tuple-element.212), channel_id=1, source_target_pairs={{0,24},{4,28},{8,16},{12,20},{16,8},{20,12},{24,0},{28,4},{1,25},{... | collective-permute-start | bytes 442376 | tf_op jit(solution)/shard_map/ppermute | solution.py:214
  110.0 31.7 %collective-permute-start.30 = (f32[48,768]{1,0:T(8,128)}, f32[48,768]{1,0:T(8,128)}, u32[]{:S(2)}, u32[]{:S(2)}) collective-permute-start(f32[48,768]{1,0:T(8,128)} %get-tuple-element.213), channel_id=1, source_target_pairs={{0,16},{4,20},{8,24},{12,28},{16,0},{20,4},{24,8},{28,12},{1,17},{... | collective-permute-start | bytes 442376 | tf_op jit(solution)/shard_map/ppermute | solution.py:214
  138.5 43.6 %collective-permute-start.10 = (bf16[384,2304]{1,0:T(8,128)(2,1)}, bf16[384,2304]{1,0:T(8,128)(2,1)S(1)}, u32[]{:S(2)}, u32[]{:S(2)}) collective-permute-start(bf16[384,2304]{1,0:T(8,128)(2,1)} %copy-done.20), channel_id=1, source_target_pairs={{1,0},{2,3},{5,4},{6,7},{9,8},{10,11},{13,12},{14,15},{17,16},{18,... | collective-permute-start | bytes 5308424 | tf_op jit(solution)/shard_map/ppermute | solution.py:184
  139.8 42.3 %collective-permute-start.11 = (bf16[384,2304]{1,0:T(8,128)(2,1)}, bf16[384,2304]{1,0:T(8,128)(2,1)}, u32[]{:S(2)}, u32[]{:S(2)}) collective-permute-start(bf16[384,2304]{1,0:T(8,128)(2,1)} %copy-done.22), channel_id=1, source_target_pairs={{1,2},{2,1},{5,6},{6,5},{9,10},{10,9},{13,14},{14,13},{17,18},{18,... | collective-permute-start | bytes 5308424 | tf_op jit(solution)/shard_map/ppermute | solution.py:184
  152.4 35.0 %collective-permute-start.36 = (f32[192,768]{1,0:T(8,128)S(1)}, f32[192,768]{1,0:T(8,128)S(1)}, u32[]{:S(2)}, u32[]{:S(2)}) collective-permute-start(f32[192,768]{1,0:T(8,128)S(1)} %constant_dynamic-slice_fusion.15), channel_id=1, source_target_pairs={{0,4},{4,0},{8,12},{12,8},{16,20},{20,16},{24,28},{28,24},{1,5},{5... | collective-permute-start | bytes 1769480 | tf_op jit(solution)/shard_map/ppermute | solution.py:214
  166.7 50.9 %collective-permute-start.4 = (bf16[384,2304]{1,0:T(8,128)(2,1)}, bf16[384,2304]{1,0:T(8,128)(2,1)S(1)}, u32[]{:S(2)}, u32[]{:S(2)}) collective-permute-start(bf16[384,2304]{1,0:T(8,128)(2,1)} %collective-permute-done.3), channel_id=1, source_target_pairs={{1,0},{2,3},{5,4},{6,7},{9,8},{10,11},{13,12},{14,15},{17,16},{18,... | collective-permute-start | bytes 5308424 | tf_op jit(solution)/shard_map/ppermute | solution.py:184
  214.5 42.3 %collective-permute-start.59 = (bf16[384,2304]{1,0:T(8,128)(2,1)}, bf16[384,2304]{1,0:T(8,128)(2,1)S(1)}, u32[]{:S(2)}, u32[]{:S(2)}) collective-permute-start(bf16[384,2304]{1,0:T(8,128)(2,1)} %collective-permute-done.11), channel_id=1, source_target_pairs={{1,0},{2,3},{5,4},{6,7},{9,8},{10,11},{13,12},{14,15},{17,16},{18,... | collective-permute-start | bytes 5308424 | tf_op jit(solution)/shard_map/ppermute | solution.py:184
  273.4 15.1 %collective-permute-start.67 = (bf16[48,768]{1,0:T(8,128)(2,1)S(1)}, bf16[48,768]{1,0:T(8,128)(2,1)S(1)}, u32[]{:S(2)}, u32[]{:S(2)}) collective-permute-start(bf16[48,768]{1,0:T(8,128)(2,1)S(1)} %multiply_convert_fusion.4), channel_id=1, source_target_pairs={{0,24},{4,28},{8,16},{12,20},{16,8},{20,12},{24,0},{28,4},{1,25},{... | collective-permute-start | bytes 221192 | tf_op jit(solution)/shard_map/ppermute | solution.py:214
  274.8 13.8 %collective-permute-start.66 = (bf16[48,768]{1,0:T(8,128)(2,1)S(1)}, bf16[48,768]{1,0:T(8,128)(2,1)S(1)}, u32[]{:S(2)}, u32[]{:S(2)}) collective-permute-start(bf16[48,768]{1,0:T(8,128)(2,1)S(1)} %multiply_convert_fusion.4), channel_id=1, source_target_pairs={{0,16},{4,20},{8,24},{12,28},{16,0},{20,4},{24,8},{28,12},{1,17},{... | collective-permute-start | bytes 221192 | tf_op jit(solution)/shard_map/ppermute | solution.py:214
  (71 other events, 438.6 us)

commit v9 on v7

--- a/solution.py
+++ b/solution.py
@@ -72,15 +72,15 @@
     shapes = [pltpu.VMEM((x.shape[0], x.shape[1] // parts), x.dtype) for x in arrays] * parts
     fetched = pl.pallas_call(
         functools.partial(fetch_kernel, parts),
-        in_specs=[pl.BlockSpec(memory_space=pl.ANY)] * len(arrays),
+        in_specs=[pl.BlockSpec(memory_space=pltpu.HBM)] * len(arrays),
         out_specs=[pl.BlockSpec(memory_space=pltpu.VMEM)] * len(shapes),
         out_shape=shapes,
         scratch_shapes=[pltpu.SemaphoreType.DMA((len(shapes),))],
-        compiler_params=pltpu.CompilerParams(vmem_limit_bytes=26 * 2**20),
+        compiler_params=pltpu.CompilerParams(vmem_limit_bytes=4 * 2**20),
         cost_estimate=pl.CostEstimate(
             flops=0, bytes_accessed=4 * sum(x.size for x in arrays), transcendentals=0
         ),
-    )(*arrays)
+    )(*[pltpu.with_memory_space_constraint(x, pltpu.HBM) for x in arrays])
     return [fetched[i : i + len(arrays)] for i in range(0, len(shapes), len(arrays))]
 
 
@@ -107,7 +107,7 @@
         out_specs=panel,
         out_shape=pltpu.VMEM((height, width), jnp.float32),
         input_output_aliases={2 * pieces + i: i for i in range(len(so_far))},
-        compiler_params=pltpu.CompilerParams(vmem_limit_bytes=20 * 2**20),
+        compiler_params=pltpu.CompilerParams(vmem_limit_bytes=16 * 2**20),
         cost_estimate=pl.CostEstimate(
             flops=2 * pieces * rows * height * width,
             bytes_accessed=4 * height * width + 2 * pieces * rows * (height + width),
@@ -116,31 +116,48 @@
     )(*lefts, *rights, *so_far)
 
 
-def update_kernel(left, right, grad, w, m, v, *refs):
-    new_w, new_m, new_v = refs[-3:]
-    total = grad[...] + over_rows(left[...], right[...])
-    new_w[...], new_m[...], new_v[...] = adamw(w[...], m[...], v[...], total)
-
-
-def update(left, right, grad, w, m, v, most, limit, part=0, parts=1, so_far=()):
+def update_kernel(resident, part, left, right, grad, w, m, v, *refs):
+    new_w, new_m, new_v, late = refs[-4:]
+    block, width = late.shape
+    count = 16 if width <= 768 else 8
+    late[...] = over_rows(left[...], right[...])
+
+    def some_rows(i, carry):
+        rows = pl.ds(pl.multiple_of(count * i, count), count)
+        far = pl.ds(pl.multiple_of(pl.program_id(0) * block + count * i, count), count)
+        own = far if resident else rows
+        total = grad[far, part * width : (part + 1) * width] + late[rows, :]
+        new_w[rows, :], new_m[rows, :], new_v[rows, :] = adamw(
+            w[own, :], m[own, :], v[own, :], total
+        )
+        return carry
+
+    lax.fori_loop(0, block // count, some_rows, 0, unroll=4)
+
+
+def update(left, right, grad, state, most, limit, resident, part=0, parts=1, so_far=()):
     rows, height = left.shape
     width = right.shape[1] // parts
     block = block_of(height, most)
     panel = pl.BlockSpec((block, width), lambda i: (i, part))
-    own = pl.BlockSpec((block, width), lambda i: (i, 0))
+    whole = pl.BlockSpec(memory_space=pltpu.VMEM)
+    own = whole if resident else pl.BlockSpec((block, width), lambda i: (i, 0))
     shape = jax.ShapeDtypeStruct((height, right.shape[1]), jnp.float32)
+    if resident:
+        state = [pltpu.with_memory_space_constraint(x, pltpu.VMEM) for x in state]
     return pl.pallas_call(
-        update_kernel,
+        functools.partial(update_kernel, resident, part),
         grid=(height // block,),
         in_specs=[
             pl.BlockSpec((rows, block), lambda i: (0, i)),
             pl.BlockSpec((rows, width), lambda i: (0, part)),
-            panel,
+            whole,
         ]
         + [own] * 3
         + [pl.BlockSpec(memory_space=pl.ANY)] * len(so_far),
         out_specs=[panel] * 3,
         out_shape=[shape] * 3,
+        scratch_shapes=[pltpu.VMEM((block, width), jnp.float32)],
         input_output_aliases={6 + i: i for i in range(len(so_far))},
         compiler_params=pltpu.CompilerParams(vmem_limit_bytes=limit * 2**20),
         cost_estimate=pl.CostEstimate(
@@ -148,7 +165,7 @@
             bytes_accessed=7 * 4 * height * width + 2 * rows * (height + width),
             transcendentals=2 * height * width,
         ),
-    )(left, right, grad, w, m, v, *so_far)
+    )(left, right, pltpu.with_memory_space_constraint(grad, pltpu.VMEM), *state, *so_far)
 
 
 def link_pairs(n, first, step):
@@ -326,7 +343,7 @@
         def run():
             nonlocal outs_out
             outs_out = update(
-                acts[-1], dys[-1], grad_out, *state_out[part], 128, 20, part, parts, outs_out
+                acts[-1], dys[-1], grad_out, state_out[part], 256, 16, True, part, parts, outs_out
             )
             return outs_out
 
@@ -369,7 +386,7 @@
     dpres.append(row_gather(chain(pre, back), "row", work))
     while work:
         work.pop(0)()
-    outs_in = update(token_slots[-1], dpres[-1], grad_in, w_in, m_in, v_in, 256, 42)
+    outs_in = update(token_slots[-1], dpres[-1], grad_in, (w_in, m_in, v_in), 256, 40, False)
     return (*outs_in, *outs_out)
 
 

time: 308 us -> 309 us (level)
  Pallas kernels: 59.3 us -> 63.6 us
  local copies, waits for them, and re-layouts: 16.6 us -> 12.3 us
    unnamed x95 -> x73, local copies, waits for them, and re-layouts: 11.1 us -> 7.65 us
    ppermute x56, waiting for transfers between devices: 52.1 us -> 48.9 us  [exchange(): lax.ppermute(part, axis, [(i, i ^ mask) for i in range(lax.axis_size(axis...]
where the time goes in v9:
time: 309 us; the launch traced here: 308 us
  waiting for transfers between devices  119 us (39%)
  starting transfers between devices  76 us (25%)
  Pallas kernels  63.6 us (21%)
  other arithmetic  19.8 us (6%)
  matrix products  13.9 us (4%)
  local copies, waits for them, and re-layouts  12.3 us (4%)
  between operations  4.03 us (1%)
    ppermute x10, waiting for transfers between devices, line_gather(): arrived[links, step] = lax.ppermute(came[1 - links, step - 1], axis, pairs)  69.8 us
    ppermute x56, starting transfers between devices, exchange(): lax.ppermute(part, axis, [(i, i ^ mask) for i in range(lax.axis_size(axis...  52.8 us
    ppermute x56, waiting for transfers between devices, exchange(): lax.ppermute(part, axis, [(i, i ^ mask) for i in range(lax.axis_size(axis...  48.9 us
    pallas_call x3, Pallas kernels, update(): pl.pallas_call(functools.partial(update_kernel, resident, part), grid=(he...  35.8 us
    pallas_call x4, Pallas kernels, grad_sum(): pl.pallas_call(functools.partial(grad_kernel, pieces), grid=(height // bl...  20.6 us
    ppermute x10, starting transfers between devices, line_gather(): arrived[links, step] = lax.ppermute(came[1 - links, step - 1], axis, pairs)  15.2 us
    ppermute x3, starting transfers between devices, on_device(): lax.ppermute(codes, 'col', [(i, (i + shift) % n) for i in range(n)])  7.93 us
    unnamed x73, local copies, waits for them, and re-layouts  7.65 us
  transfers between devices with their start and end apart: 69, of which 31 were waited for; matrix products, arithmetic and copies ran while one was open for 10% of the time, Pallas kernels for 13%

profile of v9, /device:TPU:0, one launch (start us, length us, event | category | flops | bytes accessed | tf_op | source)
XLA Modules:
  0.0 308.3 jit_solution(10608685776742134944)
XLA Ops:
  1.4 4.1 %collective-permute-start.6 = (f32[2,384]{1,0:T(2,128)S(1)}, f32[2,384]{1,0:T(2,128)S(1)}, u32[]{:S(2)}, u32[]{:S(2)}) collective-permute-start(f32[2,384]{1,0:T(2,128)S(1)} %get-tuple-element.214), channel_id=1, source_target_pairs={{0,2},{1,3},{2,0},{3,1},{4,6},{5,7},{6,4},{7,5},{8,10},{9,11},{10,... | collective-permute-start | bytes 9224 | tf_op jit(solution)/shard_map/ppermute | solution.py:312
  7.1 2.2 collective-permute-start.7
  13.2 3.5 %convert_element_type.80 = bf16[2304,768]{1,0:T(8,128)(2,1)S(1)} convert(f32[2304,768]{1,0:T(8,128)} %w.1) | non-fusion elementwise | flops 1769472 | bytes 10616832 | tf_op jit(solution)/shard_map/convert_element_type | solution.py:319
  18.2 2.1 convert_element_type.81
  32.4 3.2 %collective-permute-done.13 = f32[48,768]{1,0:T(8,128)S(1)} collective-permute-done((f32[48,768]{1,0:T(8,128)S(1)}, f32[48,768]{1,0:T(8,128)S(1)}, u32[]{:S(2)}, u32[]{:S(2)}) %collective-permute-start.13) | collective-permute-done | bytes 147488 | tf_op jit(solution)/shard_map/ppermute | solution.py:229
  35.6 3.4 %collective-permute-done.15 = f32[48,768]{1,0:T(8,128)S(1)} collective-permute-done((f32[48,768]{1,0:T(8,128)S(1)}, f32[48,768]{1,0:T(8,128)S(1)}, u32[]{:S(2)}, u32[]{:S(2)}) %collective-permute-start.15) | collective-permute-done | bytes 147488 | tf_op jit(solution)/shard_map/ppermute | solution.py:229
  51.1 3.0 convolution_bitcast_fusion
  55.3 3.2 %collective-permute-start.8 = (bf16[384,2304]{1,0:T(8,128)(2,1)S(1)}, bf16[384,2304]{1,0:T(8,128)(2,1)S(1)}, u32[]{:S(2)}, u32[]{:S(2)}) collective-permute-start(bf16[384,2304]{1,0:T(8,128)(2,1)S(1)} %copy-done.19), channel_id=1, source_target_pairs={{0,1},{1,0},{2,3},{3,2},{4,5},{5,4},{6,7},{7,6},{8,9},{9,8},{10,11... | collective-permute-start | bytes 5308424 | tf_op jit(solution)/shard_map/ppermute | solution.py:199
  62.3 6.4 %collective-permute-done.21 = f32[2,48,768]{2,1,0:T(8,128)S(1)} collective-permute-done((f32[2,48,768]{2,1,0:T(8,128)S(1)}, f32[2,48,768]{2,1,0:T(8,128)S(1)}, u32[]{:S(2)}, u32[]{:S(2)}) %collective-permute-start.21) | collective-permute-done | bytes 294944 | tf_op jit(solution)/shard_map/ppermute | solution.py:229
  68.7 6.1 %collective-permute-done.23 = f32[2,48,768]{2,1,0:T(8,128)S(1)} collective-permute-done((f32[2,48,768]{2,1,0:T(8,128)S(1)}, f32[2,48,768]{2,1,0:T(8,128)S(1)}, u32[]{:S(2)}, u32[]{:S(2)}) %collective-permute-start.23) | collective-permute-done | bytes 294944 | tf_op jit(solution)/shard_map/ppermute | solution.py:229
  81.9 15.4 %collective-permute-done.8 = bf16[384,2304]{1,0:T(8,128)(2,1)S(1)} collective-permute-done((bf16[384,2304]{1,0:T(8,128)(2,1)S(1)}, bf16[384,2304]{1,0:T(8,128)(2,1)S(1)}, u32[]{:S(2)}, u32[]{:S(2)}) %collective-permute-start.8) | collective-permute-done | bytes 1769504 | tf_op jit(solution)/shard_map/ppermute | solution.py:199
  110.5 28.0 %collective-permute-done.2 = bf16[384,2304]{1,0:T(8,128)(2,1)} collective-permute-done((bf16[384,2304]{1,0:T(8,128)(2,1)}, bf16[384,2304]{1,0:T(8,128)(2,1)}, u32[]{:S(2)}, u32[]{:S(2)}) %collective-permute-start.2) | collective-permute-done | bytes 1769504 | tf_op jit(solution)/shard_map/ppermute | solution.py:199
  153.0 7.2 %shard_map.192 = (f32[768,1152]{1,0:T(8,128)S(1)}, f32[768,1152]{1,0:T(8,128)S(1)}, f32[768,1152]{1,0:T(8,128)S(1)}, f32[768,1152]{1,0:T(8,128)S(1)}, f32[768,1152]{1,0:T(8,128)S(1)}, /*index=5*/f32[768,1152]{1,0:T(8,128)S(1)}) custom-call(f32[768,2304]{1,0:T(8,128)} %refs_0_.3, f32[768,2304]{1,0:T(8,128)} %refs_1_.1, f32[768,2304]{1,0:T(8,128)} %refs_2_.1), custom_call_target="tpu_custom_call" | custom-call | bytes 21233664 | tf_op jit(solution)/shard_map/pallas_call | solution.py:73
  165.2 16.9 %collective-permute-done.10 = bf16[384,2304]{1,0:T(8,128)(2,1)S(1)} collective-permute-done((bf16[384,2304]{1,0:T(8,128)(2,1)}, bf16[384,2304]{1,0:T(8,128)(2,1)S(1)}, u32[]{:S(2)}, u32[]{:S(2)}) %collective-permute-start.10) | collective-permute-done | bytes 1769504 | tf_op jit(solution)/shard_map/ppermute | solution.py:199
  182.2 5.2 %shard_map.191.refs_2_ = f32[768,2304]{1,0:T(8,128)S(1)} custom-call(bf16[384,768]{1,0:T(8,128)(2,1)S(1)} %copy-done.6, bf16[384,768]{1,0:T(8,128)(2,1)S(1)} %get-tuple-element.174.refs_1_, bf16[384,2304]{1,0:T(8,128)(2,1)S(1)} %multiply_convert_fusion.1.refs_2_, bf16[384,2304]{1,0:T(8,128)(2,1)S(1)} %multiply_convert_fusion.2.refs_3_), custom_call_target="tpu_custom_call" | custom-call | flops 2717908992 | bytes 11796480 | tf_op jit(solution)/shard_map/pallas_call | solution.py:101
  191.1 7.9 %shard_map.190.refs_2_ = f32[2304,768]{1,0:T(8,128)S(1)} custom-call(bf16[384,2304]{1,0:T(8,128)(2,1)S(1)} %copy-done.8, bf16[384,2304]{1,0:T(8,128)(2,1)} %collective-permute-done.refs_1_, bf16[384,768]{1,0:T(8,128)(2,1)S(1)} %get-tuple-element.175.refs_2_, bf16[384,768]{1,0:T(8,128)(2,1)S(1)} %broadcast_select_fusion.7.refs_3_), custom_call_target="tpu_custom_call" | custom-call | flops 2717908992 | bytes 11796480 | tf_op jit(solution)/shard_map/pallas_call | solution.py:101
  204.1 2.4 collective-permute-done.40
  217.7 2.6 collective-permute-done.47
  238.1 3.6 %shard_map.194.grad = f32[768,2304]{1,0:T(8,128)S(1)} custom-call(bf16[384,768]{1,0:T(8,128)(2,1)S(1)} %broadcast_select_fusion.6.refs_0_, bf16[384,2304]{1,0:T(8,128)(2,1)S(1)} %multiply_convert_fusion.3.refs_1_, f32[768,2304]{1,0:T(8,128)S(1)} %shard_map.191.refs_2_), custom_call_target="tpu_custom_call", output_to_operand_aliasing={{}: (2, {})} | custom-call | flops 1358954496 | bytes 9437184 | tf_op jit(solution)/shard_map/pallas_call | solution.py:101
  241.7 3.9 %shard_map.193.grad = f32[2304,768]{1,0:T(8,128)S(1)} custom-call(bf16[384,2304]{1,0:T(8,128)(2,1)S(1)} %broadcast_select_fusion.refs_0_, bf16[384,768]{1,0:T(8,128)(2,1)S(1)} %broadcast_select_fusion.5.refs_1_, f32[2304,768]{1,0:T(8,128)S(1)} %shard_map.190.refs_2_), custom_call_target="tpu_custom_call", output_to_operand_aliasing={{}: (2, {})} | custom-call | flops 1358954496 | bytes 9437184 | tf_op jit(solution)/shard_map/pallas_call | solution.py:101
  249.3 7.5 %collective-permute-done.59 = bf16[384,2304]{1,0:T(8,128)(2,1)S(1)} collective-permute-done((bf16[384,2304]{1,0:T(8,128)(2,1)}, bf16[384,2304]{1,0:T(8,128)(2,1)S(1)}, u32[]{:S(2)}, u32[]{:S(2)}) %collective-permute-start.59) | collective-permute-done | bytes 1769504 | tf_op jit(solution)/shard_map/ppermute | solution.py:199
  266.8 6.9 %shard_map.195 = (f32[768,2304]{1,0:T(8,128)}, f32[768,2304]{1,0:T(8,128)}, f32[768,2304]{1,0:T(8,128)}) custom-call(bf16[384,768]{1,0:T(8,128)(2,1)S(1)} %broadcast_select_fusion.4.left, bf16[384,2304]{1,0:T(8,128)(2,1)S(1)} %multiply_convert_fusion.right, f32[768,2304]{1,0:T(8,128)S(1)} %shard_map.194.grad, f32[768,1152]{1,0:T(8,128)S(1)} %copy-done.5, ...), custom_call_target="tpu_custom_call" | custom-call | flops 679477248 | bytes 26247168 | tf_op jit(solution)/shard_map/pallas_call | solution.py:148
  277.4 6.9 %shard_map.196 = (f32[768,2304]{1,0:T(8,128)}, f32[768,2304]{1,0:T(8,128)}, f32[768,2304]{1,0:T(8,128)}) custom-call(bf16[384,768]{1,0:T(8,128)(2,1)S(1)} %broadcast_select_fusion.4.left, bf16[384,2304]{1,0:T(8,128)(2,1)S(1)} %multiply_convert_fusion.right, ...), custom_call_target="tpu_custom_call", output_to_operand_aliasing={{0}: (6, {}), {1}: (7, {}), {2}: (8, {})} | custom-call | flops 679477248 | bytes 26247168 | tf_op jit(solution)/shard_map/pallas_call | solution.py:148
  286.3 22.0 %shard_map.197 = (f32[2304,768]{1,0:T(8,128)}, f32[2304,768]{1,0:T(8,128)}, f32[2304,768]{1,0:T(8,128)}) custom-call(bf16[384,2304]{1,0:T(8,128)(2,1)S(1)} %broadcast_select_fusion.1.left, bf16[384,768]{1,0:T(8,128)(2,1)S(1)} %broadcast_select_fusion.3.right, f32[2304,768]{1,0:T(8,128)S(1)} %shard_map.193.grad, f32[2304,768]{1,0:T(8,128)} %w.1, ...), custom_call_target="tpu_custom_call" | custom-call | flops 1358954496 | bytes 51904512 | tf_op jit(solution)/shard_map/pallas_call | solution.py:148
  (325 shorter events, 130.4 us)
Async XLA Ops:
  1.4 24.0 %collective-permute-start.6 = (f32[2,384]{1,0:T(2,128)S(1)}, f32[2,384]{1,0:T(2,128)S(1)}, u32[]{:S(2)}, u32[]{:S(2)}) collective-permute-start(f32[2,384]{1,0:T(2,128)S(1)} %get-tuple-element.214), channel_id=1, source_target_pairs={{0,2},{1,3},{2,0},{3,1},{4,6},{5,7},{6,4},{7,5},{8,10},{9,11},{10,... | collective-permute-start | bytes 9224 | tf_op jit(solution)/shard_map/ppermute | solution.py:312
  5.5 20.0 %collective-permute-start.5 = (f32[2,384]{1,0:T(2,128)S(1)}, f32[2,384]{1,0:T(2,128)S(1)}, u32[]{:S(2)}, u32[]{:S(2)}) collective-permute-start(f32[2,384]{1,0:T(2,128)S(1)} %get-tuple-element.214), channel_id=1, source_target_pairs={{0,1},{1,2},{2,3},{3,0},{4,5},{5,6},{6,7},{7,4},{8,9},{9,10},{10,1... | collective-permute-start | bytes 9224 | tf_op jit(solution)/shard_map/ppermute | solution.py:312
  7.1 18.4 %collective-permute-start.7 = (f32[2,384]{1,0:T(2,128)S(1)}, f32[2,384]{1,0:T(2,128)S(1)}, u32[]{:S(2)}, u32[]{:S(2)}) collective-permute-start(f32[2,384]{1,0:T(2,128)S(1)} %get-tuple-element.214), channel_id=1, source_target_pairs={{0,3},{1,0},{2,1},{3,2},{4,7},{5,4},{6,5},{7,6},{8,11},{9,8},{10,9... | collective-permute-start | bytes 9224 | tf_op jit(solution)/shard_map/ppermute | solution.py:312
  9.4 41.3 %collective-permute-start.1 = (bf16[384,2304]{1,0:T(8,128)(2,1)}, bf16[384,2304]{1,0:T(8,128)(2,1)}, u32[]{:S(2)}, u32[]{:S(2)}) collective-permute-start(bf16[384,2304]{1,0:T(8,128)(2,1)} %refs_0_.2), channel_id=1, source_target_pairs={{1,2},{2,1},{5,6},{6,5},{9,10},{10,9},{13,14},{14,13},{17,18},{18,... | collective-permute-start | bytes 5308424 | tf_op jit(solution)/shard_map/ppermute | solution.py:199
  11.2 39.8 %collective-permute-start = (bf16[384,2304]{1,0:T(8,128)(2,1)}, bf16[384,2304]{1,0:T(8,128)(2,1)}, u32[]{:S(2)}, u32[]{:S(2)}) collective-permute-start(bf16[384,2304]{1,0:T(8,128)(2,1)} %refs_0_.2), channel_id=1, source_target_pairs={{0,1},{1,0},{2,3},{3,2},{4,5},{5,4},{6,7},{7,6},{8,9},{9,8},{10,11... | collective-permute-start | bytes 5308424 | tf_op jit(solution)/shard_map/ppermute | solution.py:199
  54.5 26.1 %collective-permute-start.9 = (bf16[384,2304]{1,0:T(8,128)(2,1)S(1)}, bf16[384,2304]{1,0:T(8,128)(2,1)S(1)}, u32[]{:S(2)}, u32[]{:S(2)}) collective-permute-start(bf16[384,2304]{1,0:T(8,128)(2,1)S(1)} %copy-done.19), channel_id=1, source_target_pairs={{1,2},{2,1},{5,6},{6,5},{9,10},{10,9},{13,14},{14,13},{17,18},{18,... | collective-permute-start | bytes 5308424 | tf_op jit(solution)/shard_map/ppermute | solution.py:199
  55.3 42.0 %collective-permute-start.8 = (bf16[384,2304]{1,0:T(8,128)(2,1)S(1)}, bf16[384,2304]{1,0:T(8,128)(2,1)S(1)}, u32[]{:S(2)}, u32[]{:S(2)}) collective-permute-start(bf16[384,2304]{1,0:T(8,128)(2,1)S(1)} %copy-done.19), channel_id=1, source_target_pairs={{0,1},{1,0},{2,3},{3,2},{4,5},{5,4},{6,7},{7,6},{8,9},{9,8},{10,11... | collective-permute-start | bytes 5308424 | tf_op jit(solution)/shard_map/ppermute | solution.py:199
  59.8 15.0 %collective-permute-start.23 = (f32[2,48,768]{2,1,0:T(8,128)S(1)}, f32[2,48,768]{2,1,0:T(8,128)S(1)}, u32[]{:S(2)}, u32[]{:S(2)}) collective-permute-start(f32[2,48,768]{2,1,0:T(8,128)S(1)} %get-tuple-element.177), channel_id=1, source_target_pairs={{0,24},{4,28},{8,16},{12,20},{16,8},{20,12},{24,0},{28,4},{1,25},{... | collective-permute-start | bytes 884744 | tf_op jit(solution)/shard_map/ppermute | solution.py:229
  61.8 14.4 %collective-permute-start.22 = (f32[2,48,768]{2,1,0:T(8,128)S(1)}, f32[2,48,768]{2,1,0:T(8,128)S(1)}, u32[]{:S(2)}, u32[]{:S(2)}) collective-permute-start(f32[2,48,768]{2,1,0:T(8,128)S(1)} %get-tuple-element.178), channel_id=1, source_target_pairs={{0,16},{4,20},{8,24},{12,28},{16,0},{20,4},{24,8},{28,12},{1,17},{... | collective-permute-start | bytes 884744 | tf_op jit(solution)/shard_map/ppermute | solution.py:229
  77.0 22.3 %collective-permute-start.26 = (bf16[2,48,768]{2,1,0:T(8,128)(2,1)S(1)}, bf16[2,48,768]{2,1,0:T(8,128)(2,1)S(1)}, u32[]{:S(2)}, u32[]{:S(2)}) collective-permute-start(bf16[2,48,768]{2,1,0:T(8,128)(2,1)S(1)} %pad_maximum_fusion.8), channel_id=1, source_target_pairs={{0,8},{4,12},{8,0},{12,4},{16,24},{20,28},{24,16},{28,20},{1,9},{5... | collective-permute-start | bytes 442376 | tf_op jit(solution)/shard_map/ppermute | solution.py:229
  78.3 21.0 %collective-permute-start.25 = (bf16[2,48,768]{2,1,0:T(8,128)(2,1)S(1)}, bf16[2,48,768]{2,1,0:T(8,128)(2,1)S(1)}, u32[]{:S(2)}, u32[]{:S(2)}) collective-permute-start(bf16[2,48,768]{2,1,0:T(8,128)(2,1)S(1)} %pad_maximum_fusion.8), channel_id=1, source_target_pairs={{0,16},{4,20},{8,24},{12,28},{16,0},{20,4},{24,8},{28,12},{1,17},{... | collective-permute-start | bytes 442376 | tf_op jit(solution)/shard_map/ppermute | solution.py:229
  78.8 20.5 %collective-permute-start.24 = (bf16[2,48,768]{2,1,0:T(8,128)(2,1)S(1)}, bf16[2,48,768]{2,1,0:T(8,128)(2,1)S(1)}, u32[]{:S(2)}, u32[]{:S(2)}) collective-permute-start(bf16[2,48,768]{2,1,0:T(8,128)(2,1)S(1)} %pad_maximum_fusion.8), channel_id=1, source_target_pairs={{0,24},{4,28},{8,16},{12,20},{16,8},{20,12},{24,0},{28,4},{1,25},{... | collective-permute-start | bytes 442376 | tf_op jit(solution)/shard_map/ppermute | solution.py:229
  80.6 57.9 %collective-permute-start.2 = (bf16[384,2304]{1,0:T(8,128)(2,1)}, bf16[384,2304]{1,0:T(8,128)(2,1)}, u32[]{:S(2)}, u32[]{:S(2)}) collective-permute-start(bf16[384,2304]{1,0:T(8,128)(2,1)} %collective-permute-done.1), channel_id=1, source_target_pairs={{1,0},{2,3},{5,4},{6,7},{9,8},{10,11},{13,12},{14,15},{17,16},{18,... | collective-permute-start | bytes 5308424 | tf_op jit(solution)/shard_map/ppermute | solution.py:199
  97.3 42.5 %collective-permute-start.3 = (bf16[384,2304]{1,0:T(8,128)(2,1)}, bf16[384,2304]{1,0:T(8,128)(2,1)}, u32[]{:S(2)}, u32[]{:S(2)}) collective-permute-start(bf16[384,2304]{1,0:T(8,128)(2,1)} %collective-permute-done.refs_1_), channel_id=1, source_target_pairs={{1,2},{2,1},{5,6},{6,5},{9,10},{10,9},{13,14},{14,13},{17,18},{18,... | collective-permute-start | bytes 5308424 | tf_op jit(solution)/shard_map/ppermute | solution.py:199
  107.0 34.7 %collective-permute-start.29 = (f32[48,768]{1,0:T(8,128)}, f32[48,768]{1,0:T(8,128)}, u32[]{:S(2)}, u32[]{:S(2)}) collective-permute-start(f32[48,768]{1,0:T(8,128)} %get-tuple-element.191), channel_id=1, source_target_pairs={{0,8},{4,12},{8,0},{12,4},{16,24},{20,28},{24,16},{28,20},{1,9},{5... | collective-permute-start | bytes 442376 | tf_op jit(solution)/shard_map/ppermute | solution.py:229
  108.2 33.5 %collective-permute-start.31 = (f32[48,768]{1,0:T(8,128)}, f32[48,768]{1,0:T(8,128)}, u32[]{:S(2)}, u32[]{:S(2)}) collective-permute-start(f32[48,768]{1,0:T(8,128)} %get-tuple-element.192), channel_id=1, source_target_pairs={{0,24},{4,28},{8,16},{12,20},{16,8},{20,12},{24,0},{28,4},{1,25},{... | collective-permute-start | bytes 442376 | tf_op jit(solution)/shard_map/ppermute | solution.py:229
  110.0 31.7 %collective-permute-start.30 = (f32[48,768]{1,0:T(8,128)}, f32[48,768]{1,0:T(8,128)}, u32[]{:S(2)}, u32[]{:S(2)}) collective-permute-start(f32[48,768]{1,0:T(8,128)} %get-tuple-element.193), channel_id=1, source_target_pairs={{0,16},{4,20},{8,24},{12,28},{16,0},{20,4},{24,8},{28,12},{1,17},{... | collective-permute-start | bytes 442376 | tf_op jit(solution)/shard_map/ppermute | solution.py:229
  138.5 43.6 %collective-permute-start.10 = (bf16[384,2304]{1,0:T(8,128)(2,1)}, bf16[384,2304]{1,0:T(8,128)(2,1)S(1)}, u32[]{:S(2)}, u32[]{:S(2)}) collective-permute-start(bf16[384,2304]{1,0:T(8,128)(2,1)} %copy-done.20), channel_id=1, source_target_pairs={{1,0},{2,3},{5,4},{6,7},{9,8},{10,11},{13,12},{14,15},{17,16},{18,... | collective-permute-start | bytes 5308424 | tf_op jit(solution)/shard_map/ppermute | solution.py:199
  139.8 42.3 %collective-permute-start.11 = (bf16[384,2304]{1,0:T(8,128)(2,1)}, bf16[384,2304]{1,0:T(8,128)(2,1)}, u32[]{:S(2)}, u32[]{:S(2)}) collective-permute-start(bf16[384,2304]{1,0:T(8,128)(2,1)} %copy-done.22), channel_id=1, source_target_pairs={{1,2},{2,1},{5,6},{6,5},{9,10},{10,9},{13,14},{14,13},{17,18},{18,... | collective-permute-start | bytes 5308424 | tf_op jit(solution)/shard_map/ppermute | solution.py:199
  152.5 35.0 %collective-permute-start.36 = (f32[192,768]{1,0:T(8,128)S(1)}, f32[192,768]{1,0:T(8,128)S(1)}, u32[]{:S(2)}, u32[]{:S(2)}) collective-permute-start(f32[192,768]{1,0:T(8,128)S(1)} %constant_dynamic-slice_fusion.15), channel_id=1, source_target_pairs={{0,4},{4,0},{8,12},{12,8},{16,20},{20,16},{24,28},{28,24},{1,5},{5... | collective-permute-start | bytes 1769480 | tf_op jit(solution)/shard_map/ppermute | solution.py:229
  163.8 53.8 %collective-permute-start.4 = (bf16[384,2304]{1,0:T(8,128)(2,1)}, bf16[384,2304]{1,0:T(8,128)(2,1)S(1)}, u32[]{:S(2)}, u32[]{:S(2)}) collective-permute-start(bf16[384,2304]{1,0:T(8,128)(2,1)} %collective-permute-done.3), channel_id=1, source_target_pairs={{1,0},{2,3},{5,4},{6,7},{9,8},{10,11},{13,12},{14,15},{17,16},{18,... | collective-permute-start | bytes 5308424 | tf_op jit(solution)/shard_map/ppermute | solution.py:199
  187.6 11.5 %collective-permute-start.39 = (f32[48,768]{1,0:T(8,128)S(1)}, f32[48,768]{1,0:T(8,128)S(1)}, u32[]{:S(2)}, u32[]{:S(2)}) collective-permute-start(f32[48,768]{1,0:T(8,128)S(1)} %get-tuple-element.188), channel_id=1, source_target_pairs={{0,24},{4,28},{8,16},{12,20},{16,8},{20,12},{24,0},{28,4},{1,25},{... | collective-permute-start | bytes 442376 | tf_op jit(solution)/shard_map/ppermute | solution.py:229
  214.5 42.3 %collective-permute-start.59 = (bf16[384,2304]{1,0:T(8,128)(2,1)}, bf16[384,2304]{1,0:T(8,128)(2,1)S(1)}, u32[]{:S(2)}, u32[]{:S(2)}) collective-permute-start(bf16[384,2304]{1,0:T(8,128)(2,1)} %collective-permute-done.11), channel_id=1, source_target_pairs={{1,0},{2,3},{5,4},{6,7},{9,8},{10,11},{13,12},{14,15},{17,16},{18,... | collective-permute-start | bytes 5308424 | tf_op jit(solution)/shard_map/ppermute | solution.py:199
  234.5 11.1 %collective-permute-start.55 = (f32[48,768]{1,0:T(8,128)S(1)}, f32[48,768]{1,0:T(8,128)S(1)}, u32[]{:S(2)}, u32[]{:S(2)}) collective-permute-start(f32[48,768]{1,0:T(8,128)S(1)} %get-tuple-element.182), channel_id=1, source_target_pairs={{0,24},{4,28},{8,16},{12,20},{16,8},{20,12},{24,0},{28,4},{1,25},{... | collective-permute-start | bytes 442376 | tf_op jit(solution)/shard_map/ppermute | solution.py:229
  (71 other events, 469.6 us)

commit v10 on v7

--- a/solution.py
+++ b/solution.py
@@ -72,15 +72,15 @@
     shapes = [pltpu.VMEM((x.shape[0], x.shape[1] // parts), x.dtype) for x in arrays] * parts
     fetched = pl.pallas_call(
         functools.partial(fetch_kernel, parts),
-        in_specs=[pl.BlockSpec(memory_space=pl.ANY)] * len(arrays),
+        in_specs=[pl.BlockSpec(memory_space=pltpu.HBM)] * len(arrays),
         out_specs=[pl.BlockSpec(memory_space=pltpu.VMEM)] * len(shapes),
         out_shape=shapes,
         scratch_shapes=[pltpu.SemaphoreType.DMA((len(shapes),))],
-        compiler_params=pltpu.CompilerParams(vmem_limit_bytes=26 * 2**20),
+        compiler_params=pltpu.CompilerParams(vmem_limit_bytes=4 * 2**20),
         cost_estimate=pl.CostEstimate(
             flops=0, bytes_accessed=4 * sum(x.size for x in arrays), transcendentals=0
         ),
-    )(*arrays)
+    )(*[pltpu.with_memory_space_constraint(x, pltpu.HBM) for x in arrays])
     return [fetched[i : i + len(arrays)] for i in range(0, len(shapes), len(arrays))]
 
 
@@ -107,7 +107,7 @@
         out_specs=panel,
         out_shape=pltpu.VMEM((height, width), jnp.float32),
         input_output_aliases={2 * pieces + i: i for i in range(len(so_far))},
-        compiler_params=pltpu.CompilerParams(vmem_limit_bytes=20 * 2**20),
+        compiler_params=pltpu.CompilerParams(vmem_limit_bytes=16 * 2**20),
         cost_estimate=pl.CostEstimate(
             flops=2 * pieces * rows * height * width,
             bytes_accessed=4 * height * width + 2 * pieces * rows * (height + width),
@@ -233,7 +233,7 @@
     return functools.reduce(jnp.add, came, piece_of(place))
 
 
-def row_gather(part, axis, beside=None):
+def row_gather(part, axis, beside=None, seen=None):
     here = lax.axis_index(axis)
     others = lax.axis_size(axis) // 2
     odd, place = here % 2, here // 2
@@ -247,6 +247,8 @@
         ]
         bit *= 2
     part = jnp.concatenate(pieces, axis=-2)
+    if seen is not None:
+        seen.append(part)
     came = exchange(part, axis, 1, beside)
     return jnp.where(
         odd == 1,
@@ -326,7 +328,7 @@
         def run():
             nonlocal outs_out
             outs_out = update(
-                acts[-1], dys[-1], grad_out, *state_out[part], 128, 20, part, parts, outs_out
+                acts[-1], dys[-1], grad_out, *state_out[part], 128, 16, part, parts, outs_out
             )
             return outs_out
 
@@ -355,7 +357,7 @@
                 grad_out = grad_sum(acts[-1:], dys[-1:], 128, (grad_out,))
                 beside, latest = [None, (grad_in, grad_out)], [out_grads_came[slot]]
             pre = row_sum(after(pre_of(token_slots[slot]), last), "row", beside)
-            last = row_gather(square(pre), "row", latest)
+            last = row_gather(square(pre), "row", latest, seen := [])
             acts.append(last)
         if slot < n - 1:
             dys.append(scaled(out_grad_slots[slot], owners[slot]))
@@ -363,7 +365,7 @@
             last = row_gather(chain(pre, row_sum(back, "row")), "row")
             dpres.append(last)
 
-    dys.append(scaled(out_grad_slots[n - 1], owners[n - 1], acts[-1]))
+    dys.append(scaled(out_grad_slots[n - 1], owners[n - 1], seen))
     work = [None] + [update_part(part) for part in range(parts)]
     back = row_sum(against(dys[n - 1], w_out16), "row", work)
     dpres.append(row_gather(chain(pre, back), "row", work))

time: 308 us -> 305 us (level)
  local copies, waits for them, and re-layouts: 16.6 us -> 12.3 us
    ppermute x56, waiting for transfers between devices: 52.1 us -> 47.1 us  [exchange(): lax.ppermute(part, axis, [(i, i ^ mask) for i in range(lax.axis_size(axis...]
    unnamed x95 -> x77, local copies, waits for them, and re-layouts: 11.1 us -> 7.66 us
  transfers between devices with their start and end apart: 69 -> 69, of which waited for: 31 -> 30; matrix products, arithmetic and copies ran while one was open for 10% -> 11% of each run, Pallas kernels for 13% -> 13%
where the time goes in v10:
time: 305 us; the launch traced here: 304 us
  waiting for transfers between devices  117 us (38%)
  starting transfers between devices  76.3 us (25%)
  Pallas kernels  61 us (20%)
  other arithmetic  19.7 us (6%)
  matrix products  13.9 us (5%)
  local copies, waits for them, and re-layouts  12.3 us (4%)
  between operations  4.07 us (1%)
    ppermute x10, waiting for transfers between devices, line_gather(): arrived[links, step] = lax.ppermute(came[1 - links, step - 1], axis, pairs)  69.7 us
    ppermute x56, starting transfers between devices, exchange(): lax.ppermute(part, axis, [(i, i ^ mask) for i in range(lax.axis_size(axis...  53.2 us
    ppermute x56, waiting for transfers between devices, exchange(): lax.ppermute(part, axis, [(i, i ^ mask) for i in range(lax.axis_size(axis...  47.1 us
    pallas_call x3, Pallas kernels, update(): pl.pallas_call(update_kernel, grid=(height // block,), in_specs=[pl.Block...  33.2 us
    pallas_call x4, Pallas kernels, grad_sum(): pl.pallas_call(functools.partial(grad_kernel, pieces), grid=(height // bl...  20.6 us
    ppermute x10, starting transfers between devices, line_gather(): arrived[links, step] = lax.ppermute(came[1 - links, step - 1], axis, pairs)  15.2 us
    ppermute x3, starting transfers between devices, on_device(): lax.ppermute(codes, 'col', [(i, (i + shift) % n) for i in range(n)])  7.93 us
    unnamed x77, local copies, waits for them, and re-layouts  7.66 us
  transfers between devices with their start and end apart: 69, of which 30 were waited for; matrix products, arithmetic and copies ran while one was open for 11% of the time, Pallas kernels for 13%

profile of v10, /device:TPU:0, one launch (start us, length us, event | category | flops | bytes accessed | tf_op | source)
XLA Modules:
  0.0 304.3 jit_solution(11771640959126735868)
XLA Ops:
  1.4 4.1 %collective-permute-start.6 = (f32[2,384]{1,0:T(2,128)S(1)}, f32[2,384]{1,0:T(2,128)S(1)}, u32[]{:S(2)}, u32[]{:S(2)}) collective-permute-start(f32[2,384]{1,0:T(2,128)S(1)} %get-tuple-element.214), channel_id=1, source_target_pairs={{0,2},{1,3},{2,0},{3,1},{4,6},{5,7},{6,4},{7,5},{8,10},{9,11},{10,... | collective-permute-start | bytes 9224 | tf_op jit(solution)/shard_map/ppermute | solution.py:297
  7.1 2.2 collective-permute-start.7
  13.2 3.5 %convert_element_type.80 = bf16[2304,768]{1,0:T(8,128)(2,1)S(1)} convert(f32[2304,768]{1,0:T(8,128)} %w.1) | non-fusion elementwise | flops 1769472 | bytes 10616832 | tf_op jit(solution)/shard_map/convert_element_type | solution.py:304
  18.2 2.1 convert_element_type.81
  32.5 3.2 %collective-permute-done.13 = f32[48,768]{1,0:T(8,128)S(1)} collective-permute-done((f32[48,768]{1,0:T(8,128)S(1)}, f32[48,768]{1,0:T(8,128)S(1)}, u32[]{:S(2)}, u32[]{:S(2)}) %collective-permute-start.13) | collective-permute-done | bytes 147488 | tf_op jit(solution)/shard_map/ppermute | solution.py:212
  35.6 3.4 %collective-permute-done.15 = f32[48,768]{1,0:T(8,128)S(1)} collective-permute-done((f32[48,768]{1,0:T(8,128)S(1)}, f32[48,768]{1,0:T(8,128)S(1)}, u32[]{:S(2)}, u32[]{:S(2)}) %collective-permute-start.15) | collective-permute-done | bytes 147488 | tf_op jit(solution)/shard_map/ppermute | solution.py:212
  51.1 3.0 convolution_bitcast_fusion
  55.3 3.2 %collective-permute-start.8 = (bf16[384,2304]{1,0:T(8,128)(2,1)S(1)}, bf16[384,2304]{1,0:T(8,128)(2,1)S(1)}, u32[]{:S(2)}, u32[]{:S(2)}) collective-permute-start(bf16[384,2304]{1,0:T(8,128)(2,1)S(1)} %copy-done.19), channel_id=1, source_target_pairs={{0,1},{1,0},{2,3},{3,2},{4,5},{5,4},{6,7},{7,6},{8,9},{9,8},{10,11... | collective-permute-start | bytes 5308424 | tf_op jit(solution)/shard_map/ppermute | solution.py:182
  62.3 6.4 %collective-permute-done.21 = f32[2,48,768]{2,1,0:T(8,128)S(1)} collective-permute-done((f32[2,48,768]{2,1,0:T(8,128)S(1)}, f32[2,48,768]{2,1,0:T(8,128)S(1)}, u32[]{:S(2)}, u32[]{:S(2)}) %collective-permute-start.21) | collective-permute-done | bytes 294944 | tf_op jit(solution)/shard_map/ppermute | solution.py:212
  68.8 6.1 %collective-permute-done.23 = f32[2,48,768]{2,1,0:T(8,128)S(1)} collective-permute-done((f32[2,48,768]{2,1,0:T(8,128)S(1)}, f32[2,48,768]{2,1,0:T(8,128)S(1)}, u32[]{:S(2)}, u32[]{:S(2)}) %collective-permute-start.23) | collective-permute-done | bytes 294944 | tf_op jit(solution)/shard_map/ppermute | solution.py:212
  81.9 15.4 %collective-permute-done.8 = bf16[384,2304]{1,0:T(8,128)(2,1)S(1)} collective-permute-done((bf16[384,2304]{1,0:T(8,128)(2,1)S(1)}, bf16[384,2304]{1,0:T(8,128)(2,1)S(1)}, u32[]{:S(2)}, u32[]{:S(2)}) %collective-permute-start.8) | collective-permute-done | bytes 1769504 | tf_op jit(solution)/shard_map/ppermute | solution.py:182
  110.5 28.0 %collective-permute-done.2 = bf16[384,2304]{1,0:T(8,128)(2,1)} collective-permute-done((bf16[384,2304]{1,0:T(8,128)(2,1)}, bf16[384,2304]{1,0:T(8,128)(2,1)}, u32[]{:S(2)}, u32[]{:S(2)}) %collective-permute-start.2) | collective-permute-done | bytes 1769504 | tf_op jit(solution)/shard_map/ppermute | solution.py:182
  153.1 7.2 %shard_map.192 = (f32[768,1152]{1,0:T(8,128)S(1)}, f32[768,1152]{1,0:T(8,128)S(1)}, f32[768,1152]{1,0:T(8,128)S(1)}, f32[768,1152]{1,0:T(8,128)S(1)}, f32[768,1152]{1,0:T(8,128)S(1)}, /*index=5*/f32[768,1152]{1,0:T(8,128)S(1)}) custom-call(f32[768,2304]{1,0:T(8,128)} %refs_0_.3, f32[768,2304]{1,0:T(8,128)} %refs_1_.1, f32[768,2304]{1,0:T(8,128)} %refs_2_.1), custom_call_target="tpu_custom_call" | custom-call | bytes 21233664 | tf_op jit(solution)/shard_map/pallas_call | solution.py:73
  165.2 16.9 %collective-permute-done.10 = bf16[384,2304]{1,0:T(8,128)(2,1)S(1)} collective-permute-done((bf16[384,2304]{1,0:T(8,128)(2,1)}, bf16[384,2304]{1,0:T(8,128)(2,1)S(1)}, u32[]{:S(2)}, u32[]{:S(2)}) %collective-permute-start.10) | collective-permute-done | bytes 1769504 | tf_op jit(solution)/shard_map/ppermute | solution.py:182
  182.3 5.2 %shard_map.191.refs_2_ = f32[768,2304]{1,0:T(8,128)S(1)} custom-call(bf16[384,768]{1,0:T(8,128)(2,1)S(1)} %copy-done.6, bf16[384,768]{1,0:T(8,128)(2,1)S(1)} %get-tuple-element.174.refs_1_, bf16[384,2304]{1,0:T(8,128)(2,1)S(1)} %multiply_convert_fusion.1.refs_2_, bf16[384,2304]{1,0:T(8,128)(2,1)S(1)} %multiply_convert_fusion.2.refs_3_), custom_call_target="tpu_custom_call" | custom-call | flops 2717908992 | bytes 11796480 | tf_op jit(solution)/shard_map/pallas_call | solution.py:101
  191.2 7.9 %shard_map.190.refs_2_ = f32[2304,768]{1,0:T(8,128)S(1)} custom-call(bf16[384,2304]{1,0:T(8,128)(2,1)S(1)} %copy-done.8, bf16[384,2304]{1,0:T(8,128)(2,1)} %collective-permute-done.refs_1_, bf16[384,768]{1,0:T(8,128)(2,1)S(1)} %get-tuple-element.175.refs_2_, bf16[384,768]{1,0:T(8,128)(2,1)S(1)} %broadcast_select_fusion.7.refs_3_), custom_call_target="tpu_custom_call" | custom-call | flops 2717908992 | bytes 11796480 | tf_op jit(solution)/shard_map/pallas_call | solution.py:101
  204.2 2.4 collective-permute-done.40
  217.8 2.6 collective-permute-done.47
  238.2 3.6 %shard_map.194.grad = f32[768,2304]{1,0:T(8,128)S(1)} custom-call(bf16[384,768]{1,0:T(8,128)(2,1)S(1)} %broadcast_select_fusion.6.refs_0_, bf16[384,2304]{1,0:T(8,128)(2,1)S(1)} %multiply_convert_fusion.3.refs_1_, f32[768,2304]{1,0:T(8,128)S(1)} %shard_map.191.refs_2_), custom_call_target="tpu_custom_call", output_to_operand_aliasing={{}: (2, {})} | custom-call | flops 1358954496 | bytes 9437184 | tf_op jit(solution)/shard_map/pallas_call | solution.py:101
  241.8 3.9 %shard_map.193.grad = f32[2304,768]{1,0:T(8,128)S(1)} custom-call(bf16[384,2304]{1,0:T(8,128)(2,1)S(1)} %broadcast_select_fusion.refs_0_, bf16[384,768]{1,0:T(8,128)(2,1)S(1)} %broadcast_select_fusion.5.refs_1_, f32[2304,768]{1,0:T(8,128)S(1)} %shard_map.190.refs_2_), custom_call_target="tpu_custom_call", output_to_operand_aliasing={{}: (2, {})} | custom-call | flops 1358954496 | bytes 9437184 | tf_op jit(solution)/shard_map/pallas_call | solution.py:101
  249.4 7.5 %collective-permute-done.59 = bf16[384,2304]{1,0:T(8,128)(2,1)S(1)} collective-permute-done((bf16[384,2304]{1,0:T(8,128)(2,1)}, bf16[384,2304]{1,0:T(8,128)(2,1)S(1)}, u32[]{:S(2)}, u32[]{:S(2)}) %collective-permute-start.59) | collective-permute-done | bytes 1769504 | tf_op jit(solution)/shard_map/ppermute | solution.py:182
  265.3 6.6 %shard_map.195 = (f32[768,2304]{1,0:T(8,128)}, f32[768,2304]{1,0:T(8,128)}, f32[768,2304]{1,0:T(8,128)}) custom-call(bf16[384,768]{1,0:T(8,128)(2,1)S(1)} %broadcast_select_fusion.4.left, bf16[384,2304]{1,0:T(8,128)(2,1)S(1)} %multiply_convert_fusion.right, f32[768,2304]{1,0:T(8,128)S(1)} %shard_map.194.grad, f32[768,1152]{1,0:T(8,128)S(1)} %copy-done.5, ...), custom_call_target="tpu_custom_call" | custom-call | flops 679477248 | bytes 26247168 | tf_op jit(solution)/shard_map/pallas_call | solution.py:132
  275.5 6.5 %shard_map.196 = (f32[768,2304]{1,0:T(8,128)}, f32[768,2304]{1,0:T(8,128)}, f32[768,2304]{1,0:T(8,128)}) custom-call(bf16[384,768]{1,0:T(8,128)(2,1)S(1)} %broadcast_select_fusion.4.left, bf16[384,2304]{1,0:T(8,128)(2,1)S(1)} %multiply_convert_fusion.right, ...), custom_call_target="tpu_custom_call", output_to_operand_aliasing={{0}: (6, {}), {1}: (7, {}), {2}: (8, {})} | custom-call | flops 679477248 | bytes 26247168 | tf_op jit(solution)/shard_map/pallas_call | solution.py:132
  284.1 20.1 %shard_map.197 = (f32[2304,768]{1,0:T(8,128)}, f32[2304,768]{1,0:T(8,128)}, f32[2304,768]{1,0:T(8,128)}) custom-call(bf16[384,2304]{1,0:T(8,128)(2,1)S(1)} %broadcast_select_fusion.1.left, bf16[384,768]{1,0:T(8,128)(2,1)S(1)} %broadcast_select_fusion.3.right, f32[2304,768]{1,0:T(8,128)S(1)} %shard_map.193.grad, f32[2304,768]{1,0:T(8,128)} %w.1, ...), custom_call_target="tpu_custom_call" | custom-call | flops 1358954496 | bytes 51904512 | tf_op jit(solution)/shard_map/pallas_call | solution.py:132
  (329 shorter events, 128.8 us)
Async XLA Ops:
  1.4 24.1 %collective-permute-start.6 = (f32[2,384]{1,0:T(2,128)S(1)}, f32[2,384]{1,0:T(2,128)S(1)}, u32[]{:S(2)}, u32[]{:S(2)}) collective-permute-start(f32[2,384]{1,0:T(2,128)S(1)} %get-tuple-element.214), channel_id=1, source_target_pairs={{0,2},{1,3},{2,0},{3,1},{4,6},{5,7},{6,4},{7,5},{8,10},{9,11},{10,... | collective-permute-start | bytes 9224 | tf_op jit(solution)/shard_map/ppermute | solution.py:297
  5.5 20.1 %collective-permute-start.5 = (f32[2,384]{1,0:T(2,128)S(1)}, f32[2,384]{1,0:T(2,128)S(1)}, u32[]{:S(2)}, u32[]{:S(2)}) collective-permute-start(f32[2,384]{1,0:T(2,128)S(1)} %get-tuple-element.214), channel_id=1, source_target_pairs={{0,1},{1,2},{2,3},{3,0},{4,5},{5,6},{6,7},{7,4},{8,9},{9,10},{10,1... | collective-permute-start | bytes 9224 | tf_op jit(solution)/shard_map/ppermute | solution.py:297
  7.1 18.5 %collective-permute-start.7 = (f32[2,384]{1,0:T(2,128)S(1)}, f32[2,384]{1,0:T(2,128)S(1)}, u32[]{:S(2)}, u32[]{:S(2)}) collective-permute-start(f32[2,384]{1,0:T(2,128)S(1)} %get-tuple-element.214), channel_id=1, source_target_pairs={{0,3},{1,0},{2,1},{3,2},{4,7},{5,4},{6,5},{7,6},{8,11},{9,8},{10,9... | collective-permute-start | bytes 9224 | tf_op jit(solution)/shard_map/ppermute | solution.py:297
  9.4 41.4 %collective-permute-start.1 = (bf16[384,2304]{1,0:T(8,128)(2,1)}, bf16[384,2304]{1,0:T(8,128)(2,1)}, u32[]{:S(2)}, u32[]{:S(2)}) collective-permute-start(bf16[384,2304]{1,0:T(8,128)(2,1)} %refs_0_.2), channel_id=1, source_target_pairs={{1,2},{2,1},{5,6},{6,5},{9,10},{10,9},{13,14},{14,13},{17,18},{18,... | collective-permute-start | bytes 5308424 | tf_op jit(solution)/shard_map/ppermute | solution.py:182
  11.3 39.8 %collective-permute-start = (bf16[384,2304]{1,0:T(8,128)(2,1)}, bf16[384,2304]{1,0:T(8,128)(2,1)}, u32[]{:S(2)}, u32[]{:S(2)}) collective-permute-start(bf16[384,2304]{1,0:T(8,128)(2,1)} %refs_0_.2), channel_id=1, source_target_pairs={{0,1},{1,0},{2,3},{3,2},{4,5},{5,4},{6,7},{7,6},{8,9},{9,8},{10,11... | collective-permute-start | bytes 5308424 | tf_op jit(solution)/shard_map/ppermute | solution.py:182
  54.5 26.1 %collective-permute-start.9 = (bf16[384,2304]{1,0:T(8,128)(2,1)S(1)}, bf16[384,2304]{1,0:T(8,128)(2,1)S(1)}, u32[]{:S(2)}, u32[]{:S(2)}) collective-permute-start(bf16[384,2304]{1,0:T(8,128)(2,1)S(1)} %copy-done.19), channel_id=1, source_target_pairs={{1,2},{2,1},{5,6},{6,5},{9,10},{10,9},{13,14},{14,13},{17,18},{18,... | collective-permute-start | bytes 5308424 | tf_op jit(solution)/shard_map/ppermute | solution.py:182
  55.3 42.0 %collective-permute-start.8 = (bf16[384,2304]{1,0:T(8,128)(2,1)S(1)}, bf16[384,2304]{1,0:T(8,128)(2,1)S(1)}, u32[]{:S(2)}, u32[]{:S(2)}) collective-permute-start(bf16[384,2304]{1,0:T(8,128)(2,1)S(1)} %copy-done.19), channel_id=1, source_target_pairs={{0,1},{1,0},{2,3},{3,2},{4,5},{5,4},{6,7},{7,6},{8,9},{9,8},{10,11... | collective-permute-start | bytes 5308424 | tf_op jit(solution)/shard_map/ppermute | solution.py:182
  59.8 15.1 %collective-permute-start.23 = (f32[2,48,768]{2,1,0:T(8,128)S(1)}, f32[2,48,768]{2,1,0:T(8,128)S(1)}, u32[]{:S(2)}, u32[]{:S(2)}) collective-permute-start(f32[2,48,768]{2,1,0:T(8,128)S(1)} %get-tuple-element.177), channel_id=1, source_target_pairs={{0,24},{4,28},{8,16},{12,20},{16,8},{20,12},{24,0},{28,4},{1,25},{... | collective-permute-start | bytes 884744 | tf_op jit(solution)/shard_map/ppermute | solution.py:212
  61.8 14.4 %collective-permute-start.22 = (f32[2,48,768]{2,1,0:T(8,128)S(1)}, f32[2,48,768]{2,1,0:T(8,128)S(1)}, u32[]{:S(2)}, u32[]{:S(2)}) collective-permute-start(f32[2,48,768]{2,1,0:T(8,128)S(1)} %get-tuple-element.178), channel_id=1, source_target_pairs={{0,16},{4,20},{8,24},{12,28},{16,0},{20,4},{24,8},{28,12},{1,17},{... | collective-permute-start | bytes 884744 | tf_op jit(solution)/shard_map/ppermute | solution.py:212
  77.1 22.2 %collective-permute-start.26 = (bf16[2,48,768]{2,1,0:T(8,128)(2,1)S(1)}, bf16[2,48,768]{2,1,0:T(8,128)(2,1)S(1)}, u32[]{:S(2)}, u32[]{:S(2)}) collective-permute-start(bf16[2,48,768]{2,1,0:T(8,128)(2,1)S(1)} %pad_maximum_fusion.8), channel_id=1, source_target_pairs={{0,8},{4,12},{8,0},{12,4},{16,24},{20,28},{24,16},{28,20},{1,9},{5... | collective-permute-start | bytes 442376 | tf_op jit(solution)/shard_map/ppermute | solution.py:212
  78.3 21.0 %collective-permute-start.25 = (bf16[2,48,768]{2,1,0:T(8,128)(2,1)S(1)}, bf16[2,48,768]{2,1,0:T(8,128)(2,1)S(1)}, u32[]{:S(2)}, u32[]{:S(2)}) collective-permute-start(bf16[2,48,768]{2,1,0:T(8,128)(2,1)S(1)} %pad_maximum_fusion.8), channel_id=1, source_target_pairs={{0,16},{4,20},{8,24},{12,28},{16,0},{20,4},{24,8},{28,12},{1,17},{... | collective-permute-start | bytes 442376 | tf_op jit(solution)/shard_map/ppermute | solution.py:212
  78.8 20.5 %collective-permute-start.24 = (bf16[2,48,768]{2,1,0:T(8,128)(2,1)S(1)}, bf16[2,48,768]{2,1,0:T(8,128)(2,1)S(1)}, u32[]{:S(2)}, u32[]{:S(2)}) collective-permute-start(bf16[2,48,768]{2,1,0:T(8,128)(2,1)S(1)} %pad_maximum_fusion.8), channel_id=1, source_target_pairs={{0,24},{4,28},{8,16},{12,20},{16,8},{20,12},{24,0},{28,4},{1,25},{... | collective-permute-start | bytes 442376 | tf_op jit(solution)/shard_map/ppermute | solution.py:212
  80.6 57.9 %collective-permute-start.2 = (bf16[384,2304]{1,0:T(8,128)(2,1)}, bf16[384,2304]{1,0:T(8,128)(2,1)}, u32[]{:S(2)}, u32[]{:S(2)}) collective-permute-start(bf16[384,2304]{1,0:T(8,128)(2,1)} %collective-permute-done.1), channel_id=1, source_target_pairs={{1,0},{2,3},{5,4},{6,7},{9,8},{10,11},{13,12},{14,15},{17,16},{18,... | collective-permute-start | bytes 5308424 | tf_op jit(solution)/shard_map/ppermute | solution.py:182
  97.4 42.5 %collective-permute-start.3 = (bf16[384,2304]{1,0:T(8,128)(2,1)}, bf16[384,2304]{1,0:T(8,128)(2,1)}, u32[]{:S(2)}, u32[]{:S(2)}) collective-permute-start(bf16[384,2304]{1,0:T(8,128)(2,1)} %collective-permute-done.refs_1_), channel_id=1, source_target_pairs={{1,2},{2,1},{5,6},{6,5},{9,10},{10,9},{13,14},{14,13},{17,18},{18,... | collective-permute-start | bytes 5308424 | tf_op jit(solution)/shard_map/ppermute | solution.py:182
  107.0 34.7 %collective-permute-start.29 = (f32[48,768]{1,0:T(8,128)}, f32[48,768]{1,0:T(8,128)}, u32[]{:S(2)}, u32[]{:S(2)}) collective-permute-start(f32[48,768]{1,0:T(8,128)} %get-tuple-element.191), channel_id=1, source_target_pairs={{0,8},{4,12},{8,0},{12,4},{16,24},{20,28},{24,16},{28,20},{1,9},{5... | collective-permute-start | bytes 442376 | tf_op jit(solution)/shard_map/ppermute | solution.py:212
  108.2 33.6 %collective-permute-start.31 = (f32[48,768]{1,0:T(8,128)}, f32[48,768]{1,0:T(8,128)}, u32[]{:S(2)}, u32[]{:S(2)}) collective-permute-start(f32[48,768]{1,0:T(8,128)} %get-tuple-element.192), channel_id=1, source_target_pairs={{0,24},{4,28},{8,16},{12,20},{16,8},{20,12},{24,0},{28,4},{1,25},{... | collective-permute-start | bytes 442376 | tf_op jit(solution)/shard_map/ppermute | solution.py:212
  110.0 31.7 %collective-permute-start.30 = (f32[48,768]{1,0:T(8,128)}, f32[48,768]{1,0:T(8,128)}, u32[]{:S(2)}, u32[]{:S(2)}) collective-permute-start(f32[48,768]{1,0:T(8,128)} %get-tuple-element.193), channel_id=1, source_target_pairs={{0,16},{4,20},{8,24},{12,28},{16,0},{20,4},{24,8},{28,12},{1,17},{... | collective-permute-start | bytes 442376 | tf_op jit(solution)/shard_map/ppermute | solution.py:212
  138.5 43.6 %collective-permute-start.10 = (bf16[384,2304]{1,0:T(8,128)(2,1)}, bf16[384,2304]{1,0:T(8,128)(2,1)S(1)}, u32[]{:S(2)}, u32[]{:S(2)}) collective-permute-start(bf16[384,2304]{1,0:T(8,128)(2,1)} %copy-done.20), channel_id=1, source_target_pairs={{1,0},{2,3},{5,4},{6,7},{9,8},{10,11},{13,12},{14,15},{17,16},{18,... | collective-permute-start | bytes 5308424 | tf_op jit(solution)/shard_map/ppermute | solution.py:182
  139.8 42.3 %collective-permute-start.11 = (bf16[384,2304]{1,0:T(8,128)(2,1)}, bf16[384,2304]{1,0:T(8,128)(2,1)}, u32[]{:S(2)}, u32[]{:S(2)}) collective-permute-start(bf16[384,2304]{1,0:T(8,128)(2,1)} %copy-done.22), channel_id=1, source_target_pairs={{1,2},{2,1},{5,6},{6,5},{9,10},{10,9},{13,14},{14,13},{17,18},{18,... | collective-permute-start | bytes 5308424 | tf_op jit(solution)/shard_map/ppermute | solution.py:182
  152.5 35.0 %collective-permute-start.36 = (f32[192,768]{1,0:T(8,128)S(1)}, f32[192,768]{1,0:T(8,128)S(1)}, u32[]{:S(2)}, u32[]{:S(2)}) collective-permute-start(f32[192,768]{1,0:T(8,128)S(1)} %constant_dynamic-slice_fusion.15), channel_id=1, source_target_pairs={{0,4},{4,0},{8,12},{12,8},{16,20},{20,16},{24,28},{28,24},{1,5},{5... | collective-permute-start | bytes 1769480 | tf_op jit(solution)/shard_map/ppermute | solution.py:212
  163.8 53.8 %collective-permute-start.4 = (bf16[384,2304]{1,0:T(8,128)(2,1)}, bf16[384,2304]{1,0:T(8,128)(2,1)S(1)}, u32[]{:S(2)}, u32[]{:S(2)}) collective-permute-start(bf16[384,2304]{1,0:T(8,128)(2,1)} %collective-permute-done.3), channel_id=1, source_target_pairs={{1,0},{2,3},{5,4},{6,7},{9,8},{10,11},{13,12},{14,15},{17,16},{18,... | collective-permute-start | bytes 5308424 | tf_op jit(solution)/shard_map/ppermute | solution.py:182
  187.7 11.5 %collective-permute-start.39 = (f32[48,768]{1,0:T(8,128)S(1)}, f32[48,768]{1,0:T(8,128)S(1)}, u32[]{:S(2)}, u32[]{:S(2)}) collective-permute-start(f32[48,768]{1,0:T(8,128)S(1)} %get-tuple-element.188), channel_id=1, source_target_pairs={{0,24},{4,28},{8,16},{12,20},{16,8},{20,12},{24,0},{28,4},{1,25},{... | collective-permute-start | bytes 442376 | tf_op jit(solution)/shard_map/ppermute | solution.py:212
  214.7 42.2 %collective-permute-start.59 = (bf16[384,2304]{1,0:T(8,128)(2,1)}, bf16[384,2304]{1,0:T(8,128)(2,1)S(1)}, u32[]{:S(2)}, u32[]{:S(2)}) collective-permute-start(bf16[384,2304]{1,0:T(8,128)(2,1)} %collective-permute-done.11), channel_id=1, source_target_pairs={{1,0},{2,3},{5,4},{6,7},{9,8},{10,11},{13,12},{14,15},{17,16},{18,... | collective-permute-start | bytes 5308424 | tf_op jit(solution)/shard_map/ppermute | solution.py:182
  234.6 11.1 %collective-permute-start.55 = (f32[48,768]{1,0:T(8,128)S(1)}, f32[48,768]{1,0:T(8,128)S(1)}, u32[]{:S(2)}, u32[]{:S(2)}) collective-permute-start(f32[48,768]{1,0:T(8,128)S(1)} %get-tuple-element.182), channel_id=1, source_target_pairs={{0,24},{4,28},{8,16},{12,20},{16,8},{20,12},{24,0},{28,4},{1,25},{... | collective-permute-start | bytes 442376 | tf_op jit(solution)/shard_map/ppermute | solution.py:212
  (73 other events, 482.6 us)

commit v11 on v10

--- a/solution.py
+++ b/solution.py
@@ -337,8 +337,8 @@
     dys = [scaled(out_grad, here)]
     pre = row_sum(pre_of(tokens), "row")
     acts, dpres = [row_gather(square(pre), "row")], []
-    both = jnp.stack([against(dys[0], w_out16), pre_of(token_slots[1])])
-    both = row_sum(after(both, (acts[0], tokens_came[1])), "row")
+    both = [against(dys[0], w_out16), pre_of(token_slots[1])]
+    both = row_sum(jnp.stack(after(both, (acts[0], tokens_came[1]))), "row")
     both, pre = jnp.stack([chain(pre, both[0]), square(both[1])]), both[1]
     last = both = row_gather(both, "row")
     acts.append(both[1])

time: 305 us -> 305 us (level)
  no operation moved by 1% of the time
where the time goes in v11:
time: 305 us; the launch traced here: 304 us
  waiting for transfers between devices  117 us (38%)
  starting transfers between devices  76.3 us (25%)
  Pallas kernels  61 us (20%)
  other arithmetic  19.8 us (6%)
  matrix products  13.9 us (5%)
  local copies, waits for them, and re-layouts  12.2 us (4%)
  between operations  4.05 us (1%)
    ppermute x10, waiting for transfers between devices, line_gather(): arrived[links, step] = lax.ppermute(came[1 - links, step - 1], axis, pairs)  69.7 us
    ppermute x56, starting transfers between devices, exchange(): lax.ppermute(part, axis, [(i, i ^ mask) for i in range(lax.axis_size(axis...  53.1 us
    ppermute x56, waiting for transfers between devices, exchange(): lax.ppermute(part, axis, [(i, i ^ mask) for i in range(lax.axis_size(axis...  47.1 us
    pallas_call x3, Pallas kernels, update(): pl.pallas_call(update_kernel, grid=(height // block,), in_specs=[pl.Block...  33.2 us
    pallas_call x4, Pallas kernels, grad_sum(): pl.pallas_call(functools.partial(grad_kernel, pieces), grid=(height // bl...  20.6 us
    ppermute x10, starting transfers between devices, line_gather(): arrived[links, step] = lax.ppermute(came[1 - links, step - 1], axis, pairs)  15.2 us
    ppermute x3, starting transfers between devices, on_device(): lax.ppermute(codes, 'col', [(i, (i + shift) % n) for i in range(n)])  7.93 us
    unnamed x77, local copies, waits for them, and re-layouts  7.66 us
  transfers between devices with their start and end apart: 69, of which 30 were waited for; matrix products, arithmetic and copies ran while one was open for 11% of the time, Pallas kernels for 13%

profile of v11, /device:TPU:0, one launch (start us, length us, event | category | flops | bytes accessed | tf_op | source)
XLA Modules:
  0.0 304.1 jit_solution(15519144177198827627)
XLA Ops:
  1.4 4.1 %collective-permute-start.6 = (f32[2,384]{1,0:T(2,128)S(1)}, f32[2,384]{1,0:T(2,128)S(1)}, u32[]{:S(2)}, u32[]{:S(2)}) collective-permute-start(f32[2,384]{1,0:T(2,128)S(1)} %get-tuple-element.216), channel_id=1, source_target_pairs={{0,2},{1,3},{2,0},{3,1},{4,6},{5,7},{6,4},{7,5},{8,10},{9,11},{10,... | collective-permute-start | bytes 9224 | tf_op jit(solution)/shard_map/ppermute | solution.py:297
  7.1 2.2 collective-permute-start.7
  13.2 3.5 %convert_element_type.80 = bf16[2304,768]{1,0:T(8,128)(2,1)S(1)} convert(f32[2304,768]{1,0:T(8,128)} %w.1) | non-fusion elementwise | flops 1769472 | bytes 10616832 | tf_op jit(solution)/shard_map/convert_element_type | solution.py:304
  18.2 2.1 convert_element_type.81
  32.5 3.2 %collective-permute-done.13 = f32[48,768]{1,0:T(8,128)S(1)} collective-permute-done((f32[48,768]{1,0:T(8,128)S(1)}, f32[48,768]{1,0:T(8,128)S(1)}, u32[]{:S(2)}, u32[]{:S(2)}) %collective-permute-start.13) | collective-permute-done | bytes 147488 | tf_op jit(solution)/shard_map/ppermute | solution.py:212
  35.6 3.4 %collective-permute-done.15 = f32[48,768]{1,0:T(8,128)S(1)} collective-permute-done((f32[48,768]{1,0:T(8,128)S(1)}, f32[48,768]{1,0:T(8,128)S(1)}, u32[]{:S(2)}, u32[]{:S(2)}) %collective-permute-start.15) | collective-permute-done | bytes 147488 | tf_op jit(solution)/shard_map/ppermute | solution.py:212
  51.1 3.0 fusion.28
  55.2 3.2 %collective-permute-start.8 = (bf16[384,2304]{1,0:T(8,128)(2,1)S(1)}, bf16[384,2304]{1,0:T(8,128)(2,1)S(1)}, u32[]{:S(2)}, u32[]{:S(2)}) collective-permute-start(bf16[384,2304]{1,0:T(8,128)(2,1)S(1)} %copy-done.19), channel_id=1, source_target_pairs={{0,1},{1,0},{2,3},{3,2},{4,5},{5,4},{6,7},{7,6},{8,9},{9,8},{10,11... | collective-permute-start | bytes 5308424 | tf_op jit(solution)/shard_map/ppermute | solution.py:182
  62.3 6.4 %collective-permute-done.21 = f32[2,48,768]{2,1,0:T(8,128)S(1)} collective-permute-done((f32[2,48,768]{2,1,0:T(8,128)S(1)}, f32[2,48,768]{2,1,0:T(8,128)S(1)}, u32[]{:S(2)}, u32[]{:S(2)}) %collective-permute-start.21) | collective-permute-done | bytes 294944 | tf_op jit(solution)/shard_map/ppermute | solution.py:212
  68.7 6.1 %collective-permute-done.23 = f32[2,48,768]{2,1,0:T(8,128)S(1)} collective-permute-done((f32[2,48,768]{2,1,0:T(8,128)S(1)}, f32[2,48,768]{2,1,0:T(8,128)S(1)}, u32[]{:S(2)}, u32[]{:S(2)}) %collective-permute-start.23) | collective-permute-done | bytes 294944 | tf_op jit(solution)/shard_map/ppermute | solution.py:212
  81.9 15.4 %collective-permute-done.8 = bf16[384,2304]{1,0:T(8,128)(2,1)S(1)} collective-permute-done((bf16[384,2304]{1,0:T(8,128)(2,1)S(1)}, bf16[384,2304]{1,0:T(8,128)(2,1)S(1)}, u32[]{:S(2)}, u32[]{:S(2)}) %collective-permute-start.8) | collective-permute-done | bytes 1769504 | tf_op jit(solution)/shard_map/ppermute | solution.py:182
  110.4 28.0 %collective-permute-done.2 = bf16[384,2304]{1,0:T(8,128)(2,1)} collective-permute-done((bf16[384,2304]{1,0:T(8,128)(2,1)}, bf16[384,2304]{1,0:T(8,128)(2,1)}, u32[]{:S(2)}, u32[]{:S(2)}) %collective-permute-start.2) | collective-permute-done | bytes 1769504 | tf_op jit(solution)/shard_map/ppermute | solution.py:182
  153.0 7.2 %shard_map.192 = (f32[768,1152]{1,0:T(8,128)S(1)}, f32[768,1152]{1,0:T(8,128)S(1)}, f32[768,1152]{1,0:T(8,128)S(1)}, f32[768,1152]{1,0:T(8,128)S(1)}, f32[768,1152]{1,0:T(8,128)S(1)}, /*index=5*/f32[768,1152]{1,0:T(8,128)S(1)}) custom-call(f32[768,2304]{1,0:T(8,128)} %refs_0_.3, f32[768,2304]{1,0:T(8,128)} %refs_1_.1, f32[768,2304]{1,0:T(8,128)} %refs_2_.1), custom_call_target="tpu_custom_call" | custom-call | bytes 21233664 | tf_op jit(solution)/shard_map/pallas_call | solution.py:73
  165.1 16.9 %collective-permute-done.10 = bf16[384,2304]{1,0:T(8,128)(2,1)S(1)} collective-permute-done((bf16[384,2304]{1,0:T(8,128)(2,1)}, bf16[384,2304]{1,0:T(8,128)(2,1)S(1)}, u32[]{:S(2)}, u32[]{:S(2)}) %collective-permute-start.10) | collective-permute-done | bytes 1769504 | tf_op jit(solution)/shard_map/ppermute | solution.py:182
  182.2 5.2 %shard_map.191.refs_2_ = f32[768,2304]{1,0:T(8,128)S(1)} custom-call(bf16[384,768]{1,0:T(8,128)(2,1)S(1)} %copy-done.6, bf16[384,768]{1,0:T(8,128)(2,1)S(1)} %get-tuple-element.176.refs_1_, bf16[384,2304]{1,0:T(8,128)(2,1)S(1)} %multiply_convert_fusion.1.refs_2_, bf16[384,2304]{1,0:T(8,128)(2,1)S(1)} %multiply_convert_fusion.2.refs_3_), custom_call_target="tpu_custom_call" | custom-call | flops 2717908992 | bytes 11796480 | tf_op jit(solution)/shard_map/pallas_call | solution.py:101
  191.1 7.9 %shard_map.190.refs_2_ = f32[2304,768]{1,0:T(8,128)S(1)} custom-call(bf16[384,2304]{1,0:T(8,128)(2,1)S(1)} %copy-done.8, bf16[384,2304]{1,0:T(8,128)(2,1)} %collective-permute-done.refs_1_, bf16[384,768]{1,0:T(8,128)(2,1)S(1)} %get-tuple-element.177.refs_2_, bf16[384,768]{1,0:T(8,128)(2,1)S(1)} %broadcast_select_fusion.7.refs_3_), custom_call_target="tpu_custom_call" | custom-call | flops 2717908992 | bytes 11796480 | tf_op jit(solution)/shard_map/pallas_call | solution.py:101
  204.1 2.4 collective-permute-done.40
  217.7 2.6 collective-permute-done.47
  238.1 3.6 %shard_map.194.grad = f32[768,2304]{1,0:T(8,128)S(1)} custom-call(bf16[384,768]{1,0:T(8,128)(2,1)S(1)} %broadcast_select_fusion.6.refs_0_, bf16[384,2304]{1,0:T(8,128)(2,1)S(1)} %multiply_convert_fusion.3.refs_1_, f32[768,2304]{1,0:T(8,128)S(1)} %shard_map.191.refs_2_), custom_call_target="tpu_custom_call", output_to_operand_aliasing={{}: (2, {})} | custom-call | flops 1358954496 | bytes 9437184 | tf_op jit(solution)/shard_map/pallas_call | solution.py:101
  241.7 3.9 %shard_map.193.grad = f32[2304,768]{1,0:T(8,128)S(1)} custom-call(bf16[384,2304]{1,0:T(8,128)(2,1)S(1)} %broadcast_select_fusion.refs_0_, bf16[384,768]{1,0:T(8,128)(2,1)S(1)} %broadcast_select_fusion.5.refs_1_, f32[2304,768]{1,0:T(8,128)S(1)} %shard_map.190.refs_2_), custom_call_target="tpu_custom_call", output_to_operand_aliasing={{}: (2, {})} | custom-call | flops 1358954496 | bytes 9437184 | tf_op jit(solution)/shard_map/pallas_call | solution.py:101
  249.3 7.5 %collective-permute-done.59 = bf16[384,2304]{1,0:T(8,128)(2,1)S(1)} collective-permute-done((bf16[384,2304]{1,0:T(8,128)(2,1)}, bf16[384,2304]{1,0:T(8,128)(2,1)S(1)}, u32[]{:S(2)}, u32[]{:S(2)}) %collective-permute-start.59) | collective-permute-done | bytes 1769504 | tf_op jit(solution)/shard_map/ppermute | solution.py:182
  265.2 6.6 %shard_map.195 = (f32[768,2304]{1,0:T(8,128)}, f32[768,2304]{1,0:T(8,128)}, f32[768,2304]{1,0:T(8,128)}) custom-call(bf16[384,768]{1,0:T(8,128)(2,1)S(1)} %broadcast_select_fusion.4.left, bf16[384,2304]{1,0:T(8,128)(2,1)S(1)} %multiply_convert_fusion.right, f32[768,2304]{1,0:T(8,128)S(1)} %shard_map.194.grad, f32[768,1152]{1,0:T(8,128)S(1)} %copy-done.5, ...), custom_call_target="tpu_custom_call" | custom-call | flops 679477248 | bytes 26247168 | tf_op jit(solution)/shard_map/pallas_call | solution.py:132
  275.4 6.5 %shard_map.196 = (f32[768,2304]{1,0:T(8,128)}, f32[768,2304]{1,0:T(8,128)}, f32[768,2304]{1,0:T(8,128)}) custom-call(bf16[384,768]{1,0:T(8,128)(2,1)S(1)} %broadcast_select_fusion.4.left, bf16[384,2304]{1,0:T(8,128)(2,1)S(1)} %multiply_convert_fusion.right, ...), custom_call_target="tpu_custom_call", output_to_operand_aliasing={{0}: (6, {}), {1}: (7, {}), {2}: (8, {})} | custom-call | flops 679477248 | bytes 26247168 | tf_op jit(solution)/shard_map/pallas_call | solution.py:132
  284.0 20.1 %shard_map.197 = (f32[2304,768]{1,0:T(8,128)}, f32[2304,768]{1,0:T(8,128)}, f32[2304,768]{1,0:T(8,128)}) custom-call(bf16[384,2304]{1,0:T(8,128)(2,1)S(1)} %broadcast_select_fusion.1.left, bf16[384,768]{1,0:T(8,128)(2,1)S(1)} %broadcast_select_fusion.3.right, f32[2304,768]{1,0:T(8,128)S(1)} %shard_map.193.grad, f32[2304,768]{1,0:T(8,128)} %w.1, ...), custom_call_target="tpu_custom_call" | custom-call | flops 1358954496 | bytes 51904512 | tf_op jit(solution)/shard_map/pallas_call | solution.py:132
  (328 shorter events, 128.8 us)
Async XLA Ops:
  1.4 24.1 %collective-permute-start.6 = (f32[2,384]{1,0:T(2,128)S(1)}, f32[2,384]{1,0:T(2,128)S(1)}, u32[]{:S(2)}, u32[]{:S(2)}) collective-permute-start(f32[2,384]{1,0:T(2,128)S(1)} %get-tuple-element.216), channel_id=1, source_target_pairs={{0,2},{1,3},{2,0},{3,1},{4,6},{5,7},{6,4},{7,5},{8,10},{9,11},{10,... | collective-permute-start | bytes 9224 | tf_op jit(solution)/shard_map/ppermute | solution.py:297
  5.5 20.1 %collective-permute-start.5 = (f32[2,384]{1,0:T(2,128)S(1)}, f32[2,384]{1,0:T(2,128)S(1)}, u32[]{:S(2)}, u32[]{:S(2)}) collective-permute-start(f32[2,384]{1,0:T(2,128)S(1)} %get-tuple-element.216), channel_id=1, source_target_pairs={{0,1},{1,2},{2,3},{3,0},{4,5},{5,6},{6,7},{7,4},{8,9},{9,10},{10,1... | collective-permute-start | bytes 9224 | tf_op jit(solution)/shard_map/ppermute | solution.py:297
  7.1 18.5 %collective-permute-start.7 = (f32[2,384]{1,0:T(2,128)S(1)}, f32[2,384]{1,0:T(2,128)S(1)}, u32[]{:S(2)}, u32[]{:S(2)}) collective-permute-start(f32[2,384]{1,0:T(2,128)S(1)} %get-tuple-element.216), channel_id=1, source_target_pairs={{0,3},{1,0},{2,1},{3,2},{4,7},{5,4},{6,5},{7,6},{8,11},{9,8},{10,9... | collective-permute-start | bytes 9224 | tf_op jit(solution)/shard_map/ppermute | solution.py:297
  9.4 41.4 %collective-permute-start.1 = (bf16[384,2304]{1,0:T(8,128)(2,1)}, bf16[384,2304]{1,0:T(8,128)(2,1)}, u32[]{:S(2)}, u32[]{:S(2)}) collective-permute-start(bf16[384,2304]{1,0:T(8,128)(2,1)} %refs_0_.2), channel_id=1, source_target_pairs={{1,2},{2,1},{5,6},{6,5},{9,10},{10,9},{13,14},{14,13},{17,18},{18,... | collective-permute-start | bytes 5308424 | tf_op jit(solution)/shard_map/ppermute | solution.py:182
  11.3 39.8 %collective-permute-start = (bf16[384,2304]{1,0:T(8,128)(2,1)}, bf16[384,2304]{1,0:T(8,128)(2,1)}, u32[]{:S(2)}, u32[]{:S(2)}) collective-permute-start(bf16[384,2304]{1,0:T(8,128)(2,1)} %refs_0_.2), channel_id=1, source_target_pairs={{0,1},{1,0},{2,3},{3,2},{4,5},{5,4},{6,7},{7,6},{8,9},{9,8},{10,11... | collective-permute-start | bytes 5308424 | tf_op jit(solution)/shard_map/ppermute | solution.py:182
  54.4 26.1 %collective-permute-start.9 = (bf16[384,2304]{1,0:T(8,128)(2,1)S(1)}, bf16[384,2304]{1,0:T(8,128)(2,1)S(1)}, u32[]{:S(2)}, u32[]{:S(2)}) collective-permute-start(bf16[384,2304]{1,0:T(8,128)(2,1)S(1)} %copy-done.19), channel_id=1, source_target_pairs={{1,2},{2,1},{5,6},{6,5},{9,10},{10,9},{13,14},{14,13},{17,18},{18,... | collective-permute-start | bytes 5308424 | tf_op jit(solution)/shard_map/ppermute | solution.py:182
  55.2 42.0 %collective-permute-start.8 = (bf16[384,2304]{1,0:T(8,128)(2,1)S(1)}, bf16[384,2304]{1,0:T(8,128)(2,1)S(1)}, u32[]{:S(2)}, u32[]{:S(2)}) collective-permute-start(bf16[384,2304]{1,0:T(8,128)(2,1)S(1)} %copy-done.19), channel_id=1, source_target_pairs={{0,1},{1,0},{2,3},{3,2},{4,5},{5,4},{6,7},{7,6},{8,9},{9,8},{10,11... | collective-permute-start | bytes 5308424 | tf_op jit(solution)/shard_map/ppermute | solution.py:182
  59.7 15.1 %collective-permute-start.23 = (f32[2,48,768]{2,1,0:T(8,128)S(1)}, f32[2,48,768]{2,1,0:T(8,128)S(1)}, u32[]{:S(2)}, u32[]{:S(2)}) collective-permute-start(f32[2,48,768]{2,1,0:T(8,128)S(1)} %get-tuple-element.179), channel_id=1, source_target_pairs={{0,24},{4,28},{8,16},{12,20},{16,8},{20,12},{24,0},{28,4},{1,25},{... | collective-permute-start | bytes 884744 | tf_op jit(solution)/shard_map/ppermute | solution.py:212
  61.8 14.4 %collective-permute-start.22 = (f32[2,48,768]{2,1,0:T(8,128)S(1)}, f32[2,48,768]{2,1,0:T(8,128)S(1)}, u32[]{:S(2)}, u32[]{:S(2)}) collective-permute-start(f32[2,48,768]{2,1,0:T(8,128)S(1)} %get-tuple-element.180), channel_id=1, source_target_pairs={{0,16},{4,20},{8,24},{12,28},{16,0},{20,4},{24,8},{28,12},{1,17},{... | collective-permute-start | bytes 884744 | tf_op jit(solution)/shard_map/ppermute | solution.py:212
  77.0 22.2 %collective-permute-start.26 = (bf16[2,48,768]{2,1,0:T(8,128)(2,1)S(1)}, bf16[2,48,768]{2,1,0:T(8,128)(2,1)S(1)}, u32[]{:S(2)}, u32[]{:S(2)}) collective-permute-start(bf16[2,48,768]{2,1,0:T(8,128)(2,1)S(1)} %pad_maximum_fusion.7), channel_id=1, source_target_pairs={{0,8},{4,12},{8,0},{12,4},{16,24},{20,28},{24,16},{28,20},{1,9},{5... | collective-permute-start | bytes 442376 | tf_op jit(solution)/shard_map/ppermute | solution.py:212
  78.2 21.0 %collective-permute-start.25 = (bf16[2,48,768]{2,1,0:T(8,128)(2,1)S(1)}, bf16[2,48,768]{2,1,0:T(8,128)(2,1)S(1)}, u32[]{:S(2)}, u32[]{:S(2)}) collective-permute-start(bf16[2,48,768]{2,1,0:T(8,128)(2,1)S(1)} %pad_maximum_fusion.7), channel_id=1, source_target_pairs={{0,16},{4,20},{8,24},{12,28},{16,0},{20,4},{24,8},{28,12},{1,17},{... | collective-permute-start | bytes 442376 | tf_op jit(solution)/shard_map/ppermute | solution.py:212
  78.7 20.5 %collective-permute-start.24 = (bf16[2,48,768]{2,1,0:T(8,128)(2,1)S(1)}, bf16[2,48,768]{2,1,0:T(8,128)(2,1)S(1)}, u32[]{:S(2)}, u32[]{:S(2)}) collective-permute-start(bf16[2,48,768]{2,1,0:T(8,128)(2,1)S(1)} %pad_maximum_fusion.7), channel_id=1, source_target_pairs={{0,24},{4,28},{8,16},{12,20},{16,8},{20,12},{24,0},{28,4},{1,25},{... | collective-permute-start | bytes 442376 | tf_op jit(solution)/shard_map/ppermute | solution.py:212
  80.6 57.9 %collective-permute-start.2 = (bf16[384,2304]{1,0:T(8,128)(2,1)}, bf16[384,2304]{1,0:T(8,128)(2,1)}, u32[]{:S(2)}, u32[]{:S(2)}) collective-permute-start(bf16[384,2304]{1,0:T(8,128)(2,1)} %collective-permute-done.1), channel_id=1, source_target_pairs={{1,0},{2,3},{5,4},{6,7},{9,8},{10,11},{13,12},{14,15},{17,16},{18,... | collective-permute-start | bytes 5308424 | tf_op jit(solution)/shard_map/ppermute | solution.py:182
  97.3 42.5 %collective-permute-start.3 = (bf16[384,2304]{1,0:T(8,128)(2,1)}, bf16[384,2304]{1,0:T(8,128)(2,1)}, u32[]{:S(2)}, u32[]{:S(2)}) collective-permute-start(bf16[384,2304]{1,0:T(8,128)(2,1)} %collective-permute-done.refs_1_), channel_id=1, source_target_pairs={{1,2},{2,1},{5,6},{6,5},{9,10},{10,9},{13,14},{14,13},{17,18},{18,... | collective-permute-start | bytes 5308424 | tf_op jit(solution)/shard_map/ppermute | solution.py:182
  106.9 34.7 %collective-permute-start.29 = (f32[48,768]{1,0:T(8,128)}, f32[48,768]{1,0:T(8,128)}, u32[]{:S(2)}, u32[]{:S(2)}) collective-permute-start(f32[48,768]{1,0:T(8,128)} %get-tuple-element.193), channel_id=1, source_target_pairs={{0,8},{4,12},{8,0},{12,4},{16,24},{20,28},{24,16},{28,20},{1,9},{5... | collective-permute-start | bytes 442376 | tf_op jit(solution)/shard_map/ppermute | solution.py:212
  108.0 33.6 %collective-permute-start.31 = (f32[48,768]{1,0:T(8,128)}, f32[48,768]{1,0:T(8,128)}, u32[]{:S(2)}, u32[]{:S(2)}) collective-permute-start(f32[48,768]{1,0:T(8,128)} %get-tuple-element.194), channel_id=1, source_target_pairs={{0,24},{4,28},{8,16},{12,20},{16,8},{20,12},{24,0},{28,4},{1,25},{... | collective-permute-start | bytes 442376 | tf_op jit(solution)/shard_map/ppermute | solution.py:212
  109.9 31.7 %collective-permute-start.30 = (f32[48,768]{1,0:T(8,128)}, f32[48,768]{1,0:T(8,128)}, u32[]{:S(2)}, u32[]{:S(2)}) collective-permute-start(f32[48,768]{1,0:T(8,128)} %get-tuple-element.195), channel_id=1, source_target_pairs={{0,16},{4,20},{8,24},{12,28},{16,0},{20,4},{24,8},{28,12},{1,17},{... | collective-permute-start | bytes 442376 | tf_op jit(solution)/shard_map/ppermute | solution.py:212
  138.4 43.6 %collective-permute-start.10 = (bf16[384,2304]{1,0:T(8,128)(2,1)}, bf16[384,2304]{1,0:T(8,128)(2,1)S(1)}, u32[]{:S(2)}, u32[]{:S(2)}) collective-permute-start(bf16[384,2304]{1,0:T(8,128)(2,1)} %copy-done.20), channel_id=1, source_target_pairs={{1,0},{2,3},{5,4},{6,7},{9,8},{10,11},{13,12},{14,15},{17,16},{18,... | collective-permute-start | bytes 5308424 | tf_op jit(solution)/shard_map/ppermute | solution.py:182
  139.7 42.3 %collective-permute-start.11 = (bf16[384,2304]{1,0:T(8,128)(2,1)}, bf16[384,2304]{1,0:T(8,128)(2,1)}, u32[]{:S(2)}, u32[]{:S(2)}) collective-permute-start(bf16[384,2304]{1,0:T(8,128)(2,1)} %copy-done.22), channel_id=1, source_target_pairs={{1,2},{2,1},{5,6},{6,5},{9,10},{10,9},{13,14},{14,13},{17,18},{18,... | collective-permute-start | bytes 5308424 | tf_op jit(solution)/shard_map/ppermute | solution.py:182
  152.4 35.0 %collective-permute-start.36 = (f32[192,768]{1,0:T(8,128)S(1)}, f32[192,768]{1,0:T(8,128)S(1)}, u32[]{:S(2)}, u32[]{:S(2)}) collective-permute-start(f32[192,768]{1,0:T(8,128)S(1)} %constant_dynamic-slice_fusion.15), channel_id=1, source_target_pairs={{0,4},{4,0},{8,12},{12,8},{16,20},{20,16},{24,28},{28,24},{1,5},{5... | collective-permute-start | bytes 1769480 | tf_op jit(solution)/shard_map/ppermute | solution.py:212
  163.7 53.8 %collective-permute-start.4 = (bf16[384,2304]{1,0:T(8,128)(2,1)}, bf16[384,2304]{1,0:T(8,128)(2,1)S(1)}, u32[]{:S(2)}, u32[]{:S(2)}) collective-permute-start(bf16[384,2304]{1,0:T(8,128)(2,1)} %collective-permute-done.3), channel_id=1, source_target_pairs={{1,0},{2,3},{5,4},{6,7},{9,8},{10,11},{13,12},{14,15},{17,16},{18,... | collective-permute-start | bytes 5308424 | tf_op jit(solution)/shard_map/ppermute | solution.py:182
  187.6 11.5 %collective-permute-start.39 = (f32[48,768]{1,0:T(8,128)S(1)}, f32[48,768]{1,0:T(8,128)S(1)}, u32[]{:S(2)}, u32[]{:S(2)}) collective-permute-start(f32[48,768]{1,0:T(8,128)S(1)} %get-tuple-element.190), channel_id=1, source_target_pairs={{0,24},{4,28},{8,16},{12,20},{16,8},{20,12},{24,0},{28,4},{1,25},{... | collective-permute-start | bytes 442376 | tf_op jit(solution)/shard_map/ppermute | solution.py:212
  214.5 42.2 %collective-permute-start.59 = (bf16[384,2304]{1,0:T(8,128)(2,1)}, bf16[384,2304]{1,0:T(8,128)(2,1)S(1)}, u32[]{:S(2)}, u32[]{:S(2)}) collective-permute-start(bf16[384,2304]{1,0:T(8,128)(2,1)} %collective-permute-done.11), channel_id=1, source_target_pairs={{1,0},{2,3},{5,4},{6,7},{9,8},{10,11},{13,12},{14,15},{17,16},{18,... | collective-permute-start | bytes 5308424 | tf_op jit(solution)/shard_map/ppermute | solution.py:182
  234.5 11.1 %collective-permute-start.55 = (f32[48,768]{1,0:T(8,128)S(1)}, f32[48,768]{1,0:T(8,128)S(1)}, u32[]{:S(2)}, u32[]{:S(2)}) collective-permute-start(f32[48,768]{1,0:T(8,128)S(1)} %get-tuple-element.184), channel_id=1, source_target_pairs={{0,24},{4,28},{8,16},{12,20},{16,8},{20,12},{24,0},{28,4},{1,25},{... | collective-permute-start | bytes 442376 | tf_op jit(solution)/shard_map/ppermute | solution.py:212
  (73 other events, 482.5 us)
